TPU v7x, 32 devices: a whole 2x2x4 slice. The times are simulated.
32 devices in a mesh: graph: 8 (over z, y), leaf: 4 (over x, core).
Axes of the slice: x: 2, y: 2, z: 4, core: 2. Of those that a mesh axis runs over, the one named last changes fastest.
Arguments:
- weights: float32 [2, 1171200], P(None, ('graph', 'leaf'))
- first_moment: float32 [2, 1171200], P(None, ('graph', 'leaf'))
- second_moment: float32 [2, 1171200], P(None, ('graph', 'leaf'))
- centers: bfloat16 [8, 80, 300], P('graph'), may hold values from -6 to 6
- leaves: bfloat16 [8, 4096, 300], P('graph', 'leaf'), may hold values from -6 to 6
- edge_feats: bfloat16 [8, 4096, 300], P('graph', 'leaf'), may hold values from -6 to 6
- center_cot: bfloat16 [8, 80, 300], P('graph'), may hold values from -6 to 6
- leaf_cot: bfloat16 [8, 4096, 300], P('graph', 'leaf'), may hold values from -6 to 6
- edge_cot: bfloat16 [8, 4096, 300], P('graph', 'leaf'), may hold values from -6 to 6
- graph_ids: int32 [8, 4096], P('graph', 'leaf'), may hold values from 0 to 79, never falling along the last dimension, each value on 1 to 100 neighbouring positions
- star_sizes: int32 [8, 80], P('graph'), may hold values from 5 to 100
- leaf_mask: int32 [8, 4096], P('graph', 'leaf'), may hold values 0 or 1
- owner_list: int32 [32], replicated, may hold values from 0 to 31, as said below
Outputs:
- centers_out: bfloat16 [8, 80, 300], P('graph')
- leaves_out: bfloat16 [8, 4096, 300], P('graph', 'leaf')
- edges_out: bfloat16 [8, 4096, 300], P('graph', 'leaf')
- grad_centers: float32 [8, 80, 300], P('graph')
- grad_leaves: float32 [8, 4096, 300], P('graph', 'leaf')
- grad_edges: float32 [8, 4096, 300], P('graph', 'leaf')
- first_new: float32 [2, 1171200], P(None, ('graph', 'leaf'))
- second_new: float32 [2, 1171200], P(None, ('graph', 'leaf'))
- weights_new: float32 [2, 1171200], P(None, ('graph', 'leaf'))
- weights_low: bfloat16 [2, 1171200], P(None, ('graph', 'leaf'))
- weight_grads: float32 [2, 1171200], P(None, ('graph', 'leaf'))
Inputs may be any that keep to these rules, and one draw needn't show every extreme that they name: `graph_ids`: star numbers never fall along a group's slots; each star has 1 to 100 slots, one exactly 100. `owner_list`: a permutation of the holders.
All inputs are finite; a program needn't handle non-finite values. No bound on the sum of `leaf_mask` on one device may be relied on, other than what follows from the above.
Results may differ from a plain program's by a relative error of at most 0.04.
Values may be sent and summed in bfloat16 or wider, within the bound.
No kernel may reach another device: no remote copies, remote signals or barrier semaphores. Data moves between devices by JAX's collectives and lax.ppermute only.
A program may use at most 192 MiB of HBM per device.

v0:
```python
import math

import jax
import jax.numpy as jnp
from jax import lax
from jax.experimental import pallas as pl
from jax.experimental.pallas import tpu as pltpu
from jax.sharding import PartitionSpec as P

D = 300
HEADS = 12
HEAD = 25
FF = 1200
LAYERS = 2
STEP = 5
ROWS_LAYER = 5 * D + 2 * FF + 4

NEG = -1e30
EPS_NORM = 1e-05
BETA_ONE = 0.9
BETA_TWO = 0.999
RATE = 0.05
DECAY = 0.01
EPS_ADAM = 1e-08
INV_ROOT_TWO = 0.7071067811865476
INV_ROOT_TWO_PI = 0.3989422804014327

HALO = 128
TILE = 320
WIDE = 2
FFN_WIDE = 1
HP = 16
PACK = 320
CHUNKS = tuple((i, min(i + 256, FF)) for i in range(0, FF, 256))
VMEM = 60 << 20
F32 = jnp.float32
BF = jnp.bfloat16

STEP_COLUMNS = 384
PAIR = STEP_COLUMNS + D

WEIGHTS = ("wq", "wkv", "wo", "we", "wvo", "w1", "w2", "norm")
WEIGHT_SHAPES = (
    ((D, D), BF),
    ((D, PAIR), BF),
    ((D, D), BF),
    ((D, D), BF),
    ((D, D), BF),
    ((D, FF), BF),
    ((FF, D), BF),
    ((8, D), F32),
)


def nn(a, b):
    return lax.dot_general(a, b, (((1,), (0,)), ((), ())), preferred_element_type=F32)


def nt(a, b):
    return lax.dot_general(a, b, (((1,), (1,)), ((), ())), preferred_element_type=F32)


def tn(a, b):
    return lax.dot_general(a, b, (((0,), (0,)), ((), ())), preferred_element_type=F32)


def halves(x):
    high = x.astype(BF)
    return high, (x - high.astype(F32)).astype(BF)


def thirds(x):
    high = x.astype(BF)
    rest = x - high.astype(F32)
    mid = rest.astype(BF)
    return high, mid, (rest - mid.astype(F32)).astype(BF)


def stacked(parts, axis=0):
    return jnp.concatenate([p.astype(F32) for p in parts], axis=axis).astype(BF)


def side_by_side(*parts):
    zeros = jnp.zeros((parts[0].shape[0], STEP_COLUMNS - D), F32)
    pieces = [parts[0]]
    for part in parts[1:]:
        pieces += [zeros, part]
    return jnp.concatenate(pieces, axis=1)


def column(values, i):
    return values[:, i * STEP_COLUMNS : i * STEP_COLUMNS + D]


def table(rows, repeat=1):
    head = lax.broadcasted_iota(jnp.int32, (repeat * rows, D), 0) % rows
    feature = lax.broadcasted_iota(jnp.int32, (repeat * rows, D), 1)
    low = head * HEAD
    return jnp.where((feature >= low) & (feature < low + HEAD), 1.0, 0.0).astype(BF)


def head_sum(values):
    high, low = halves(values)
    tab = table(HP)
    return nt(high, tab) + nt(low, tab)


def head_sum_t(values):
    high, low = halves(values)
    tab = table(HP)
    return nt(tab, high) + nt(tab, low)


def spread(values):
    high, low = halves(values)
    tab = table(HP)
    return nn(high, tab) + nn(low, tab)


def spread_t(values):
    return tn(stacked(halves(values)), table(HP, 2))


def onehot_col(ids, stars, repeat):
    lane = lax.broadcasted_iota(jnp.int32, (ids.shape[0], repeat * stars), 1)
    hit = lane == ids
    for i in range(1, repeat):
        hit = hit | (lane == ids + i * stars) & (ids >= 0)
    return jnp.where(hit, 1.0, 0.0).astype(BF)


def onehot_row(ids, stars, repeat):
    sub = lax.broadcasted_iota(jnp.int32, (repeat * stars, ids.shape[1]), 0)
    hit = sub == ids
    for i in range(1, repeat):
        hit = hit | (sub == ids + i * stars) & (ids >= 0)
    return jnp.where(hit, 1.0, 0.0).astype(BF)


def row_mean(x):
    return jnp.sum(x, axis=-1, keepdims=True) * (1.0 / D)


def normalized(x):
    dev = x - row_mean(x)
    inverse = lax.rsqrt(row_mean(dev * dev) + EPS_NORM)
    return dev * inverse, inverse


def norm_back(grad, scaled, inverse):
    return inverse * (grad - row_mean(grad) - scaled * row_mean(grad * scaled))


def put_normalized(ref, rows, scaled, inverse):
    ref[rows, 0:D] = scaled.astype(BF)
    high, low = halves(inverse)
    ref[rows, D : D + 1] = high
    ref[rows, D + 1 : D + 2] = low


def get_normalized(ref, rows):
    inverse = ref[rows, D : D + 1].astype(F32) + ref[rows, D + 1 : D + 2].astype(F32)
    return ref[rows, 0:D].astype(F32), inverse


def ffn_forward(r, z, rows):
    norm = r.norm
    g1, b1, g2, b2 = (norm[i : i + 1, :] for i in range(4))
    xh1, inv1 = normalized(z)
    h = xh1 * g1 + b1
    hb = h.astype(BF)
    r.hb[rows, :] = hb
    put_normalized(r.xh1, rows, xh1, inv1)
    total = h
    for lo, hi in CHUNKS:
        pre = nn(hb, r.w1[:, lo:hi])
        cdf = 0.5 * (1.0 + lax.erf(pre * INV_ROOT_TWO))
        act = (pre * cdf).astype(BF)
        r.act[rows, lo:hi] = act
        r.slope[rows, lo:hi] = (
            cdf + pre * jnp.exp(-0.5 * pre * pre) * INV_ROOT_TWO_PI
        ).astype(BF)
        total = total + nn(act, r.w2[lo:hi, :])
    xh2, inv2 = normalized(total)
    put_normalized(r.xh2, rows, xh2, inv2)
    return xh2 * g2 + b2


def fold(x):
    return jnp.sum(x.reshape(x.shape[0] // 8, 8, x.shape[1]), axis=0)


def ffn_backward(r, gy, rows, weight):
    norm = r.norm
    g1, g2 = norm[0:1, :], norm[2:3, :]
    xh2, inv2 = get_normalized(r.xh2, rows)
    gw = gy * weight
    r.dn[2] += fold(gw * xh2)
    r.dn[3] += fold(gw)
    mid = norm_back(gy * g2, xh2, inv2)
    branch = mid.astype(BF)
    r.dbr[rows, 0:D] = (mid * weight).astype(BF)
    total = mid
    for lo, hi in CHUNKS:
        dact = nt(branch, r.w2[lo:hi, :])
        dpre = dact * r.slope[rows, lo:hi].astype(F32)
        low = dpre.astype(BF)
        r.dpre[rows, lo:hi] = (dpre * weight).astype(BF)
        total = total + nt(low, r.w1[:, lo:hi])
    xh1, inv1 = get_normalized(r.xh1, rows)
    gw = total * weight
    r.dn[0] += fold(gw * xh1)
    r.dn[1] += fold(gw)
    return norm_back(total * g1, xh1, inv1)


def forward(r, stars, leaf_rows):
    xc = r.xc[...].astype(F32)
    low = xc.astype(BF)
    r.wait("wq", "wkv", "wo", "we", "wvo")
    r.settle("kv")
    qs = nn(low, r.wq[...]) * r.scale[...]
    kvc = nn(low, r.wkv[...])
    own_score = head_sum(qs * column(kvc, 0))
    r.qs[...] = qs
    r.kvc[...] = kvc
    r.self[...] = own_score
    r.cat[:, 0:PAIR] = stacked(halves(side_by_side(qs, xc)))

    def tile(start, size, rows, carry):
        el = r.el[rows, :]
        ew = el.astype(F32)
        xl = r.xl[rows, :].astype(F32)
        r.en[rows, :] = nn(el, r.we[...]).astype(BF)
        from_star = nn(onehot_col(r.idc[rows, :], stars, 2), r.cat[:, 0:PAIR])
        kv = nn((xl * ew).astype(BF), r.wkv[...])
        r.kv[rows, :] = kv.astype(BF)
        r.s[:, rows] = head_sum_t(column(from_star, 0) * column(kv, 0))
        mc = (column(from_star, 1) * ew).astype(BF)
        r.z[rows, :] = xl + nn(mc, r.wvo[...])
        return carry

    def ffn_tile(start, size, rows, carry):
        if start == 0:
            r.wait("w1", "w2")
            r.settle(*made)
        if start + size == leaf_rows:
            r.z[leaf_rows:, :] = xc + attend(r, stars, leaf_rows, own_score, column(kvc, 1))
        y = ffn_forward(r, r.z[rows, :], rows)
        r.yl[start : start + size, :] = y[:size].astype(r.yl.dtype)
        if start + size == leaf_rows:
            r.yc[...] = y[size:]
        return carry

    made = ("yl", "hb", "xh1", "xh2", "act", "slope")
    r.loop(("xl", "el"), ("en", "kv"), tile, 0)
    r.loop((), made, ffn_tile, 0, stars, FFN_WIDE)
    r.finish("en", "kv", *made)


def attend(r, stars, leaf_rows, own_score, vc):
    ids = r.idr[...]
    live = r.live[...] > 0.5
    score = r.s[...]
    top = jnp.where(live, score, NEG)
    lane = lax.broadcasted_iota(jnp.int32, (1, leaf_rows), 1)
    shift = 1
    while shift < 128:
        same = (pltpu.roll(ids, shift, 1) == ids) & (lane >= shift)
        top = jnp.maximum(top, jnp.where(same, pltpu.roll(top, shift, 1), NEG))
        shift *= 2
    hot_row = onehot_row(ids, stars, 1)
    last = hot_row.astype(F32) * r.last[...]
    present = jnp.sum(last, axis=1, keepdims=True) > 0.5
    last = last.astype(BF)
    star_top = sum(nt(last, part) for part in thirds(top))
    peak = jnp.where(present, jnp.maximum(star_top, own_score), own_score)
    peak_row = tn(stacked(thirds(peak)), onehot_row(ids, stars, 3))
    e = jnp.where(live, jnp.exp(jnp.where(live, score - peak_row, 0.0)), 0.0)
    self_weight = jnp.exp(own_score - peak)
    total = self_weight + sum(nt(hot_row, part) for part in halves(e))
    r.logt[...] = peak + jnp.log(total)
    weighted = (spread_t(e) * column(r.kv, 1).astype(F32)).astype(BF)
    o = (nn(hot_row, weighted) + spread(self_weight) * vc) / spread(total)
    r.o[...] = o
    return nn(o.astype(BF), r.wo[...])


def backward_ffn(r, stars, leaf_rows, own_rows):
    r.dn[...] = jnp.zeros_like(r.dn)
    r.wait("w2", "w1")

    def tile(start, size, rows, carry):
        row = lax.broadcasted_iota(jnp.int32, (size, 1), 0) + start
        mine = jnp.where((row >= HALO) & (row < HALO + own_rows), 1.0, 0.0)
        gy = r.gyl[start : start + size, :].astype(F32)
        if start + size == leaf_rows:
            gy = jnp.concatenate([gy, r.gyc[...].astype(F32)], axis=0)
            mine = jnp.concatenate([mine, r.cown[...]], axis=0)
        r.dz[rows, :] = ffn_backward(r, gy, rows, mine).astype(BF)
        return carry

    made = ("dz", "dbr", "dpre")
    r.loop(("gyl", "xh2", "slope", "xh1"), made, tile, 0, stars, FFN_WIDE)
    r.finish(*made)


def backward_attention(r, stars, leaf_rows):
    r.wait("wo")
    r.arrive_rest("dz")
    do = nt(r.dz[leaf_rows:, :], r.wo[...])
    kvc = r.kvc[...]
    kc, vc = column(kvc, 0), column(kvc, 1)
    qs = r.qs[...]
    xc = r.xc[...].astype(F32)
    r.cat[...] = stacked(halves(side_by_side(qs, xc, do)))
    delta = head_sum(do * r.o[...])
    self_p = jnp.exp(r.self[...] - r.logt[...])
    d_self = self_p * (head_sum(do * vc) - delta)
    coef_c = spread(d_self)
    r.dkvc[...] = side_by_side(coef_c * qs, spread(self_p) * do).astype(BF)
    logt_parts = stacked(thirds(r.logt[...]))
    delta_parts = stacked(thirds(delta))

    def tile(start, size, rows, total):
        el = r.el[rows, :].astype(F32)
        ids_row = r.idr[:, rows]
        hot3 = onehot_row(ids_row, stars, 3)
        from_star = nn(onehot_col(r.idc[rows, :], stars, 2), r.cat[...])
        r.mc[rows, :] = (column(from_star, 1) * el).astype(BF)
        live = r.live[:, rows] > 0.5
        score = r.s[:, rows] - tn(logt_parts, hot3)
        p = jnp.where(live, jnp.exp(jnp.where(live, score, 0.0)), 0.0)
        dor = column(from_star, 2)
        kv = r.kv[rows, :]
        ds = p * (head_sum_t(dor * column(kv, 1).astype(F32)) - tn(delta_parts, hot3))
        coef = spread_t(ds)
        r.dkv[rows, :] = side_by_side(coef * column(from_star, 0), spread_t(p) * dor).astype(BF)
        r.m[rows, :] = (r.xl[rows, :].astype(F32) * el).astype(BF)
        part = (coef * column(kv, 0).astype(F32)).astype(BF)
        return total + nn(onehot_row(ids_row, stars, 1), part)

    zero = jnp.zeros((stars, D), F32)
    total = r.loop(("el", "kv", "xl", "dz"), ("dkv",), tile, zero)
    r.dq[...] = ((total + coef_c * kc) * r.scale[...]).astype(BF)
    r.finish("dkv")


def weight_grads(r, stars, leaf_rows, own_rows):
    own = r.cown[...]
    own_leaf = slice(HALO, HALO + own_rows)
    r.wait("wkv")
    r.arrive("dz", "ge", "hb", "dpre", "act", "dbr")
    nat = r.nat
    xb = r.xc[...].astype(BF)
    dq, dkvc, dac = (
        (x.astype(F32) * own).astype(BF) for x in (r.dq[...], r.dkvc[...], r.dz[leaf_rows:, :])
    )
    nat_store(nat, pl.ds(0, D), tn(xb, dq))
    pair = tn(r.m[own_leaf, :], r.dkv[own_leaf, :]) + tn(xb, dkvc)
    both = tn(r.mc[own_leaf, :], r.dz[own_leaf, :]).astype(BF)
    nat_store(nat, pl.ds(D, D), column(pair, 0))
    nat_store(nat, pl.ds(2 * D, D), column(pair, 1) + nt(both, r.wo[...]))
    out = tn(column(r.wkv, 1), both) + tn(r.o[...].astype(BF), dac)
    nat_store(nat, pl.ds(3 * D, D), out)
    nat_store(nat, pl.ds(4 * D, D), tn(r.el[own_leaf, :], r.ge[own_leaf, :]))
    base = 5 * D
    for j in range(FF // D):
        columns = slice(j * D, (j + 1) * D)
        part = tn(r.hb[HALO:, :], r.dpre[HALO:, columns])
        nat_store(nat, pl.ds(base + j, D, stride=FF // D), part)
    base = base + FF
    for lo, hi in CHUNKS:
        part = tn(r.act[HALO:, lo:hi], r.dbr[HALO:, 0:D])
        nat_store(nat, pl.ds(base + lo, hi - lo), part)
    base = base + FF
    sums = [jnp.sum(r.dn[i], axis=0, keepdims=True) for i in range(4)]
    nat_store(nat, pl.ds(base, 4), jnp.concatenate(sums, axis=0))


def backward_inputs(r, stars, leaf_rows):
    r.wait("wq", "wkv", "wvo", "we")
    xc = r.xc[...].astype(F32)
    r.xcat[...] = stacked(halves(xc))

    def tile(start, size, rows, total):
        dz = r.dz[rows, :]
        dmc = nt(dz, r.wvo[...])
        el = r.el[rows, :].astype(F32)
        hot = onehot_col(r.idc[rows, :], stars, 2)
        dm = nt(r.dkv[rows, :], r.wkv[...])
        r.gxl[rows, :] = (dz.astype(F32) + dm * el).astype(r.gxl.dtype)
        de = dmc * nn(hot, r.xcat[...]) + dm * r.xl[rows, :].astype(F32)
        de = de + nt(r.ge[rows, :], r.we[...])
        r.gel[rows, :] = de.astype(r.gel.dtype)
        return total + nn(onehot_row(r.idr[:, rows], stars, 1), (dmc * el).astype(BF))

    zero = jnp.zeros((stars, D), F32)
    total = r.loop(("dz", "el", "dkv", "xl", "ge"), ("gxl", "gel"), tile, zero)
    r.arrive("dz")
    r.gxc[...] = (
        r.dz[leaf_rows:, :].astype(F32)
        + nt(r.dq[...], r.wq[...])
        + nt(r.dkvc[...], r.wkv[...])
        + total
    )
    r.finish("gxl", "gel")


def nat_load(nat, at):
    return jnp.concatenate([nat[c, at, :] for c in range(3)], axis=1)[:, :D]


def nat_store(nat, at, value):
    nat[0, at, :] = value[:, 0:128]
    nat[1, at, :] = value[:, 128:256]
    rest = jnp.zeros((value.shape[0], 384 - D), F32)
    nat[2, at, :] = jnp.concatenate([value[:, 256:D], rest], axis=1)


def pack_blocks(r, holders, rows):
    nat = r.nat
    lane = lax.broadcasted_iota(jnp.int32, (64, 128), 1)
    half = holders // 2
    for b in range(holders):
        top = b * rows
        at = r.slot[0, b]
        r.all_a[at, 0:128, :] = nat[0, top : top + 128, :].astype(BF)
        r.all_a[at, 128:160, :] = nat[1, top : top + 32, :].astype(BF)
        at = r.slot[1, b]
        r.all_b[at, 0:96, :] = nat[1, top + 32 : top + 128, :].astype(BF)
        high = pltpu.roll(nat[2, top + 64 : top + 128, :], 64, 1)
        tail = jnp.where(lane < 64, nat[2, top : top + 64, :], high)
        r.all_b[at, 96:160, :] = tail.astype(BF)
    for i, name in enumerate(("all_a", "all_b")):
        r.keep[i * half : (i + 1) * half] = r[name][:half]
        r.send[i * half : (i + 1) * half] = r[name][half:]


def unpack_copies(r, layer, holders):
    half = holders // 2
    return [
        pltpu.make_async_copy(r[f"{k}{layer}"], r.got.at[pl.ds(i * half, half)], r.sems.at[i])
        for i, k in enumerate(("near", "far"))
    ]


def unpack_blocks(r, layer, holders, rows):
    nat = r.nat
    for copy in unpack_copies(r, layer, holders):
        copy.wait()

    for b in range(holders):
        top = b * rows
        got = r.got[r.slot[layer, b]].astype(F32)
        nat[0, top : top + rows, :] = got[:rows]
        nat[1, top : top + rows, :] = got[128 : 128 + rows]
        tail = got[256:]
        nat[2, top : top + 64, :] = tail
        nat[2, top + 64 : top + rows, :] = pltpu.roll(tail, 64, 1)[: rows - 64]
    wq, wk, wv, wo, we = (nat_load(nat, pl.ds(i * D, D)).astype(BF) for i in range(5))
    put_squares(r, wq, wk, wv, wo, we)
    base = 5 * D
    for j in range(FF // D):
        part = nat_load(nat, pl.ds(base + j, D, stride=FF // D))
        r.w1[:, j * D : (j + 1) * D] = part.astype(BF)
    base = base + FF
    r.w2[...] = nat_load(nat, pl.ds(base, FF)).astype(BF)
    base = base + FF
    r.norm[...] = nat_load(nat, pl.ds(base, 8))
    r.finish(*WEIGHTS)


def put_squares(r, wq, wk, wv, wo, we):
    r.wq[...] = wq
    r.wkv[...] = side_by_side(wk.astype(F32), wv.astype(F32)).astype(BF)
    r.wo[...] = wo
    r.we[...] = we
    r.wvo[...] = nn(wv, wo).astype(BF)


class Bag(dict):
    def __getattr__(self, name):
        return self[name]


class Refs(Bag):
    def __init__(self, refs, leaf_rows):
        super().__init__(refs)
        state = dict(tiles=leaf_rows // TILE, alias={}, coming={}, going={}, pending=[])
        self.__dict__.update(state)

    def view(self, alias):
        other = Refs({**self, **{k: self[v] for k, v in alias.items()}}, self.tiles * TILE)
        state = dict(alias=alias, coming=self.coming, going=self.going, pending=self.pending)
        other.__dict__.update(state)
        return other

    def keys_of(self, names):
        return [self.alias.get(k, k) for k in names]

    def wait(self, *names):
        for name in self.keys_of(names):
            for copy in self.coming.pop(name, ()):
                copy.wait()

    def arrive(self, *names):
        for name in self.keys_of(names):
            if name in self.coming:
                for copy in self.coming.pop(name)["all"]():
                    copy.wait()

    def arrive_rest(self, name):
        (name,) = self.keys_of([name])
        if name in self.coming:
            for copy in self.coming[name]["rest"]():
                copy.wait()
            self.coming[name]["all"] = self.coming[name]["every"]
            self.coming[name]["rest"] = list

    def loop(self, names, made, body, carry, more=0, group=WIDE):
        coming = [self.coming[k] for k in self.keys_of(names) if "tile" in self.coming.get(k, ())]
        going = [self.going[k] for k in self.keys_of(made) if k in self.going]
        for first in range(0, self.tiles, group):
            stop = min(first + group, self.tiles)
            extra = more if stop == self.tiles else 0
            for k in coming:
                for t in range(first, stop):
                    k["tile"](t, t * TILE).wait()
            if extra:
                for name in names:
                    self.arrive_rest(name)
            start, size = first * TILE, (stop - first) * TILE
            carry = body(start, size, pl.ds(start, size + extra), carry)
            for t in range(first, stop):
                for k in going:
                    k["tile"](t, t * TILE)
        for k in coming:
            k["all"] = k["rest"]
            del k["tile"]
        return carry

    def finish(self, *names):
        for name in self.keys_of(names):
            if name in self.going:
                self.pending += [(name, copy) for copy in self.going.pop(name)["rest"]()]

    def settle(self, *names):
        for name, copy in self.pending:
            if name in names:
                copy.wait()
        self.pending[:] = [x for x in self.pending if x[0] not in names]


def call(body, inputs, outputs, scratch, micros, leaf_rows=TILE, lazy=(), joins=(), own=(), in_smem=(), name=None, loose=(), early=None):
    joins = dict(joins)
    tiles = leaf_rows // TILE
    raw = {k for k, _ in joins.values()} | ({"halo_l", "halo_r"} if joins else set())
    raw |= set(loose)
    lazy_in = [k for k in inputs if k in lazy and k not in raw] + list(joins)
    buffers = {}
    for k in lazy_in:
        source = inputs[joins[k][0]] if k in joins else inputs[k]
        rows = leaf_rows if k in joins else source.shape[0]
        buffers[k] = ((rows,) + source.shape[1:], source.dtype)
    lazy_out = [k for k in outputs if k in lazy]
    for k in lazy_out:
        shape, dtype = outputs[k]
        buffers[k] = ((leaf_rows,) + shape[1:] if k in own else shape, dtype)
    names = list(inputs) + list(outputs) + list(scratch)

    def kernel(*refs):
        outer = dict(zip(names, refs, strict=False))
        rest = refs[len(names) :]
        held = dict(zip(buffers, rest, strict=False))
        sems = rest[-1] if buffers else None
        r = Refs({**outer, **held}, leaf_rows)
        copy = pltpu.make_async_copy
        if early is not None:
            early(r)
        for i, k in enumerate(buffers):
            inner, total = held[k], buffers[k][0][0]
            if k in lazy_out:
                target = outer[k]
                if k in own or total < leaf_rows:
                    cut = pl.ds(HALO, leaf_rows - 2 * HALO) if k in own else pl.ds(0, total)

                    def last(inner=inner, target=target, cut=cut, i=i):
                        one = copy(inner.at[cut], target, sems.at[i, tiles])
                        one.start()
                        return [one]

                    def per_tile(t, start):
                        return None

                else:

                    def per_tile(t, start, inner=inner, target=target, i=i):
                        rows = pl.ds(start, TILE)
                        copy(inner.at[rows], target.at[rows], sems.at[i, t]).start()

                    def last(inner=inner, target=target, i=i, total=total):
                        done = [
                            copy(inner.at[pl.ds(t * TILE, TILE)], target.at[pl.ds(t * TILE, TILE)], sems.at[i, t])
                            for t in range(tiles)
                        ]
                        if total > leaf_rows:
                            rows = pl.ds(leaf_rows, total - leaf_rows)
                            done.append(copy(inner.at[rows], target.at[rows], sems.at[i, tiles]))
                            done[-1].start()
                        return done

                r.going[k] = {"tile": per_tile, "rest": last}
            elif total < leaf_rows or k in WEIGHTS or k[:-1] in WEIGHTS:
                one = copy(outer[k], inner, sems.at[i, 0])
                one.start()
                r.coming[k] = [one]
            else:

                def wait_for(t, start, inner=inner, i=i):
                    rows = inner.at[pl.ds(start, TILE)]
                    return copy(rows, rows, sems.at[i, t])

                def behind(inner=inner, i=i, total=total):
                    if total == leaf_rows:
                        return []
                    rows = inner.at[pl.ds(leaf_rows, total - leaf_rows)]
                    return [copy(rows, rows, sems.at[i, tiles])]

                def every(wait_for=wait_for):
                    return [wait_for(t, t * TILE) for t in range(tiles)]

                def whole(every=every, behind=behind):
                    return every() + behind()

                r.coming[k] = {"tile": wait_for, "rest": behind, "every": every, "all": whole}
        for t in [tiles] + list(range(tiles)):
            for i, k in enumerate(buffers):
                if k in lazy_out or not isinstance(r.coming.get(k), dict):
                    continue
                inner, total = held[k], buffers[k][0][0]
                low, high = t * TILE, min((t + 1) * TILE, leaf_rows)
                if t == tiles:
                    high = total
                if k in joins:
                    source, place = joins[k]
                    stop = leaf_rows - HALO
                    pieces = [
                        (outer["halo_l"], place * HALO, 0, HALO),
                        (outer[source], 0, HALO, stop),
                        (outer["halo_r"], place * HALO, stop, leaf_rows),
                    ]
                else:
                    pieces = [(outer[k], 0, 0, total)]
                for ref, offset, first, stop in pieces:
                    a, b = max(first, low), min(stop, high)
                    if a < b:
                        piece = ref.at[pl.ds(a - first + offset, b - a)]
                        copy(piece, inner.at[pl.ds(a, b - a)], sems.at[i, t]).start()
        body(r)
        for k in list(r.coming):
            if isinstance(r.coming[k], dict):
                r.arrive(k)
            else:
                r.wait(k)
        r.finish(*list(r.going))
        for _, one in r.pending:
            one.wait()

    vmem = pl.BlockSpec(memory_space=pltpu.VMEM)
    smem = pl.BlockSpec(memory_space=pltpu.SMEM)
    anywhere = pl.BlockSpec(memory_space=pl.ANY)

    def place(k):
        return smem if k in in_smem else anywhere if k in lazy or k in raw else vmem

    results = pl.pallas_call(
        kernel,
        out_shape=[jax.ShapeDtypeStruct(s, d) for s, d in outputs.values()],
        in_specs=[place(k) for k in inputs],
        out_specs=[place(k) for k in outputs],
        scratch_shapes=[
            pltpu.SemaphoreType.DMA(s) if d is None else pltpu.VMEM(s, d) for s, d in scratch.values()
        ]
        + [pltpu.VMEM(s, d) for s, d in buffers.values()]
        + ([pltpu.SemaphoreType.DMA((len(buffers), tiles + 1))] if buffers else []),
        compiler_params=pltpu.CompilerParams(vmem_limit_bytes=VMEM),
        cost_estimate=pl.CostEstimate(
            flops=int(micros * 1e9), bytes_accessed=int(micros * 1e6), transcendentals=0
        ),
        name=name,
    )(*inputs.values())
    return Bag(zip(outputs, results, strict=True))


def saved_shapes(stars, leaf_rows):
    rows = leaf_rows + stars
    return dict(
        kv=((leaf_rows, PAIR), BF),
        hb=((rows, D), BF),
        xh1=((rows, STEP_COLUMNS), BF),
        xh2=((rows, STEP_COLUMNS), BF),
        act=((rows, FF), BF),
        slope=((rows, FF), BF),
        s=((HP, leaf_rows), F32),
        qs=((stars, D), F32),
        kvc=((stars, PAIR), F32),
        o=((stars, D), F32),
        self=((stars, HP), F32),
        logt=((stars, HP), F32),
    )


def leaf_shapes(leaf_rows, *names):
    return {k: ((leaf_rows, D), BF) for k in names}


def ffn_scratch(stars, leaf_rows):
    rows = leaf_rows + stars
    return {"dn": ((4, 8, D), F32), "dbr": ((rows, STEP_COLUMNS), BF), "dpre": ((rows, FF), BF)}


def exchange(x, stage, value, sizes):
    axis, shift, bits = stage
    return lax.ppermute(x, axis, [(i, i ^ (value << shift)) for i in range(sizes[axis])])


def tree_stages(sizes, swap):
    bits = {axis: size.bit_length() - 1 for axis, size in sizes.items()}

    def cut(axis, start, stop):
        return [(axis, i, min(2, stop - i)) for i in range(start, stop, 2)]

    middle = [cut("leaf", 1, bits["leaf"]), cut("graph", 0, 1)]
    if swap:
        middle = middle[::-1]
    return [("leaf", 0, 1)] + middle[0] + middle[1] + cut("graph", 1, bits["graph"])


def tree_slot(relative, stages, leaf_bits):
    slot = jnp.zeros_like(relative)
    for axis, shift, bits in stages:
        shift = shift + (leaf_bits if axis == "graph" else 0)
        slot = (slot << bits) | ((relative >> shift) & ((1 << bits) - 1))
    return slot


def gather_step(held, stage, sizes):
    parts = [held] + [exchange(held, stage, v, sizes) for v in range(1, 1 << stage[2])]
    return jnp.concatenate(parts, axis=0)


def total(held, start, stop):
    return sum(x[at + start : at + stop].astype(F32) for x, at in held[0])


def reduce_step(held, stage, sizes):
    terms, rows = held
    count = rows >> stage[2]
    sent = [total(held, v * count, (v + 1) * count).astype(BF) for v in range(1, 1 << stage[2])]
    got = [(exchange(x, stage, v + 1, sizes), 0) for v, x in enumerate(sent)]
    return terms + got, count


def tie(helds, *others):
    newest, others = lax.optimization_barrier(([h[0][-1][0] for h in helds], others))
    return [
        (terms[:-1] + [(x, terms[-1][1])], rows)
        for (terms, rows), x in zip(helds, newest, strict=True)
    ], others


def to_rows(flat, rows):
    block = jnp.pad(flat.reshape(rows, D), ((0, 128 - rows), (0, 0)))
    tail = jnp.pad(block[:, 256:], ((0, 0), (0, 320 - D)))
    return jnp.concatenate(
        [block[:, :128], block[:, 128:256], jnp.concatenate([tail[:64], tail[64:]], axis=1)], axis=0
    )


def from_rows(packed, rows):
    tail = jnp.concatenate([packed[256:, : D - 256], packed[256:, 64 : D - 192]], axis=0)
    block = jnp.concatenate([packed[:128], packed[128:256], tail], axis=1)
    return block[:rows].reshape(-1)


def split_flat(vec):
    square = D * D
    wq, wk, wv, wo, we = (vec[i * square : (i + 1) * square].reshape(D, D) for i in range(5))
    at = 5 * square
    w1 = vec[at : at + D * FF].reshape(D, FF)
    at = at + D * FF
    w2 = vec[at : at + FF * D].reshape(FF, D)
    at = at + FF * D
    norm = jnp.pad(vec[at : at + 4 * D].reshape(4, D).astype(F32), ((0, 4), (0, 0)))
    wkv = jnp.concatenate([wk, jnp.zeros((D, STEP_COLUMNS - D), BF), wv], axis=1)
    return Bag(zip(WEIGHTS, (wq, wkv, wo, we, nn(wv, wo).astype(BF), w1, w2, norm), strict=True))


def halo(x):
    size = lax.axis_size("leaf")
    last, first = x
    left = lax.ppermute(last, "leaf", [(i, i + 1) for i in range(size - 1)])
    right = lax.ppermute(first, "leaf", [(i + 1, i) for i in range(size - 1)])
    return left, right


def local(
    weights,
    first_moment,
    second_moment,
    centers,
    leaves,
    edge_feats,
    center_cot,
    leaf_cot,
    edge_cot,
    graph_ids,
    star_sizes,
    leaf_mask,
    owner_list,
):
    sizes = {"graph": lax.axis_size("graph"), "leaf": lax.axis_size("leaf")}
    holders = sizes["graph"] * sizes["leaf"]
    block_len = weights.shape[1]
    block_rows = block_len // D
    in_rows = block_len % D == 0 and 64 < block_rows <= 128
    stars = centers.shape[1]
    own_rows = leaves.shape[1]
    leaf_rows = own_rows + 2 * HALO

    orders = [tree_stages(sizes, swap) for swap in (False, True)]
    me = lax.axis_index(("graph", "leaf"))
    leaf_bits = sizes["leaf"].bit_length() - 1
    slot = jnp.stack([tree_slot(owner_list ^ me, stages, leaf_bits) for stages in orders])
    nat_rows = ROWS_LAYER + 12
    nat = {"nat": ((3, nat_rows, 128), F32)}
    half = PACK // 2
    n_steps = len(orders[0])
    weights_low = weights.astype(BF)

    def gather_begin(rows):
        held = gather_step(jnp.concatenate(rows, axis=0)[None], orders[0][-1], sizes)
        size = rows[0].shape[0]
        return [held[:, :size], held[:, size:]]

    def gather_more(held, n):
        return [gather_step(h, o[n], sizes) for h, o in zip(held, orders, strict=True)]

    rows = [to_rows(x, block_rows) if in_rows else x for x in weights_low]
    rows, leaves, edge_feats, leaf_cot, edge_cot, graph_ids, leaf_mask = lax.optimization_barrier(
        (rows, leaves, edge_feats, leaf_cot, edge_cot, graph_ids, leaf_mask)
    )
    held = gather_begin(rows)
    raw = dict(leaves=leaves[0], edges=edge_feats[0], lcot=leaf_cot[0], ecot=edge_cot[0])
    marks = jnp.pad((graph_ids + 1).astype(BF), ((0, 15), (0, 0)))
    marks = jnp.concatenate([marks[:8], jnp.broadcast_to(leaf_mask.astype(BF), (8, own_rows))], axis=0)

    def edge(cut):
        note = jnp.pad(marks[:, cut], ((0, 0), (0, D - HALO)))
        return jnp.concatenate([x[cut] for x in raw.values()] + [note], axis=0)

    left, right = halo((edge(slice(own_rows - HALO, own_rows)), edge(slice(0, HALO))))
    at = len(raw)
    raw, held = lax.optimization_barrier((raw, held))
    raw = dict(raw, halo_l=left, halo_r=right)

    def with_marks(line, mine):
        sides = [x[at * HALO + line, :HALO].astype(jnp.int32)[None] for x in (left, right)]
        return jnp.concatenate([sides[0], mine, sides[1]], axis=1)

    ids = with_marks(0, graph_ids + 1) - 1
    live = with_marks(8, leaf_mask).astype(F32)
    edge_id = jnp.full((1, 1), -1, jnp.int32)
    last = (ids != jnp.concatenate([ids[:, 1:], edge_id], axis=1)).astype(F32)
    first = graph_ids[0] != ids[0, HALO - 1 : HALO - 1 + own_rows]
    star_index = jnp.arange(stars, dtype=jnp.int32)
    star_own = jnp.any((star_index[:, None] == graph_ids) & first[None, :], axis=1)[:, None]
    scale = (jnp.log(star_sizes[0].astype(F32)) / (math.log(32.0) * math.sqrt(HEAD)))[:, None]
    base = Bag(
        idc=ids.reshape(-1, 1),
        idr=ids,
        live=live,
        last=last,
        scale=scale,
        cown=star_own.astype(F32),
    )
    saved = saved_shapes(stars, leaf_rows)
    rows = leaf_rows + stars
    if in_rows:
        grads_out = {k: ((holders, half, 128), BF) for k in ("keep", "send")}
        grads_scratch = {k: ((holders, half, 128), BF) for k in ("all_a", "all_b")} | nat
    else:
        grads_out, grads_scratch = nat, {}
    lazy = WEIGHTS[:-1] + tuple(f"{k}{i}" for k in WEIGHTS for i in range(LAYERS)) + ("yl0", "en0", "xl", "el", "gyl", "ge", "yl", "en") + (
        "kv", "hb", "xh1", "xh2", "act", "slope", "dz", "dkv", "gxl", "gel", "dbr", "dpre",
    )
    f_scratch = dict(cat=((2 * stars, PAIR), BF), z=((rows, D), F32))
    a_scratch = {"cat": ((2 * stars, PAIR + STEP_COLUMNS), BF), **leaf_shapes(leaf_rows, "mc", "m")}
    handed = dict(
        dz=((rows, D), BF),
        dkv=((leaf_rows, PAIR), BF),
        dq=((stars, D), BF),
        dkvc=((stars, PAIR), BF),
    )
    def halves_of(*names):
        return {k: raw[k] for k in (*names, "halo_l", "halo_r")}

    join = dict(xl=("leaves", 0), el=("edges", 1), gyl=("lcot", 2), ge=("ecot", 3))

    def joined(*names):
        return {k: join[k] for k in names}

    for n in range(n_steps - 2, 0, -1):
        held = gather_more(held, n)

    def end_grads(r):
        backward_attention(r, stars, leaf_rows)
        weight_grads(r, stars, leaf_rows, own_rows)
        if in_rows:
            pack_blocks(r, holders, block_rows)

    small = [k for k in saved if k not in lazy]

    def start_first(r):
        for copy in unpack_copies(r, 0, holders):
            copy.start()

    def front(r):
        zero = r.view({**{k: k + "0" for k in WEIGHTS}, "yl": "yl0", "en": "en0", "yc": "yc0"})
        names = {**{k: k + "1" for k in (*WEIGHTS, *small)}, "xl": "yl0", "el": "en0", "xc": "yc0"}
        one = r.view(names)
        one.update(dpre=r.slope, dbr=r.xh2)
        if in_rows:
            unpack_blocks(zero, 0, holders, block_rows)
            for copy in unpack_copies(r, 1, holders):
                copy.start()
        forward(zero, stars, leaf_rows)
        if in_rows:
            unpack_blocks(one, 1, holders, block_rows)
            one.update(all_a=r.got.at[:, : PACK // 2], all_b=r.got.at[:, PACK // 2 :])
        forward(one, stars, leaf_rows)
        backward_ffn(one, stars, leaf_rows, own_rows)
        end_grads(one)

    weight_specs = dict(zip(WEIGHTS, WEIGHT_SHAPES, strict=True))
    params, unpacked, kept, loose = [], {}, {}, {}
    for i, near in enumerate(held):
        far = exchange(near, orders[i][0], 1, sizes)
        if in_rows:
            loose.update({f"near{i}": near, f"far{i}": far})
            used = WEIGHTS if i == 0 else ("wq", "wkv", "we", "wvo")
            unpacked.update({f"{k}{i}": weight_specs[k] for k in used})
            kept.update({f"{k}{i}": weight_specs[k] for k in WEIGHTS if k not in used})
        else:
            flat = jnp.concatenate([near, far], axis=0)
            params.append(split_flat(jnp.take(flat, slot[i], axis=0).reshape(-1)))
    if in_rows:
        kept.update(got=((holders, PACK, 128), BF), sems=((2,), None))
        kept.update(nat)
    scratch = {**f_scratch, **a_scratch, "dn": ((4, 8, D), F32), **kept, **{k + "1": saved[k] for k in small}}
    scratch["z"] = ((rows, D), F32)
    two = call(
        front,
        {
            "slot": slot,
            **loose,
            **{f"{k}{i}": x[k] for i, x in enumerate(params) for k in WEIGHTS},
            **halves_of("leaves", "edges", "lcot", "ecot"),
            **base,
            "xc": centers[0],
            "gyc": center_cot[0],
        },
        {
            "yc0": ((stars, D), F32),
            "yc": ((stars, D), F32),
            **leaf_shapes(leaf_rows, "yl0", "en0"),
            **leaf_shapes(own_rows, "yl", "en"),
            **unpacked,
            **saved,
            **handed,
            **grads_out,
        },
        scratch,
        60,
        leaf_rows,
        in_smem=("slot",),
        lazy=lazy,
        joins=joined("xl", "el", "gyl", "ge"),
        own=("yl", "en"),
        name="front",
        loose=loose,
        early=start_first if in_rows else None,
    )
    one = two
    if in_rows:
        params = [Bag({k[:-1]: two[k] for k in unpacked if k[-1] == str(i)}) for i in range(LAYERS)]
    two_in = dict(xc=two.yc0, xl=two.yl0, el=two.en0, **halves_of("ecot"))

    def inputs_of(params, given, made, joins, out_rows, dtype, name):
        return call(
            lambda r: backward_inputs(r, stars, leaf_rows),
            {
                **{k: params[k] for k in ("wvo", "wkv", "we", "wq")},
                **{k: base[k] for k in ("idc", "idr")},
                **given,
                **{k: made[k] for k in handed},
            },
            {"gxc": ((stars, D), F32), "gxl": ((out_rows, D), dtype), "gel": ((out_rows, D), dtype)},
            {"xcat": ((2 * stars, D), BF)},
            9,
            leaf_rows,
            lazy=lazy,
            joins=joins,
            own=("gxl", "gel") if out_rows == own_rows else (),
            name=name,
        )

    def begin(made):
        if not in_rows:
            flat = jnp.swapaxes(made.nat[:, :ROWS_LAYER], 0, 1).reshape(ROWS_LAYER, 384)
            flat = flat[:, :D].reshape(holders, block_len)
            placed = jnp.zeros_like(flat).at[slot[0]].set(flat).astype(BF)
            return [reduce_step(([(placed, 0)], holders), orders[0][0], sizes)]
        got = exchange(made.send, orders[0][0], 1, sizes)
        count = holders // 2
        return [([(made.keep, i), (got, i)], count) for i in (0, count)]

    def advance(held, n):
        return [reduce_step(h, o[n], sizes) for h, o in zip(held, orders, strict=False)]

    def finish(helds):
        flat = [h for held in helds for h in held]
        rows = flat[0][1]
        both = jnp.concatenate([total(h, 0, rows) for h in flat], axis=1)
        block = total(reduce_step(([(both, 0)], rows), orders[0][-1], sizes), 0, 1)[0]
        parts = jnp.split(block, LAYERS)
        return jnp.stack([from_rows(x, block_rows) if in_rows else x for x in parts])

    held_two = begin(two)
    two_grads = inputs_of(params[1], two_in, two, joined("ge"), leaf_rows, BF, "last_inputs")
    held_two, (gyc,) = tie(held_two, two_grads.gxc)
    held_two = advance(held_two, 1)
    made = {"dz": handed["dz"], **ffn_scratch(stars, leaf_rows)}
    mid = call(
        lambda r: backward_ffn(r, stars, leaf_rows, own_rows),
        {
            "w2": params[0].w2,
            "gyl": two_grads.gxl,
            **{k: one[k] for k in ("xh2", "slope")},
            "w1": params[0].w1,
            "xh1": one.xh1,
            "norm": params[0].norm,
            "cown": base.cown,
            "gyc": gyc,
        },
        made,
        {},
        13,
        leaf_rows,
        lazy=lazy,
        name="first_ffn",
    )
    held_two, (dn,) = tie(held_two, mid.dn)
    if n_steps > 2:
        held_two = advance(held_two, 2)
    ffn_names = ("xh2", "slope", "xh1")
    three = call(
        end_grads,
        {
            **{k: params[0][k] for k in ("wo", "wkv")},
            **mid,
            **{k: one[k] for k in saved if k not in ffn_names},
            **halves_of("leaves", "edges"),
            **base,
            "slot": slot,
            "xc": centers[0],
            "ge": two_grads.gel,
            "dn": dn,
        },
        {**{k: handed[k] for k in handed if k != "dz"}, **grads_out},
        {**a_scratch, **grads_scratch},
        18,
        leaf_rows,
        in_smem=("slot",),
        lazy=lazy,
        joins=joined("xl", "el"),
        name="first",
    )
    three["dz"] = mid.dz
    held_three = begin(three)
    yl, en, yc, _ = lax.optimization_barrier((two.yl, two.en, two.yc, three.dq))
    held_three, (dq,) = tie(held_three, three.dq)
    handed_three = {**{k: three[k] for k in handed}, "dq": dq}
    held_three = advance(held_three, 1)
    three_in = dict(xc=centers[0], ge=two_grads.gel, **halves_of("leaves", "edges"))
    three_grads = inputs_of(
        params[0], three_in, handed_three, joined("xl", "el"), own_rows, F32, "first_inputs"
    )
    held_three, (gxc, yc) = tie(held_three, three_grads.gxc, yc)
    center_rows = jnp.where(star_own, jnp.concatenate([yc, gxc], axis=1), 0.0)
    center_rows = center_rows + exchange(center_rows, ("leaf", 0, 1), 1, sizes)
    held_three = advance(held_three, 2) if n_steps > 3 else held_three
    for n in range(3, n_steps - 1):
        held_two = advance(held_two, n)
        held_three = advance(held_three, n)
    held_three, (gxl, gel, center_rows) = tie(
        held_three, three_grads.gxl, three_grads.gel, center_rows
    )
    for bit in range(1, leaf_bits):
        center_rows = center_rows + exchange(center_rows, ("leaf", bit, 1), 1, sizes)
    centers_out, grad_centers = center_rows[:, :D].astype(BF), center_rows[:, D:]
    grad_total = finish([held_three, held_two])
    first_new = BETA_ONE * first_moment + (1.0 - BETA_ONE) * grad_total
    second_new = BETA_TWO * second_moment + (1.0 - BETA_TWO) * grad_total * grad_total
    step_one = first_new / (1.0 - BETA_ONE**STEP)
    step_two = second_new / (1.0 - BETA_TWO**STEP)
    weights_new = weights - RATE * (step_one / (jnp.sqrt(step_two) + EPS_ADAM) + DECAY * weights)
    return (
        centers_out[None],
        yl[None],
        en[None],
        grad_centers[None],
        gxl[None],
        gel[None],
        first_new,
        second_new,
        weights_new,
        weights_new.astype(BF),
        grad_total,
    )


def solution(mesh):
    both = ("graph", "leaf")
    return jax.shard_map(
        local,
        mesh=mesh,
        in_specs=(
            P(None, both),
            P(None, both),
            P(None, both),
            P("graph", None, None),
            P("graph", "leaf", None),
            P("graph", "leaf", None),
            P("graph", None, None),
            P("graph", "leaf", None),
            P("graph", "leaf", None),
            P("graph", "leaf"),
            P("graph", None),
            P("graph", "leaf"),
            P(),
        ),
        out_specs=(
            P("graph", None, None),
            P("graph", "leaf", None),
            P("graph", "leaf", None),
            P("graph", None, None),
            P("graph", "leaf", None),
            P("graph", "leaf", None),
            P(None, both),
            P(None, both),
            P(None, both),
            P(None, both),
            P(None, both),
        ),
        check_vma=False,
    )
```

profile of v0, /device:TPU:0, one launch (start us, length us, event | category | flops | bytes accessed | tf_op | source)
XLA Modules:
  0.0 210.8 jit_solution(2889488026041123863)
XLA Ops:
  0.7 1.1 convert_element_type.206
  1.8 0.8 slice_reduce_fusion
  3.3 5.1 %collective-permute-start.2 = (bf16[1,640,128]{2,1,0:T(8,128)(2,1)S(1)}, bf16[1,640,128]{2,1,0:T(8,128)(2,1)S(1)}, u32[]{:S(2)}, u32[]{:S(2)}) collective-permute-start(bf16[1,640,128]{2,1,0:T(8,128)(2,1)S(1)} %maximum_bitcast_fusion), channel_id=1, source_target_pairs={{0,24},{4,28},{8,16},{12,20},{16,8},{20,12},{24,0},{28,4},{1,25},{... | collective-permute-start | bytes 491528 | tf_op jit(solution)/shard_map/ppermute | solution.py:725
  9.9 2.5 %copy.101 = bf16[1,1024,300]{2,1,0:T(8,128)(2,1)} copy(bf16[1,1024,300]{1,2,0:T(8,128)(2,1)} %param.20) | data formatting | bytes 1228800 | tf_op jit(solution)/shard_map/optimization_barrier | solution.py:851
  12.4 1.5 copy.102
  13.9 0.7 fusion.10
  15.3 1.6 fusion.8
  18.2 1.3 collective-permute-start.10
  19.4 4.0 %collective-permute-start.9 = (bf16[528,300]{1,0:T(8,128)(2,1)}, bf16[528,300]{1,0:T(8,128)(2,1)}, u32[]{:S(2)}, u32[]{:S(2)}) collective-permute-start(bf16[528,300]{1,0:T(8,128)(2,1)} %get-tuple-element.278), channel_id=1, source_target_pairs={{0,1},{1,2},{2,3},{4,5},{5,6},{6,7},{8,9},{9,10},{10,11},{12,13},{... | collective-permute-start | bytes 950408 | tf_op jit(solution)/shard_map/ppermute | solution.py:803
  23.5 0.7 copy.112.refs_15_.refs_23_
  24.9 1.7 collective-permute-start.3
  26.7 1.5 collective-permute-start.6
  28.9 0.7 slice_convert_fusion.2
  29.6 5.5 %collective-permute-done.3 = bf16[4,320,128]{2,1,0:T(8,128)(2,1)S(1)} collective-permute-done((bf16[4,320,128]{2,1,0:T(8,128)(2,1)S(1)}, bf16[4,320,128]{2,1,0:T(8,128)(2,1)S(1)}, u32[]{:S(2)}, u32[]{:S(2)}) %collective-permute-start.3) | collective-permute-done | bytes 327712 | tf_op jit(solution)/shard_map/ppermute | solution.py:725
  36.4 1.0 collective-permute-start.7
  37.8 14.5 %collective-permute-done.7 = bf16[8,320,128]{2,1,0:T(8,128)(2,1)S(1)} collective-permute-done((bf16[8,320,128]{2,1,0:T(8,128)(2,1)S(1)}, bf16[8,320,128]{2,1,0:T(8,128)(2,1)S(1)}, u32[]{:S(2)}, u32[]{:S(2)}) %collective-permute-start.7) | collective-permute-done | bytes 655392 | tf_op jit(solution)/shard_map/ppermute | solution.py:725
  53.2 0.7 copy.113.refs_16_.refs_7_.refs_24_
  55.5 0.9 broadcast_add_fusion.refs_11_.refs_4_.refs_19_
  56.4 1.2 collective-permute-done.5.refs_2_
  57.6 52.2 %front.1 = (f32[80,300]{1,0:T(8,128)}, f32[80,300]{1,0:T(8,128)}, bf16[1280,300]{1,0:T(8,128)(2,1)}, bf16[1280,300]{1,0:T(8,128)(2,1)}, bf16[1024,300]{1,0:T(8,1...) custom-call(s32[2,32]{1,0:T(2,128)} %pad_add_fusion.1.refs_0_.refs_2, ...), custom_call_target="tpu_custom_call" | custom-call | flops 60000002048 | bytes 60000000 | tf_op jit(solution)/shard_map/front/pallas_call | solution.py:677
  110.0 9.0 %last_inputs.1 = (f32[80,300]{1,0:T(8,128)}, bf16[1280,300]{1,0:T(8,128)(2,1)}, bf16[1280,300]{1,0:T(8,128)(2,1)}) custom-call(bf16[300,300]{1,0:T(8,128)(2,1)} %get-tuple-element.114.refs_0_, bf16[300,684]{1,0:T(8,128)(2,1)} %get-tuple-element.115.refs_1_, bf16[300,300]{1,0:T(8,128)(2,1)} %get-tuple-element.116.refs_2_, ...), custom_call_target="tpu_custom_call" | custom-call | flops 8999999488 | bytes 9000000 | tf_op jit(solution)/shard_map/last_inputs/pallas_call | solution.py:677
  119.0 0.9 add_convert_fusion.2
  119.9 1.7 collective-permute-start.13
  121.7 2.2 %collective-permute-start.12 = (bf16[8,160,128]{2,1,0:T(8,128)(2,1)S(1)}, bf16[8,160,128]{2,1,0:T(8,128)(2,1)S(1)}, u32[]{:S(2)}, u32[]{:S(2)}) collective-permute-start(bf16[8,160,128]{2,1,0:T(8,128)(2,1)S(1)} %get-tuple-element.243), channel_id=1, source_target_pairs={{0,2},{1,3},{2,0},{3,1},{4,6},{5,7},{6,4},{7,5},{8,10},{9,11},{10,... | collective-permute-start | bytes 983048 | tf_op jit(solution)/shard_map/ppermute | solution.py:725
  123.9 12.2 %first_ffn.1 = (bf16[1360,300]{1,0:T(8,128)(2,1)}, f32[4,8,300]{2,1,0:T(8,128)}, bf16[1360,384]{1,0:T(8,128)(2,1)}, bf16[1360,1200]{1,0:T(8,128)(2,1)}) custom-call(bf16[1200,300]{1,0:T(8,128)(2,1)} %get-tuple-element.113.refs_0_, bf16[1280,300]{1,0:T(8,128)(2,1)} %get-tuple-element.125.refs_1_, bf16[1360,384]{1,0:T(8,128)(2,1)} %get-tuple-element.126.refs_2_, ...), custom_call_target="tpu_custom_call" | custom-call | flops 12999999488 | bytes 13000000 | tf_op jit(solution)/shard_map/first_ffn/pallas_call | solution.py:677
  136.1 17.5 %first.1 = (bf16[1280,684]{1,0:T(8,128)(2,1)}, bf16[80,300]{1,0:T(8,128)(2,1)}, bf16[80,684]{1,0:T(8,128)(2,1)}, bf16[32,160,128]{2,1,0:T(8,128)(2,1)}, bf16[32,160,128]{2,1,0:T(8,128)(2,1)}) custom-call(bf16[300,300]{1,0:T(8,128)(2,1)} %get-tuple-element.111.refs_0_, bf16[300,684]{1,0:T(8,128)(2,1)} %get-tuple-element.112.refs_1_, ...), custom_call_target="tpu_custom_call" | custom-call | flops 17999998976 | bytes 18000000 | tf_op jit(solution)/shard_map/first/pallas_call | solution.py:677
  154.1 6.3 %collective-permute-done.21 = bf16[4,160,128]{2,1,0:T(8,128)(2,1)S(1)} collective-permute-done((bf16[4,160,128]{2,1,0:T(8,128)(2,1)S(1)}, bf16[4,160,128]{2,1,0:T(8,128)(2,1)S(1)}, u32[]{:S(2)}, u32[]{:S(2)}) %collective-permute-start.21) | collective-permute-done | bytes 163872 | tf_op jit(solution)/shard_map/ppermute | solution.py:725
  160.7 1.2 add_convert_fusion
  162.2 2.0 collective-permute-start.15
  164.3 9.8 %first_inputs.1 = (f32[80,300]{1,0:T(8,128)}, f32[1024,300]{1,0:T(8,128)}, f32[1024,300]{1,0:T(8,128)}) custom-call(bf16[300,300]{1,0:T(8,128)(2,1)} %get-tuple-element.157.refs_0_, bf16[300,684]{1,0:T(8,128)(2,1)} %get-tuple-element.112.refs_1_, bf16[300,300]{1,0:T(8,128)(2,1)} %get-tuple-element.158.refs_2_, bf16[300,300]{1,0:T(8,128)(2,1)} %get-tuple-element.159.refs_3_, ...), custom_call_target="tpu_custom_call" | custom-call | flops 8999999488 | bytes 9000000 | tf_op jit(solution)/shard_map/first_inputs/pallas_call | solution.py:677
  174.1 1.1 maximum_select_fusion
  175.3 1.4 add_convert_fusion.6
  176.8 1.8 collective-permute-start.17
  178.6 1.0 convert_add_fusion
  179.7 3.7 %collective-permute-done.18 = bf16[4,160,128]{2,1,0:T(8,128)(2,1)S(1)} collective-permute-done((bf16[4,160,128]{2,1,0:T(8,128)(2,1)S(1)}, bf16[4,160,128]{2,1,0:T(8,128)(2,1)S(1)}, u32[]{:S(2)}, u32[]{:S(2)}) %collective-permute-start.18) | collective-permute-done | bytes 163872 | tf_op jit(solution)/shard_map/ppermute | solution.py:725
  183.5 1.4 convert_add_fusion.3
  185.0 0.8 fusion.27
  185.7 1.3 collective-permute-start.23
  187.0 2.4 %collective-permute-start.25 = (bf16[1,640,128]{2,1,0:T(8,128)(2,1)}, bf16[1,640,128]{2,1,0:T(8,128)(2,1)S(1)}, u32[]{:S(2)}, u32[]{:S(2)}) collective-permute-start(bf16[1,640,128]{2,1,0:T(8,128)(2,1)} %get-tuple-element.253), channel_id=1, source_target_pairs={{0,24},{4,28},{8,16},{12,20},{16,8},{20,12},{24,0},{28,4},{1,25},{... | collective-permute-start | bytes 491528 | tf_op jit(solution)/shard_map/ppermute | solution.py:725
  189.9 1.1 copy.117
  191.0 1.1 copy.118
  192.1 4.0 %copy.119 = f32[1,1024,300]{1,0,2:T(1,128)} copy(f32[1,1024,300]{2,1,0:T(8,128)} %bitcast.76) | data formatting | bytes 2457600
  196.1 2.0 copy.120
  198.2 1.7 collective-permute-start.20
  199.9 4.6 %collective-permute-done.24 = bf16[1,640,128]{2,1,0:T(8,128)(2,1)} collective-permute-done((bf16[1,640,128]{2,1,0:T(8,128)(2,1)}, bf16[1,640,128]{2,1,0:T(8,128)(2,1)}, u32[]{:S(2)}, u32[]{:S(2)}) %collective-permute-start.24) | collective-permute-done | bytes 163872 | tf_op jit(solution)/shard_map/ppermute | solution.py:725
  204.6 1.0 fusion.1
  206.7 2.4 %fusion.25 = (bf16[2,36600]{1,0:T(2,128)(2,1)}, f32[2,36600]{1,0:T(2,128)}, f32[2,36600]{1,0:T(2,128)}, f32[2,36600]{1,0:T(2,128)}, f32[2,36600]{1,0:T(2,128)}) fusion(f32[2,36600]{1,0:T(2,128)S(1)} %copy-done.7, f32[2,36600]{1,0:T(2,128)S(1)} %copy-done.14, f32[2,36600]{1,0:T(2,128)S(1)} %copy-done.15, f32[1,36600]{1,0:T(1,128)S(1)} %stack_reshape.7, ...), kind=kLoop, calls=%fused_computation.116 | loop fusion | flops 1244400 | bytes 2488800 | tf_op jit(solution)/shard_map/convert_element_type | solution.py:1129
  209.8 0.7 slice_bitcast_fusion.2
  (140 shorter events, 13.6 us)
Async XLA Ops:
  0.6 8.4 %copy-start.21 = (s32[1,1024]{1,0:T(1,128)S(1)}, s32[1,1024]{1,0:T(1,128)}, u32[]{:S(2)}) copy-start(s32[1,1024]{1,0:T(1,128)} %param.24) | copy-start | bytes 12292
  0.7 8.4 %copy-start.20 = (s32[1,1024]{1,0:T(1,128)S(1)}, s32[1,1024]{1,0:T(1,128)}, u32[]{:S(2)}) copy-start(s32[1,1024]{1,0:T(1,128)} %param.22) | copy-start | bytes 12292
  0.7 8.4 %copy-start.10 = (bf16[1,1024,300]{1,2,0:T(8,128)(2,1)S(1)}, bf16[1,1024,300]{1,2,0:T(8,128)(2,1)}, u32[]{:S(2)}) copy-start(bf16[1,1024,300]{1,2,0:T(8,128)(2,1)} %param.21) | copy-start | bytes 1843204
  3.1 6.4 %copy-start.11 = (bf16[1,1024,300]{1,2,0:T(8,128)(2,1)S(1)}, bf16[1,1024,300]{1,2,0:T(8,128)(2,1)}, u32[]{:S(2)}) copy-start(bf16[1,1024,300]{1,2,0:T(8,128)(2,1)} %param.18) | copy-start | bytes 1843204
  3.3 21.5 %collective-permute-start.2 = (bf16[1,640,128]{2,1,0:T(8,128)(2,1)S(1)}, bf16[1,640,128]{2,1,0:T(8,128)(2,1)S(1)}, u32[]{:S(2)}, u32[]{:S(2)}) collective-permute-start(bf16[1,640,128]{2,1,0:T(8,128)(2,1)S(1)} %maximum_bitcast_fusion), channel_id=1, source_target_pairs={{0,24},{4,28},{8,16},{12,20},{16,8},{20,12},{24,0},{28,4},{1,25},{... | collective-permute-start | bytes 491528 | tf_op jit(solution)/shard_map/ppermute | solution.py:725
  8.4 16.4 %collective-permute-start.1 = (bf16[1,640,128]{2,1,0:T(8,128)(2,1)S(1)}, bf16[1,640,128]{2,1,0:T(8,128)(2,1)S(1)}, u32[]{:S(2)}, u32[]{:S(2)}) collective-permute-start(bf16[1,640,128]{2,1,0:T(8,128)(2,1)S(1)} %maximum_bitcast_fusion), channel_id=1, source_target_pairs={{0,16},{4,20},{8,24},{12,28},{16,0},{20,4},{24,8},{28,12},{1,17},{... | collective-permute-start | bytes 491528 | tf_op jit(solution)/shard_map/ppermute | solution.py:725
  8.4 16.4 %collective-permute-start = (bf16[1,640,128]{2,1,0:T(8,128)(2,1)S(1)}, bf16[1,640,128]{2,1,0:T(8,128)(2,1)S(1)}, u32[]{:S(2)}, u32[]{:S(2)}) collective-permute-start(bf16[1,640,128]{2,1,0:T(8,128)(2,1)S(1)} %maximum_bitcast_fusion), channel_id=1, source_target_pairs={{0,8},{4,12},{8,0},{12,4},{16,24},{20,28},{24,16},{28,20},{1,9},{5... | collective-permute-start | bytes 491528 | tf_op jit(solution)/shard_map/ppermute | solution.py:725
  9.5 7.4 %copy-start.6 = (bf16[1,1024,300]{2,1,0:T(8,128)(2,1)}, bf16[1,1024,300]{2,1,0:T(8,128)(2,1)S(1)}, u32[]{:S(2)}) copy-start(bf16[1,1024,300]{2,1,0:T(8,128)(2,1)S(1)} %copy.99) | copy-start | bytes 1843204
  9.8 4.8 %copy-start.4 = (bf16[1,1024,300]{2,1,0:T(8,128)(2,1)}, bf16[1,1024,300]{2,1,0:T(8,128)(2,1)S(1)}, u32[]{:S(2)}) copy-start(bf16[1,1024,300]{2,1,0:T(8,128)(2,1)S(1)} %copy.100) | copy-start | bytes 1843204
  12.4 5.2 %copy-start.22 = (pred[300]{0:T(512)(128)(4,1)S(1)}, pred[300]{0:T(512)(128)(4,1)}, u32[]{:S(2)}) copy-start(pred[300]{0:T(512)(128)(4,1)} %constant.19.clone.1) | copy-start | bytes 904
  12.4 11.0 %copy-start.23 = (s32[32]{0:T(128)S(1)}, s32[32]{0:T(128)}, u32[]{:S(2)}) copy-start(s32[32]{0:T(128)} %param.25) | copy-start | bytes 388
  12.4 11.0 %copy-start.24 = (s32[1,80]{1,0:T(1,128)S(1)}, s32[1,80]{1,0:T(1,128)}, u32[]{:S(2)}) copy-start(s32[1,80]{1,0:T(1,128)} %param.23) | copy-start | bytes 964
  13.9 11.0 %copy-start.5 = (bf16[1,1024,300]{2,1,0:T(8,128)(2,1)}, bf16[1,1024,300]{2,1,0:T(8,128)(2,1)S(1)}, u32[]{:S(2)}) copy-start(bf16[1,1024,300]{2,1,0:T(8,128)(2,1)S(1)} %copy.102) | copy-start | bytes 1843204
  18.2 10.1 %collective-permute-start.10 = (bf16[528,300]{1,0:T(8,128)(2,1)S(1)}, bf16[528,300]{1,0:T(8,128)(2,1)}, u32[]{:S(2)}, u32[]{:S(2)}) collective-permute-start(bf16[528,300]{1,0:T(8,128)(2,1)S(1)} %get-tuple-element.277), channel_id=1, source_target_pairs={{1,0},{2,1},{3,2},{5,4},{6,5},{7,6},{9,8},{10,9},{11,10},{13,12},{... | collective-permute-start | bytes 950408 | tf_op jit(solution)/shard_map/ppermute | solution.py:804
  19.4 9.5 %collective-permute-start.9 = (bf16[528,300]{1,0:T(8,128)(2,1)}, bf16[528,300]{1,0:T(8,128)(2,1)}, u32[]{:S(2)}, u32[]{:S(2)}) collective-permute-start(bf16[528,300]{1,0:T(8,128)(2,1)} %get-tuple-element.278), channel_id=1, source_target_pairs={{0,1},{1,2},{2,3},{4,5},{5,6},{6,7},{8,9},{9,10},{10,11},{12,13},{... | collective-permute-start | bytes 950408 | tf_op jit(solution)/shard_map/ppermute | solution.py:803
  24.9 10.2 %collective-permute-start.3 = (bf16[4,320,128]{2,1,0:T(8,128)(2,1)S(1)}, bf16[4,320,128]{2,1,0:T(8,128)(2,1)S(1)}, u32[]{:S(2)}, u32[]{:S(2)}) collective-permute-start(bf16[4,320,128]{2,1,0:T(8,128)(2,1)S(1)} %get-tuple-element.103), channel_id=1, source_target_pairs={{0,4},{4,0},{8,12},{12,8},{16,20},{20,16},{24,28},{28,24},{1,5},{5... | collective-permute-start | bytes 983048 | tf_op jit(solution)/shard_map/ppermute | solution.py:725
  26.7 9.7 %collective-permute-start.6 = (bf16[4,320,128]{2,1,0:T(8,128)(2,1)S(1)}, bf16[4,320,128]{2,1,0:T(8,128)(2,1)S(1)}, u32[]{:S(2)}, u32[]{:S(2)}) collective-permute-start(bf16[4,320,128]{2,1,0:T(8,128)(2,1)S(1)} %get-tuple-element.104), channel_id=1, source_target_pairs={{0,2},{1,3},{2,0},{3,1},{4,6},{5,7},{6,4},{7,5},{8,10},{9,11},{10,... | collective-permute-start | bytes 983048 | tf_op jit(solution)/shard_map/ppermute | solution.py:725
  35.2 17.4 %collective-permute-start.4 = (bf16[8,320,128]{2,1,0:T(8,128)(2,1)S(1)}, bf16[8,320,128]{2,1,0:T(8,128)(2,1)S(1)}, u32[]{:S(2)}, u32[]{:S(2)}) collective-permute-start(bf16[8,320,128]{2,1,0:T(8,128)(2,1)S(1)} %pad_maximum_fusion.2), channel_id=1, source_target_pairs={{0,2},{1,3},{2,0},{3,1},{4,6},{5,7},{6,4},{7,5},{8,10},{9,11},{10,... | collective-permute-start | bytes 1966088 | tf_op jit(solution)/shard_map/ppermute | solution.py:725
  36.4 15.9 %collective-permute-start.7 = (bf16[8,320,128]{2,1,0:T(8,128)(2,1)S(1)}, bf16[8,320,128]{2,1,0:T(8,128)(2,1)S(1)}, u32[]{:S(2)}, u32[]{:S(2)}) collective-permute-start(bf16[8,320,128]{2,1,0:T(8,128)(2,1)S(1)} %pad_maximum_fusion.3), channel_id=1, source_target_pairs={{0,4},{4,0},{8,12},{12,8},{16,20},{20,16},{24,28},{28,24},{1,5},{5... | collective-permute-start | bytes 1966088 | tf_op jit(solution)/shard_map/ppermute | solution.py:725
  37.4 15.0 %copy-start.19 = (s32[1,1280]{1,0:T(1,128)}, s32[1,1280]{1,0:T(1,128)S(1)}, u32[]{:S(2)}) copy-start(s32[1,1280]{1,0:T(1,128)S(1)} %add_add_fusion.refs_12_.refs_5_.refs_20_) | copy-start | bytes 15364
  52.5 3.9 %copy-start.17 = (bf16[16,320,128]{2,1,0:T(8,128)(2,1)}, bf16[16,320,128]{2,1,0:T(8,128)(2,1)S(1)}, u32[]{:S(2)}) copy-start(bf16[16,320,128]{2,1,0:T(8,128)(2,1)S(1)} %constant_dynamic-update-slice_fusion.3.refs_3_) | copy-start | bytes 3932164
  52.5 3.9 %collective-permute-start.8 = (bf16[16,320,128]{2,1,0:T(8,128)(2,1)S(1)}, bf16[16,320,128]{2,1,0:T(8,128)(2,1)}, u32[]{:S(2)}, u32[]{:S(2)}) collective-permute-start(bf16[16,320,128]{2,1,0:T(8,128)(2,1)S(1)} %constant_dynamic-update-slice_fusion.3.refs_3_), channel_id=1, source_target_pairs={{0,1},{1,0},{2,3},{3,2},{4,5},{5,4},{6,7},{7,6},{8,9},{9,8},{10,11... | collective-permute-start | bytes 3932168 | tf_op jit(solution)/shard_map/ppermute | solution.py:725
  52.7 4.9 %copy-start.18 = (bf16[16,320,128]{2,1,0:T(8,128)(2,1)}, bf16[16,320,128]{2,1,0:T(8,128)(2,1)S(1)}, u32[]{:S(2)}) copy-start(bf16[16,320,128]{2,1,0:T(8,128)(2,1)S(1)} %constant_dynamic-update-slice_fusion.refs_1_) | copy-start | bytes 3932164
  52.7 4.9 %collective-permute-start.5 = (bf16[16,320,128]{2,1,0:T(8,128)(2,1)S(1)}, bf16[16,320,128]{2,1,0:T(8,128)(2,1)}, u32[]{:S(2)}, u32[]{:S(2)}) collective-permute-start(bf16[16,320,128]{2,1,0:T(8,128)(2,1)S(1)} %constant_dynamic-update-slice_fusion.refs_1_), channel_id=1, source_target_pairs={{0,1},{1,0},{2,3},{3,2},{4,5},{5,4},{6,7},{7,6},{8,9},{9,8},{10,11... | collective-permute-start | bytes 3932168 | tf_op jit(solution)/shard_map/ppermute | solution.py:725
  109.8 9.2 %collective-permute-start.11 = (bf16[32,160,128]{2,1,0:T(8,128)(2,1)}, bf16[32,160,128]{2,1,0:T(8,128)(2,1)S(1)}, u32[]{:S(2)}, u32[]{:S(2)}) collective-permute-start(bf16[32,160,128]{2,1,0:T(8,128)(2,1)} %get-tuple-element.131), channel_id=1, source_target_pairs={{0,1},{1,0},{2,3},{3,2},{4,5},{5,4},{6,7},{7,6},{8,9},{9,8},{10,11... | collective-permute-start | bytes 3932168 | tf_op jit(solution)/shard_map/ppermute | solution.py:725
  110.0 9.0 %copy-start.1 = (bf16[32,160,128]{2,1,0:T(8,128)(2,1)S(1)}, bf16[32,160,128]{2,1,0:T(8,128)(2,1)}, u32[]{:S(2)}) copy-start(bf16[32,160,128]{2,1,0:T(8,128)(2,1)} %get-tuple-element.135) | copy-start | bytes 3932164
  119.9 16.2 %collective-permute-start.13 = (bf16[8,160,128]{2,1,0:T(8,128)(2,1)}, bf16[8,160,128]{2,1,0:T(8,128)(2,1)S(1)}, u32[]{:S(2)}, u32[]{:S(2)}) collective-permute-start(bf16[8,160,128]{2,1,0:T(8,128)(2,1)} %get-tuple-element.242), channel_id=1, source_target_pairs={{0,4},{4,0},{8,12},{12,8},{16,20},{20,16},{24,28},{28,24},{1,5},{5... | collective-permute-start | bytes 983048 | tf_op jit(solution)/shard_map/ppermute | solution.py:725
  121.7 14.4 %collective-permute-start.12 = (bf16[8,160,128]{2,1,0:T(8,128)(2,1)S(1)}, bf16[8,160,128]{2,1,0:T(8,128)(2,1)S(1)}, u32[]{:S(2)}, u32[]{:S(2)}) collective-permute-start(bf16[8,160,128]{2,1,0:T(8,128)(2,1)S(1)} %get-tuple-element.243), channel_id=1, source_target_pairs={{0,2},{1,3},{2,0},{3,1},{4,6},{5,7},{6,4},{7,5},{8,10},{9,11},{10,... | collective-permute-start | bytes 983048 | tf_op jit(solution)/shard_map/ppermute | solution.py:725
  153.6 7.1 %copy-start.2 = (bf16[32,160,128]{2,1,0:T(8,128)(2,1)S(1)}, bf16[32,160,128]{2,1,0:T(8,128)(2,1)}, u32[]{:S(2)}) copy-start(bf16[32,160,128]{2,1,0:T(8,128)(2,1)} %get-tuple-element.152) | copy-start | bytes 3932164
  153.6 7.1 %collective-permute-start.14 = (bf16[32,160,128]{2,1,0:T(8,128)(2,1)}, bf16[32,160,128]{2,1,0:T(8,128)(2,1)S(1)}, u32[]{:S(2)}, u32[]{:S(2)}) collective-permute-start(bf16[32,160,128]{2,1,0:T(8,128)(2,1)} %get-tuple-element.153), channel_id=1, source_target_pairs={{0,1},{1,0},{2,3},{3,2},{4,5},{5,4},{6,7},{7,6},{8,9},{9,8},{10,11... | collective-permute-start | bytes 3932168 | tf_op jit(solution)/shard_map/ppermute | solution.py:725
  153.8 6.7 %collective-permute-start.21 = (bf16[4,160,128]{2,1,0:T(8,128)(2,1)S(1)}, bf16[4,160,128]{2,1,0:T(8,128)(2,1)S(1)}, u32[]{:S(2)}, u32[]{:S(2)}) collective-permute-start(bf16[4,160,128]{2,1,0:T(8,128)(2,1)S(1)} %add_convert_fusion.5), channel_id=1, source_target_pairs={{0,4},{4,0},{8,12},{12,8},{16,20},{20,16},{24,28},{28,24},{1,5},{5... | collective-permute-start | bytes 491528 | tf_op jit(solution)/shard_map/ppermute | solution.py:725
  160.6 18.0 %collective-permute-start.22 = (bf16[4,160,128]{2,1,0:T(8,128)(2,1)S(1)}, bf16[4,160,128]{2,1,0:T(8,128)(2,1)}, u32[]{:S(2)}, u32[]{:S(2)}) collective-permute-start(bf16[4,160,128]{2,1,0:T(8,128)(2,1)S(1)} %get-tuple-element.237), channel_id=1, source_target_pairs={{0,2},{1,3},{2,0},{3,1},{4,6},{5,7},{6,4},{7,5},{8,10},{9,11},{10,... | collective-permute-start | bytes 491528 | tf_op jit(solution)/shard_map/ppermute | solution.py:725
  160.7 1.3 copy-start.3
  162.0 12.1 %collective-permute-start.16 = (bf16[8,160,128]{2,1,0:T(8,128)(2,1)}, bf16[8,160,128]{2,1,0:T(8,128)(2,1)S(1)}, u32[]{:S(2)}, u32[]{:S(2)}) collective-permute-start(bf16[8,160,128]{2,1,0:T(8,128)(2,1)} %get-tuple-element.240), channel_id=1, source_target_pairs={{0,4},{4,0},{8,12},{12,8},{16,20},{20,16},{24,28},{28,24},{1,5},{5... | collective-permute-start | bytes 983048 | tf_op jit(solution)/shard_map/ppermute | solution.py:725
  162.2 11.9 %collective-permute-start.15 = (bf16[8,160,128]{2,1,0:T(8,128)(2,1)}, bf16[8,160,128]{2,1,0:T(8,128)(2,1)}, u32[]{:S(2)}, u32[]{:S(2)}) collective-permute-start(bf16[8,160,128]{2,1,0:T(8,128)(2,1)} %get-tuple-element.241), channel_id=1, source_target_pairs={{0,2},{1,3},{2,0},{3,1},{4,6},{5,7},{6,4},{7,5},{8,10},{9,11},{10,... | collective-permute-start | bytes 983048 | tf_op jit(solution)/shard_map/ppermute | solution.py:725
  164.2 9.9 %copy-start.16 = (f32[80,300]{1,0:T(8,128)S(1)}, f32[80,300]{1,0:T(8,128)}, u32[]{:S(2)}) copy-start(f32[80,300]{1,0:T(8,128)} %get-tuple-element.172) | copy-start | bytes 288004
  174.1 4.5 %copy-start.12 = (bf16[8,160,128]{2,1,0:T(8,128)(2,1)}, bf16[8,160,128]{2,1,0:T(8,128)(2,1)S(1)}, u32[]{:S(2)}) copy-start(bf16[8,160,128]{2,1,0:T(8,128)(2,1)S(1)} %collective-permute-done.16) | copy-start | bytes 983044
  175.3 4.4 %collective-permute-start.19 = (f32[80,600]{1,0:T(8,128)S(1)}, f32[80,600]{1,0:T(8,128)S(1)}, u32[]{:S(2)}, u32[]{:S(2)}) collective-permute-start(f32[80,600]{1,0:T(8,128)S(1)} %maximum_select_fusion), channel_id=1, source_target_pairs={{0,1},{1,0},{2,3},{3,2},{4,5},{5,4},{6,7},{7,6},{8,9},{9,8},{10,11... | collective-permute-start | bytes 576008 | tf_op jit(solution)/shard_map/ppermute | solution.py:725
  176.7 6.7 %collective-permute-start.18 = (bf16[4,160,128]{2,1,0:T(8,128)(2,1)S(1)}, bf16[4,160,128]{2,1,0:T(8,128)(2,1)S(1)}, u32[]{:S(2)}, u32[]{:S(2)}) collective-permute-start(bf16[4,160,128]{2,1,0:T(8,128)(2,1)S(1)} %get-tuple-element.238), channel_id=1, source_target_pairs={{0,2},{1,3},{2,0},{3,1},{4,6},{5,7},{6,4},{7,5},{8,10},{9,11},{10,... | collective-permute-start | bytes 491528 | tf_op jit(solution)/shard_map/ppermute | solution.py:725
  176.8 6.7 %collective-permute-start.17 = (bf16[4,160,128]{2,1,0:T(8,128)(2,1)S(1)}, bf16[4,160,128]{2,1,0:T(8,128)(2,1)S(1)}, u32[]{:S(2)}, u32[]{:S(2)}) collective-permute-start(bf16[4,160,128]{2,1,0:T(8,128)(2,1)S(1)} %get-tuple-element.239), channel_id=1, source_target_pairs={{0,4},{4,0},{8,12},{12,8},{16,20},{20,16},{24,28},{28,24},{1,5},{5... | collective-permute-start | bytes 491528 | tf_op jit(solution)/shard_map/ppermute | solution.py:725
  178.6 4.9 %copy-start.13 = (bf16[8,160,128]{2,1,0:T(8,128)(2,1)S(1)}, bf16[8,160,128]{2,1,0:T(8,128)(2,1)}, u32[]{:S(2)}) copy-start(bf16[8,160,128]{2,1,0:T(8,128)(2,1)} %copy-done.12) | copy-start | bytes 983044
  184.8 5.1 %copy-start.9 = (bf16[1024,300]{1,0:T(8,128)(2,1)S(1)}, bf16[1024,300]{1,0:T(8,128)(2,1)}, u32[]{:S(2)}) copy-start(bf16[1024,300]{1,0:T(8,128)(2,1)} %get-tuple-element.175) | copy-start | bytes 1843204
  184.9 6.1 %copy-start.8 = (bf16[1024,300]{1,0:T(8,128)(2,1)S(1)}, bf16[1024,300]{1,0:T(8,128)(2,1)}, u32[]{:S(2)}) copy-start(bf16[1024,300]{1,0:T(8,128)(2,1)} %get-tuple-element.176) | copy-start | bytes 1843204
  185.7 14.2 %collective-permute-start.23 = (bf16[1,640,128]{2,1,0:T(8,128)(2,1)}, bf16[1,640,128]{2,1,0:T(8,128)(2,1)S(1)}, u32[]{:S(2)}, u32[]{:S(2)}) collective-permute-start(bf16[1,640,128]{2,1,0:T(8,128)(2,1)} %get-tuple-element.252), channel_id=1, source_target_pairs={{0,8},{4,12},{8,0},{12,4},{16,24},{20,28},{24,16},{28,20},{1,9},{5... | collective-permute-start | bytes 491528 | tf_op jit(solution)/shard_map/ppermute | solution.py:725
  187.0 12.9 %collective-permute-start.25 = (bf16[1,640,128]{2,1,0:T(8,128)(2,1)}, bf16[1,640,128]{2,1,0:T(8,128)(2,1)S(1)}, u32[]{:S(2)}, u32[]{:S(2)}) collective-permute-start(bf16[1,640,128]{2,1,0:T(8,128)(2,1)} %get-tuple-element.253), channel_id=1, source_target_pairs={{0,24},{4,28},{8,16},{12,20},{16,8},{20,12},{24,0},{28,4},{1,25},{... | collective-permute-start | bytes 491528 | tf_op jit(solution)/shard_map/ppermute | solution.py:725
  189.4 15.2 %collective-permute-start.24 = (bf16[1,640,128]{2,1,0:T(8,128)(2,1)}, bf16[1,640,128]{2,1,0:T(8,128)(2,1)}, u32[]{:S(2)}, u32[]{:S(2)}) collective-permute-start(bf16[1,640,128]{2,1,0:T(8,128)(2,1)} %get-tuple-element.254), channel_id=1, source_target_pairs={{0,16},{4,20},{8,24},{12,28},{16,0},{20,4},{24,8},{28,12},{1,17},{... | collective-permute-start | bytes 491528 | tf_op jit(solution)/shard_map/ppermute | solution.py:725
  192.1 4.0 %copy-start = (f32[1024,300]{1,0:T(8,128)S(1)}, f32[1024,300]{1,0:T(8,128)}, u32[]{:S(2)}) copy-start(f32[1024,300]{1,0:T(8,128)} %get-tuple-element.178) | copy-start | bytes 3686404
  198.2 11.0 %collective-permute-start.20 = (f32[80,600]{1,0:T(8,128)S(1)}, f32[80,600]{1,0:T(8,128)S(1)}, u32[]{:S(2)}, u32[]{:S(2)}) collective-permute-start(f32[80,600]{1,0:T(8,128)S(1)} %add.151), channel_id=1, source_target_pairs={{0,2},{1,3},{2,0},{3,1},{4,6},{5,7},{6,4},{7,5},{8,10},{9,11},{10,... | collective-permute-start | bytes 576008 | tf_op jit(solution)/shard_map/ppermute | solution.py:725
  (3 other events, 3.1 us)
where the time goes:
time: 214 us; the launch traced here: 211 us
  Pallas kernels  101 us (47%)
  waiting for transfers between devices  36.6 us (17%)
  starting transfers between devices  31.1 us (15%)
  local copies, waits for them, and re-layouts  23.4 us (11%)
  other arithmetic  17.3 us (8%)
    pallas_call x5, Pallas kernels, call(): pl.pallas_call(kernel, out_shape=[jax.ShapeDtypeStruct(s, d) for s, d in...  101 us
    ppermute x24, waiting for transfers between devices, exchange(): lax.ppermute(x, axis, [(i, i ^ value << shift) for i in range(sizes[axis])])  36.6 us
    ppermute x24, starting transfers between devices, exchange(): lax.ppermute(x, axis, [(i, i ^ value << shift) for i in range(sizes[axis])])  25.9 us
    unnamed x62, local copies, waits for them, and re-layouts  12.4 us
    optimization_barrier x4, local copies, waits for them, and re-layouts, local(): lax.optimization_barrier((rows, leaves, edge_feats, leaf_cot, edge_cot, g...  4.7 us
  transfers between devices with their start and end apart: 26, of which 8 were waited for; matrix products, arithmetic and copies ran while one was open for 16% of the time, Pallas kernels for 15%

commit v1 on v0

--- a/solution.py
+++ b/solution.py
@@ -365,13 +365,13 @@
     nat_store(nat, pl.ds(3 * D, D), out)
     nat_store(nat, pl.ds(4 * D, D), tn(r.el[own_leaf, :], r.ge[own_leaf, :]))
     base = 5 * D
+    whole = tn(r.hb[HALO:, :], r.dpre[HALO:, :])
     for j in range(FF // D):
-        columns = slice(j * D, (j + 1) * D)
-        part = tn(r.hb[HALO:, :], r.dpre[HALO:, columns])
+        part = whole[:, j * D : (j + 1) * D]
         nat_store(nat, pl.ds(base + j, D, stride=FF // D), part)
     base = base + FF
     for lo, hi in CHUNKS:
-        part = tn(r.act[HALO:, lo:hi], r.dbr[HALO:, 0:D])
+        part = tn(r.dbr[HALO:, 0:D], r.act[HALO:, lo:hi]).T
         nat_store(nat, pl.ds(base + lo, hi - lo), part)
     base = base + FF
     sums = [jnp.sum(r.dn[i], axis=0, keepdims=True) for i in range(4)]
@@ -1029,13 +1029,17 @@
     def advance(held, n):
         return [reduce_step(h, o[n], sizes) for h, o in zip(held, orders, strict=False)]
 
-    def finish(helds):
-        flat = [h for held in helds for h in held]
-        rows = flat[0][1]
-        both = jnp.concatenate([total(h, 0, rows) for h in flat], axis=1)
-        block = total(reduce_step(([(both, 0)], rows), orders[0][-1], sizes), 0, 1)[0]
-        parts = jnp.split(block, LAYERS)
-        return jnp.stack([from_rows(x, block_rows) if in_rows else x for x in parts])
+    def joined_total(held):
+        rows = held[0][1]
+        both = jnp.concatenate([total(h, 0, rows) for h in held], axis=1)
+        return [([(both.astype(BF), 0)], rows)]
+
+    def last_step(held):
+        return reduce_step(held[0], orders[0][-1], sizes)
+
+    def end(held):
+        block = total(held, 0, 1)[0]
+        return from_rows(block, block_rows) if in_rows else block
 
     held_two = begin(two)
     two_grads = inputs_of(params[1], two_in, two, joined("ge"), leaf_rows, BF, "last_inputs")
@@ -1088,29 +1092,38 @@
         name="first",
     )
     three["dz"] = mid.dz
+    for n in range(3, n_steps - 1):
+        held_two = advance(held_two, n)
+    key = "send" if in_rows else "nat"
+    held_two, (three[key],) = tie(held_two, three[key])
     held_three = begin(three)
-    yl, en, yc, _ = lax.optimization_barrier((two.yl, two.en, two.yc, three.dq))
-    held_three, (dq,) = tie(held_three, three.dq)
+    held_two = joined_total(held_two)
+    count = len(held_two)
+    both, (dq,) = tie(held_two + held_three, three.dq)
+    held_three = both[count:]
+    last_two = last_step(both[:count])
     handed_three = {**{k: three[k] for k in handed}, "dq": dq}
     held_three = advance(held_three, 1)
     three_in = dict(xc=centers[0], ge=two_grads.gel, **halves_of("leaves", "edges"))
     three_grads = inputs_of(
         params[0], three_in, handed_three, joined("xl", "el"), own_rows, F32, "first_inputs"
     )
-    held_three, (gxc, yc) = tie(held_three, three_grads.gxc, yc)
+    late = [x for x, _ in last_two[0][1:]]
+    held_three, (gxc, yc, *late) = tie(held_three, three_grads.gxc, two.yc, *late)
+    last_two = (last_two[0][:1] + [(x, 0) for x in late], last_two[1])
     center_rows = jnp.where(star_own, jnp.concatenate([yc, gxc], axis=1), 0.0)
     center_rows = center_rows + exchange(center_rows, ("leaf", 0, 1), 1, sizes)
     held_three = advance(held_three, 2) if n_steps > 3 else held_three
     for n in range(3, n_steps - 1):
-        held_two = advance(held_two, n)
         held_three = advance(held_three, n)
-    held_three, (gxl, gel, center_rows) = tie(
-        held_three, three_grads.gxl, three_grads.gel, center_rows
+    held_three, (gxl, gel, yl, en, center_rows) = tie(
+        held_three, three_grads.gxl, three_grads.gel, two.yl, two.en, center_rows
     )
     for bit in range(1, leaf_bits):
         center_rows = center_rows + exchange(center_rows, ("leaf", bit, 1), 1, sizes)
     centers_out, grad_centers = center_rows[:, :D].astype(BF), center_rows[:, D:]
-    grad_total = finish([held_three, held_two])
+    lasts, _ = tie([last_step(joined_total(held_three)), last_two])
+    grad_total = jnp.stack([end(x) for x in lasts])
     first_new = BETA_ONE * first_moment + (1.0 - BETA_ONE) * grad_total
     second_new = BETA_TWO * second_moment + (1.0 - BETA_TWO) * grad_total * grad_total
     step_one = first_new / (1.0 - BETA_ONE**STEP)

time: 214 us -> 208 us (0.972)
  waiting for transfers between devices: 36.6 us -> 28.4 us
  starting transfers between devices: 31.1 us -> 35.4 us
  Pallas kernels: 101 us -> 98.4 us
    ppermute x24 -> x27, waiting for transfers between devices: 36.6 us -> 28.4 us  [exchange(): lax.ppermute(x, axis, [(i, i ^ value << shift) for i in range(sizes[axis])])]
    ppermute x24 -> x27, starting transfers between devices: 25.9 us -> 30.2 us  [exchange(): lax.ppermute(x, axis, [(i, i ^ value << shift) for i in range(sizes[axis])])]
    convert_element_type x4, other arithmetic: 3.52 us -> 0.61 us  [reduce_step(): total(held, v * count, (v + 1) * count).astype(BF)]
    pallas_call x5, Pallas kernels: 101 us -> 98.4 us  [call(): pl.pallas_call(kernel, out_shape=[jax.ShapeDtypeStruct(s, d) for s, d in...]
    unnamed x62 -> x66, local copies, waits for them, and re-layouts: 12.4 us -> 12 us
  transfers between devices with their start and end apart: 26 -> 29, of which waited for: 8 -> 8; matrix products, arithmetic and copies ran while one was open for 16% -> 16% of each run, Pallas kernels for 15% -> 23%
where the time goes in v1:
time: 208 us; the launch traced here: 205 us
  Pallas kernels  98.4 us (47%)
  starting transfers between devices  35.4 us (17%)
  waiting for transfers between devices  28.4 us (14%)
  local copies, waits for them, and re-layouts  22.9 us (11%)
  other arithmetic  17.7 us (9%)
    pallas_call x5, Pallas kernels, call(): pl.pallas_call(kernel, out_shape=[jax.ShapeDtypeStruct(s, d) for s, d in...  98.4 us
    ppermute x27, starting transfers between devices, exchange(): lax.ppermute(x, axis, [(i, i ^ value << shift) for i in range(sizes[axis])])  30.2 us
    ppermute x27, waiting for transfers between devices, exchange(): lax.ppermute(x, axis, [(i, i ^ value << shift) for i in range(sizes[axis])])  28.4 us
    unnamed x66, local copies, waits for them, and re-layouts  12 us
    optimization_barrier x4, local copies, waits for them, and re-layouts, local(): lax.optimization_barrier((rows, leaves, edge_feats, leaf_cot, edge_cot, g...  4.68 us
  transfers between devices with their start and end apart: 29, of which 8 were waited for; matrix products, arithmetic and copies ran while one was open for 16% of the time, Pallas kernels for 23%

profile of v1, /device:TPU:0, one launch (start us, length us, event | category | flops | bytes accessed | tf_op | source)
XLA Modules:
  0.0 204.6 jit_solution(4089282512528891501)
XLA Ops:
  0.7 1.1 convert_element_type.232
  1.8 0.8 slice_reduce_fusion
  3.3 5.1 %collective-permute-start.2 = (bf16[1,640,128]{2,1,0:T(8,128)(2,1)S(1)}, bf16[1,640,128]{2,1,0:T(8,128)(2,1)S(1)}, u32[]{:S(2)}, u32[]{:S(2)}) collective-permute-start(bf16[1,640,128]{2,1,0:T(8,128)(2,1)S(1)} %maximum_bitcast_fusion), channel_id=1, source_target_pairs={{0,24},{4,28},{8,16},{12,20},{16,8},{20,12},{24,0},{28,4},{1,25},{... | collective-permute-start | bytes 491528 | tf_op jit(solution)/shard_map/ppermute | solution.py:725
  9.9 2.5 %copy.101 = bf16[1,1024,300]{2,1,0:T(8,128)(2,1)} copy(bf16[1,1024,300]{1,2,0:T(8,128)(2,1)} %param.20) | data formatting | bytes 1228800 | tf_op jit(solution)/shard_map/optimization_barrier | solution.py:851
  12.4 1.5 copy.102
  13.9 0.7 fusion.8
  15.2 1.6 fusion.6
  18.1 1.3 collective-permute-start.10
  19.4 4.0 %collective-permute-start.9 = (bf16[528,300]{1,0:T(8,128)(2,1)}, bf16[528,300]{1,0:T(8,128)(2,1)}, u32[]{:S(2)}, u32[]{:S(2)}) collective-permute-start(bf16[528,300]{1,0:T(8,128)(2,1)} %get-tuple-element.297), channel_id=1, source_target_pairs={{0,1},{1,2},{2,3},{4,5},{5,6},{6,7},{8,9},{9,10},{10,11},{12,13},{... | collective-permute-start | bytes 950408 | tf_op jit(solution)/shard_map/ppermute | solution.py:803
  23.4 0.7 copy.112.refs_15_.refs_23_
  24.7 1.0 pad_maximum_fusion
  25.8 1.7 collective-permute-start.3
  27.5 1.5 collective-permute-start.6
  30.4 5.5 %collective-permute-done.3 = bf16[4,320,128]{2,1,0:T(8,128)(2,1)S(1)} collective-permute-done((bf16[4,320,128]{2,1,0:T(8,128)(2,1)S(1)}, bf16[4,320,128]{2,1,0:T(8,128)(2,1)S(1)}, u32[]{:S(2)}, u32[]{:S(2)}) %collective-permute-start.3) | collective-permute-done | bytes 327712 | tf_op jit(solution)/shard_map/ppermute | solution.py:725
  37.3 1.0 collective-permute-start.7
  38.7 14.5 %collective-permute-done.7 = bf16[8,320,128]{2,1,0:T(8,128)(2,1)S(1)} collective-permute-done((bf16[8,320,128]{2,1,0:T(8,128)(2,1)S(1)}, bf16[8,320,128]{2,1,0:T(8,128)(2,1)S(1)}, u32[]{:S(2)}, u32[]{:S(2)}) %collective-permute-start.7) | collective-permute-done | bytes 655392 | tf_op jit(solution)/shard_map/ppermute | solution.py:725
  54.0 0.8 copy.113.refs_16_.refs_7_.refs_24_
  56.4 0.9 broadcast_add_fusion.refs_11_.refs_4_.refs_19_
  57.3 1.2 collective-permute-done.5.refs_2_
  58.4 51.2 %front.1 = (f32[80,300]{1,0:T(8,128)}, f32[80,300]{1,0:T(8,128)}, bf16[1280,300]{1,0:T(8,128)(2,1)}, bf16[1280,300]{1,0:T(8,128)(2,1)}, bf16[1024,300]{1,0:T(8,1...) custom-call(s32[2,32]{1,0:T(2,128)} %pad_add_fusion.1.refs_0_.refs_2, ...), custom_call_target="tpu_custom_call" | custom-call | flops 60000002048 | bytes 60000000 | tf_op jit(solution)/shard_map/front/pallas_call | solution.py:677
  109.8 9.0 %last_inputs.1 = (f32[80,300]{1,0:T(8,128)}, bf16[1280,300]{1,0:T(8,128)(2,1)}, bf16[1280,300]{1,0:T(8,128)(2,1)}) custom-call(bf16[300,300]{1,0:T(8,128)(2,1)} %get-tuple-element.122.refs_0_, bf16[300,684]{1,0:T(8,128)(2,1)} %get-tuple-element.123.refs_1_, bf16[300,300]{1,0:T(8,128)(2,1)} %get-tuple-element.124.refs_2_, ...), custom_call_target="tpu_custom_call" | custom-call | flops 8999999488 | bytes 9000000 | tf_op jit(solution)/shard_map/last_inputs/pallas_call | solution.py:677
  119.0 0.9 collective-permute-start.13
  119.8 2.1 %collective-permute-start.12 = (bf16[8,160,128]{2,1,0:T(8,128)(2,1)S(1)}, bf16[8,160,128]{2,1,0:T(8,128)(2,1)S(1)}, u32[]{:S(2)}, u32[]{:S(2)}) collective-permute-start(bf16[8,160,128]{2,1,0:T(8,128)(2,1)S(1)} %get-tuple-element.261), channel_id=1, source_target_pairs={{0,2},{1,3},{2,0},{3,1},{4,6},{5,7},{6,4},{7,5},{8,10},{9,11},{10,... | collective-permute-start | bytes 983048 | tf_op jit(solution)/shard_map/ppermute | solution.py:725
  121.9 12.2 %first_ffn.1 = (bf16[1360,300]{1,0:T(8,128)(2,1)}, f32[4,8,300]{2,1,0:T(8,128)}, bf16[1360,384]{1,0:T(8,128)(2,1)}, bf16[1360,1200]{1,0:T(8,128)(2,1)}) custom-call(bf16[1200,300]{1,0:T(8,128)(2,1)} %get-tuple-element.121.refs_0_, bf16[1280,300]{1,0:T(8,128)(2,1)} %get-tuple-element.133.refs_1_, bf16[1360,384]{1,0:T(8,128)(2,1)} %get-tuple-element.134.refs_2_, ...), custom_call_target="tpu_custom_call" | custom-call | flops 12999999488 | bytes 13000000 | tf_op jit(solution)/shard_map/first_ffn/pallas_call | solution.py:677
  134.4 1.1 collective-permute-start.14
  135.6 16.1 %first.1 = (bf16[1280,684]{1,0:T(8,128)(2,1)}, bf16[80,300]{1,0:T(8,128)(2,1)}, bf16[80,684]{1,0:T(8,128)(2,1)}, bf16[32,160,128]{2,1,0:T(8,128)(2,1)}, bf16[32,160,128]{2,1,0:T(8,128)(2,1)}) custom-call(bf16[300,300]{1,0:T(8,128)(2,1)} %get-tuple-element.119.refs_0_, bf16[300,684]{1,0:T(8,128)(2,1)} %get-tuple-element.120.refs_1_, ...), custom_call_target="tpu_custom_call" | custom-call | flops 17999998976 | bytes 18000000 | tf_op jit(solution)/shard_map/first/pallas_call | solution.py:677
  152.4 1.5 add_convert_fusion.9
  154.0 1.7 collective-permute-done.16
  156.4 3.6 %collective-permute-start.21 = (bf16[1,320,128]{2,1,0:T(8,128)(2,1)}, bf16[1,320,128]{2,1,0:T(8,128)(2,1)}, u32[]{:S(2)}, u32[]{:S(2)}) collective-permute-start(bf16[1,320,128]{2,1,0:T(8,128)(2,1)} %get-tuple-element.281), channel_id=1, source_target_pairs={{0,24},{4,28},{8,16},{12,20},{16,8},{20,12},{24,0},{28,4},{1,25},{... | collective-permute-start | bytes 245768 | tf_op jit(solution)/shard_map/ppermute | solution.py:725
  160.0 0.7 collective-permute-start.19
  161.0 1.0 collective-permute-start.18
  162.0 1.9 collective-permute-start.17
  163.9 9.9 %first_inputs.1 = (f32[80,300]{1,0:T(8,128)}, f32[1024,300]{1,0:T(8,128)}, f32[1024,300]{1,0:T(8,128)}) custom-call(bf16[300,300]{1,0:T(8,128)(2,1)} %get-tuple-element.170.refs_0_, bf16[300,684]{1,0:T(8,128)(2,1)} %get-tuple-element.120.refs_1_, bf16[300,300]{1,0:T(8,128)(2,1)} %get-tuple-element.171.refs_2_, bf16[300,300]{1,0:T(8,128)(2,1)} %get-tuple-element.172.refs_3_, ...), custom_call_target="tpu_custom_call" | custom-call | flops 8999999488 | bytes 9000000 | tf_op jit(solution)/shard_map/first_inputs/pallas_call | solution.py:677
  173.8 1.0 maximum_select_fusion
  175.2 1.1 collective-permute-start.22
  177.1 4.6 %collective-permute-done.23 = bf16[4,160,128]{2,1,0:T(8,128)(2,1)S(1)} collective-permute-done((bf16[4,160,128]{2,1,0:T(8,128)(2,1)S(1)}, bf16[4,160,128]{2,1,0:T(8,128)(2,1)S(1)}, u32[]{:S(2)}, u32[]{:S(2)}) %collective-permute-start.23) | collective-permute-done | bytes 163872 | tf_op jit(solution)/shard_map/ppermute | solution.py:725
  182.7 3.6 %collective-permute-start.28 = (bf16[1,320,128]{2,1,0:T(8,128)(2,1)}, bf16[1,320,128]{2,1,0:T(8,128)(2,1)}, u32[]{:S(2)}, u32[]{:S(2)}) collective-permute-start(bf16[1,320,128]{2,1,0:T(8,128)(2,1)} %get-tuple-element.279), channel_id=1, source_target_pairs={{0,24},{4,28},{8,16},{12,20},{16,8},{20,12},{24,0},{28,4},{1,25},{... | collective-permute-start | bytes 245768 | tf_op jit(solution)/shard_map/ppermute | solution.py:725
  186.3 2.3 %copy.117 = bf16[1,1024,300]{1,2,0:T(8,128)(2,1)} copy(bf16[1,1024,300]{2,1,0:T(8,128)(2,1)} %bitcast.87) | data formatting | bytes 1228800
  188.6 1.1 copy.118
  189.7 1.7 collective-permute-start.25
  191.4 0.8 collective-permute-start.27
  192.2 2.0 copy.119
  194.2 2.0 copy.120
  196.2 1.0 convert_add_fusion
  197.4 1.1 convert_add_fusion.1
  199.3 2.4 %fusion.25 = (bf16[2,36600]{1,0:T(2,128)(2,1)}, f32[2,36600]{1,0:T(2,128)}, f32[2,36600]{1,0:T(2,128)}, f32[2,36600]{1,0:T(2,128)}, f32[2,36600]{1,0:T(2,128)}) fusion(f32[2,36600]{1,0:T(2,128)S(1)} %copy-done.9, f32[2,36600]{1,0:T(2,128)S(1)} %copy-done.15, f32[2,36600]{1,0:T(2,128)S(1)} %copy-done.16, f32[1,36600]{1,0:T(1,128)S(1)} %stack_reshape.7, ...), kind=kLoop, calls=%fused_computation.122 | loop fusion | flops 1244400 | bytes 2488800 | tf_op jit(solution)/shard_map/convert_element_type | solution.py:1142
  201.7 1.1 add.171
  203.4 0.7 slice_bitcast_fusion
  (150 shorter events, 15.8 us)
Async XLA Ops:
  0.6 8.4 %copy-start.23 = (s32[1,1024]{1,0:T(1,128)S(1)}, s32[1,1024]{1,0:T(1,128)}, u32[]{:S(2)}) copy-start(s32[1,1024]{1,0:T(1,128)} %param.24) | copy-start | bytes 12292
  0.7 8.4 %copy-start.22 = (s32[1,1024]{1,0:T(1,128)S(1)}, s32[1,1024]{1,0:T(1,128)}, u32[]{:S(2)}) copy-start(s32[1,1024]{1,0:T(1,128)} %param.22) | copy-start | bytes 12292
  0.7 8.4 %copy-start.11 = (bf16[1,1024,300]{1,2,0:T(8,128)(2,1)S(1)}, bf16[1,1024,300]{1,2,0:T(8,128)(2,1)}, u32[]{:S(2)}) copy-start(bf16[1,1024,300]{1,2,0:T(8,128)(2,1)} %param.21) | copy-start | bytes 1843204
  3.1 6.4 %copy-start.12 = (bf16[1,1024,300]{1,2,0:T(8,128)(2,1)S(1)}, bf16[1,1024,300]{1,2,0:T(8,128)(2,1)}, u32[]{:S(2)}) copy-start(bf16[1,1024,300]{1,2,0:T(8,128)(2,1)} %param.18) | copy-start | bytes 1843204
  3.3 21.4 %collective-permute-start.2 = (bf16[1,640,128]{2,1,0:T(8,128)(2,1)S(1)}, bf16[1,640,128]{2,1,0:T(8,128)(2,1)S(1)}, u32[]{:S(2)}, u32[]{:S(2)}) collective-permute-start(bf16[1,640,128]{2,1,0:T(8,128)(2,1)S(1)} %maximum_bitcast_fusion), channel_id=1, source_target_pairs={{0,24},{4,28},{8,16},{12,20},{16,8},{20,12},{24,0},{28,4},{1,25},{... | collective-permute-start | bytes 491528 | tf_op jit(solution)/shard_map/ppermute | solution.py:725
  8.4 16.3 %collective-permute-start.1 = (bf16[1,640,128]{2,1,0:T(8,128)(2,1)S(1)}, bf16[1,640,128]{2,1,0:T(8,128)(2,1)S(1)}, u32[]{:S(2)}, u32[]{:S(2)}) collective-permute-start(bf16[1,640,128]{2,1,0:T(8,128)(2,1)S(1)} %maximum_bitcast_fusion), channel_id=1, source_target_pairs={{0,16},{4,20},{8,24},{12,28},{16,0},{20,4},{24,8},{28,12},{1,17},{... | collective-permute-start | bytes 491528 | tf_op jit(solution)/shard_map/ppermute | solution.py:725
  8.4 16.3 %collective-permute-start = (bf16[1,640,128]{2,1,0:T(8,128)(2,1)S(1)}, bf16[1,640,128]{2,1,0:T(8,128)(2,1)}, u32[]{:S(2)}, u32[]{:S(2)}) collective-permute-start(bf16[1,640,128]{2,1,0:T(8,128)(2,1)S(1)} %maximum_bitcast_fusion), channel_id=1, source_target_pairs={{0,8},{4,12},{8,0},{12,4},{16,24},{20,28},{24,16},{28,20},{1,9},{5... | collective-permute-start | bytes 491528 | tf_op jit(solution)/shard_map/ppermute | solution.py:725
  9.5 7.4 %copy-start.8 = (bf16[1,1024,300]{2,1,0:T(8,128)(2,1)}, bf16[1,1024,300]{2,1,0:T(8,128)(2,1)S(1)}, u32[]{:S(2)}) copy-start(bf16[1,1024,300]{2,1,0:T(8,128)(2,1)S(1)} %copy.99) | copy-start | bytes 1843204
  12.4 5.2 %copy-start.24 = (pred[300]{0:T(512)(128)(4,1)S(1)}, pred[300]{0:T(512)(128)(4,1)}, u32[]{:S(2)}) copy-start(pred[300]{0:T(512)(128)(4,1)} %constant.19.clone.1) | copy-start | bytes 904
  12.4 11.0 %copy-start.25 = (s32[32]{0:T(128)S(1)}, s32[32]{0:T(128)}, u32[]{:S(2)}) copy-start(s32[32]{0:T(128)} %param.25) | copy-start | bytes 388
  12.4 11.0 %copy-start.26 = (s32[1,80]{1,0:T(1,128)S(1)}, s32[1,80]{1,0:T(1,128)}, u32[]{:S(2)}) copy-start(s32[1,80]{1,0:T(1,128)} %param.23) | copy-start | bytes 964
  13.9 11.9 %copy-start.7 = (bf16[1,1024,300]{2,1,0:T(8,128)(2,1)}, bf16[1,1024,300]{2,1,0:T(8,128)(2,1)S(1)}, u32[]{:S(2)}) copy-start(bf16[1,1024,300]{2,1,0:T(8,128)(2,1)S(1)} %copy.102) | copy-start | bytes 1843204
  18.1 10.9 %collective-permute-start.10 = (bf16[528,300]{1,0:T(8,128)(2,1)S(1)}, bf16[528,300]{1,0:T(8,128)(2,1)}, u32[]{:S(2)}, u32[]{:S(2)}) collective-permute-start(bf16[528,300]{1,0:T(8,128)(2,1)S(1)} %get-tuple-element.296), channel_id=1, source_target_pairs={{1,0},{2,1},{3,2},{5,4},{6,5},{7,6},{9,8},{10,9},{11,10},{13,12},{... | collective-permute-start | bytes 950408 | tf_op jit(solution)/shard_map/ppermute | solution.py:804
  19.4 10.3 %collective-permute-start.9 = (bf16[528,300]{1,0:T(8,128)(2,1)}, bf16[528,300]{1,0:T(8,128)(2,1)}, u32[]{:S(2)}, u32[]{:S(2)}) collective-permute-start(bf16[528,300]{1,0:T(8,128)(2,1)} %get-tuple-element.297), channel_id=1, source_target_pairs={{0,1},{1,2},{2,3},{4,5},{5,6},{6,7},{8,9},{9,10},{10,11},{12,13},{... | collective-permute-start | bytes 950408 | tf_op jit(solution)/shard_map/ppermute | solution.py:803
  25.8 10.2 %collective-permute-start.3 = (bf16[4,320,128]{2,1,0:T(8,128)(2,1)S(1)}, bf16[4,320,128]{2,1,0:T(8,128)(2,1)S(1)}, u32[]{:S(2)}, u32[]{:S(2)}) collective-permute-start(bf16[4,320,128]{2,1,0:T(8,128)(2,1)S(1)} %get-tuple-element.111), channel_id=1, source_target_pairs={{0,4},{4,0},{8,12},{12,8},{16,20},{20,16},{24,28},{28,24},{1,5},{5... | collective-permute-start | bytes 983048 | tf_op jit(solution)/shard_map/ppermute | solution.py:725
  27.5 9.7 %collective-permute-start.6 = (bf16[4,320,128]{2,1,0:T(8,128)(2,1)S(1)}, bf16[4,320,128]{2,1,0:T(8,128)(2,1)S(1)}, u32[]{:S(2)}, u32[]{:S(2)}) collective-permute-start(bf16[4,320,128]{2,1,0:T(8,128)(2,1)S(1)} %get-tuple-element.112), channel_id=1, source_target_pairs={{0,2},{1,3},{2,0},{3,1},{4,6},{5,7},{6,4},{7,5},{8,10},{9,11},{10,... | collective-permute-start | bytes 983048 | tf_op jit(solution)/shard_map/ppermute | solution.py:725
  36.0 17.4 %collective-permute-start.4 = (bf16[8,320,128]{2,1,0:T(8,128)(2,1)S(1)}, bf16[8,320,128]{2,1,0:T(8,128)(2,1)S(1)}, u32[]{:S(2)}, u32[]{:S(2)}) collective-permute-start(bf16[8,320,128]{2,1,0:T(8,128)(2,1)S(1)} %pad_maximum_fusion.1), channel_id=1, source_target_pairs={{0,2},{1,3},{2,0},{3,1},{4,6},{5,7},{6,4},{7,5},{8,10},{9,11},{10,... | collective-permute-start | bytes 1966088 | tf_op jit(solution)/shard_map/ppermute | solution.py:725
  37.3 15.9 %collective-permute-start.7 = (bf16[8,320,128]{2,1,0:T(8,128)(2,1)S(1)}, bf16[8,320,128]{2,1,0:T(8,128)(2,1)S(1)}, u32[]{:S(2)}, u32[]{:S(2)}) collective-permute-start(bf16[8,320,128]{2,1,0:T(8,128)(2,1)S(1)} %pad_maximum_fusion.2), channel_id=1, source_target_pairs={{0,4},{4,0},{8,12},{12,8},{16,20},{20,16},{24,28},{28,24},{1,5},{5... | collective-permute-start | bytes 1966088 | tf_op jit(solution)/shard_map/ppermute | solution.py:725
  38.2 15.0 %copy-start.21 = (s32[1,1280]{1,0:T(1,128)}, s32[1,1280]{1,0:T(1,128)S(1)}, u32[]{:S(2)}) copy-start(s32[1,1280]{1,0:T(1,128)S(1)} %add_add_fusion.refs_12_.refs_5_.refs_20_) | copy-start | bytes 15364
  53.3 4.0 %collective-permute-start.8 = (bf16[16,320,128]{2,1,0:T(8,128)(2,1)S(1)}, bf16[16,320,128]{2,1,0:T(8,128)(2,1)}, u32[]{:S(2)}, u32[]{:S(2)}) collective-permute-start(bf16[16,320,128]{2,1,0:T(8,128)(2,1)S(1)} %constant_dynamic-update-slice_fusion.3.refs_3_), channel_id=1, source_target_pairs={{0,1},{1,0},{2,3},{3,2},{4,5},{5,4},{6,7},{7,6},{8,9},{9,8},{10,11... | collective-permute-start | bytes 3932168 | tf_op jit(solution)/shard_map/ppermute | solution.py:725
  53.5 4.9 %copy-start.20 = (bf16[16,320,128]{2,1,0:T(8,128)(2,1)}, bf16[16,320,128]{2,1,0:T(8,128)(2,1)S(1)}, u32[]{:S(2)}) copy-start(bf16[16,320,128]{2,1,0:T(8,128)(2,1)S(1)} %constant_dynamic-update-slice_fusion.refs_1_) | copy-start | bytes 3932164
  53.5 4.9 %collective-permute-start.5 = (bf16[16,320,128]{2,1,0:T(8,128)(2,1)S(1)}, bf16[16,320,128]{2,1,0:T(8,128)(2,1)}, u32[]{:S(2)}, u32[]{:S(2)}) collective-permute-start(bf16[16,320,128]{2,1,0:T(8,128)(2,1)S(1)} %constant_dynamic-update-slice_fusion.refs_1_), channel_id=1, source_target_pairs={{0,1},{1,0},{2,3},{3,2},{4,5},{5,4},{6,7},{7,6},{8,9},{9,8},{10,11... | collective-permute-start | bytes 3932168 | tf_op jit(solution)/shard_map/ppermute | solution.py:725
  109.6 9.2 %collective-permute-start.11 = (bf16[32,160,128]{2,1,0:T(8,128)(2,1)}, bf16[32,160,128]{2,1,0:T(8,128)(2,1)S(1)}, u32[]{:S(2)}, u32[]{:S(2)}) collective-permute-start(bf16[32,160,128]{2,1,0:T(8,128)(2,1)} %get-tuple-element.139), channel_id=1, source_target_pairs={{0,1},{1,0},{2,3},{3,2},{4,5},{5,4},{6,7},{7,6},{8,9},{9,8},{10,11... | collective-permute-start | bytes 3932168 | tf_op jit(solution)/shard_map/ppermute | solution.py:725
  109.8 9.0 %copy-start.3 = (bf16[32,160,128]{2,1,0:T(8,128)(2,1)S(1)}, bf16[32,160,128]{2,1,0:T(8,128)(2,1)}, u32[]{:S(2)}) copy-start(bf16[32,160,128]{2,1,0:T(8,128)(2,1)} %get-tuple-element.143) | copy-start | bytes 3932164
  118.8 15.4 %copy-start.4 = (bf16[32,160,128]{2,1,0:T(8,128)(2,1)}, bf16[32,160,128]{2,1,0:T(8,128)(2,1)S(1)}, u32[]{:S(2)}) copy-start(bf16[32,160,128]{2,1,0:T(8,128)(2,1)S(1)} %collective-permute-done.11) | copy-start | bytes 3932164
  119.0 15.2 %collective-permute-start.13 = (bf16[8,160,128]{2,1,0:T(8,128)(2,1)S(1)}, bf16[8,160,128]{2,1,0:T(8,128)(2,1)S(1)}, u32[]{:S(2)}, u32[]{:S(2)}) collective-permute-start(bf16[8,160,128]{2,1,0:T(8,128)(2,1)S(1)} %get-tuple-element.260), channel_id=1, source_target_pairs={{0,4},{4,0},{8,12},{12,8},{16,20},{20,16},{24,28},{28,24},{1,5},{5... | collective-permute-start | bytes 983048 | tf_op jit(solution)/shard_map/ppermute | solution.py:725
  119.8 14.3 %collective-permute-start.12 = (bf16[8,160,128]{2,1,0:T(8,128)(2,1)S(1)}, bf16[8,160,128]{2,1,0:T(8,128)(2,1)S(1)}, u32[]{:S(2)}, u32[]{:S(2)}) collective-permute-start(bf16[8,160,128]{2,1,0:T(8,128)(2,1)S(1)} %get-tuple-element.261), channel_id=1, source_target_pairs={{0,2},{1,3},{2,0},{3,1},{4,6},{5,7},{6,4},{7,5},{8,10},{9,11},{10,... | collective-permute-start | bytes 983048 | tf_op jit(solution)/shard_map/ppermute | solution.py:725
  134.2 17.6 %copy-start.13 = (bf16[8,160,128]{2,1,0:T(8,128)(2,1)}, bf16[8,160,128]{2,1,0:T(8,128)(2,1)S(1)}, u32[]{:S(2)}) copy-start(bf16[8,160,128]{2,1,0:T(8,128)(2,1)S(1)} %collective-permute-done.13) | copy-start | bytes 983044
  134.2 17.6 %copy-start.14 = (bf16[8,160,128]{2,1,0:T(8,128)(2,1)}, bf16[8,160,128]{2,1,0:T(8,128)(2,1)S(1)}, u32[]{:S(2)}) copy-start(bf16[8,160,128]{2,1,0:T(8,128)(2,1)S(1)} %collective-permute-done.12) | copy-start | bytes 983044
  134.3 17.4 %collective-permute-start.15 = (bf16[4,160,128]{2,1,0:T(8,128)(2,1)S(1)}, bf16[4,160,128]{2,1,0:T(8,128)(2,1)S(1)}, u32[]{:S(2)}, u32[]{:S(2)}) collective-permute-start(bf16[4,160,128]{2,1,0:T(8,128)(2,1)S(1)} %get-tuple-element.258), channel_id=1, source_target_pairs={{0,2},{1,3},{2,0},{3,1},{4,6},{5,7},{6,4},{7,5},{8,10},{9,11},{10,... | collective-permute-start | bytes 491528 | tf_op jit(solution)/shard_map/ppermute | solution.py:725
  134.4 17.3 %collective-permute-start.14 = (bf16[4,160,128]{2,1,0:T(8,128)(2,1)S(1)}, bf16[4,160,128]{2,1,0:T(8,128)(2,1)S(1)}, u32[]{:S(2)}, u32[]{:S(2)}) collective-permute-start(bf16[4,160,128]{2,1,0:T(8,128)(2,1)S(1)} %get-tuple-element.259), channel_id=1, source_target_pairs={{0,4},{4,0},{8,12},{12,8},{16,20},{20,16},{24,28},{28,24},{1,5},{5... | collective-permute-start | bytes 491528 | tf_op jit(solution)/shard_map/ppermute | solution.py:725
  152.4 8.3 %copy-start.2 = (bf16[32,160,128]{2,1,0:T(8,128)(2,1)S(1)}, bf16[32,160,128]{2,1,0:T(8,128)(2,1)}, u32[]{:S(2)}) copy-start(bf16[32,160,128]{2,1,0:T(8,128)(2,1)} %get-tuple-element.160) | copy-start | bytes 3932164
  152.4 3.2 %collective-permute-start.16 = (bf16[32,160,128]{2,1,0:T(8,128)(2,1)}, bf16[32,160,128]{2,1,0:T(8,128)(2,1)S(1)}, u32[]{:S(2)}, u32[]{:S(2)}) collective-permute-start(bf16[32,160,128]{2,1,0:T(8,128)(2,1)} %get-tuple-element.166), channel_id=1, source_target_pairs={{0,1},{1,0},{2,3},{3,2},{4,5},{5,4},{6,7},{7,6},{8,9},{9,8},{10,11... | collective-permute-start | bytes 3932168 | tf_op jit(solution)/shard_map/ppermute | solution.py:725
  156.4 17.4 %collective-permute-start.21 = (bf16[1,320,128]{2,1,0:T(8,128)(2,1)}, bf16[1,320,128]{2,1,0:T(8,128)(2,1)}, u32[]{:S(2)}, u32[]{:S(2)}) collective-permute-start(bf16[1,320,128]{2,1,0:T(8,128)(2,1)} %get-tuple-element.281), channel_id=1, source_target_pairs={{0,24},{4,28},{8,16},{12,20},{16,8},{20,12},{24,0},{28,4},{1,25},{... | collective-permute-start | bytes 245768 | tf_op jit(solution)/shard_map/ppermute | solution.py:725
  160.0 13.8 %collective-permute-start.20 = (bf16[1,320,128]{2,1,0:T(8,128)(2,1)}, bf16[1,320,128]{2,1,0:T(8,128)(2,1)}, u32[]{:S(2)}, u32[]{:S(2)}) collective-permute-start(bf16[1,320,128]{2,1,0:T(8,128)(2,1)} %get-tuple-element.282), channel_id=1, source_target_pairs={{0,16},{4,20},{8,24},{12,28},{16,0},{20,4},{24,8},{28,12},{1,17},{... | collective-permute-start | bytes 245768 | tf_op jit(solution)/shard_map/ppermute | solution.py:725
  160.0 13.8 %collective-permute-start.19 = (bf16[1,320,128]{2,1,0:T(8,128)(2,1)}, bf16[1,320,128]{2,1,0:T(8,128)(2,1)}, u32[]{:S(2)}, u32[]{:S(2)}) collective-permute-start(bf16[1,320,128]{2,1,0:T(8,128)(2,1)} %get-tuple-element.283), channel_id=1, source_target_pairs={{0,8},{4,12},{8,0},{12,4},{16,24},{20,28},{24,16},{28,20},{1,9},{5... | collective-permute-start | bytes 245768 | tf_op jit(solution)/shard_map/ppermute | solution.py:725
  161.0 12.9 %collective-permute-start.18 = (bf16[8,160,128]{2,1,0:T(8,128)(2,1)S(1)}, bf16[8,160,128]{2,1,0:T(8,128)(2,1)S(1)}, u32[]{:S(2)}, u32[]{:S(2)}) collective-permute-start(bf16[8,160,128]{2,1,0:T(8,128)(2,1)S(1)} %get-tuple-element.254), channel_id=1, source_target_pairs={{0,4},{4,0},{8,12},{12,8},{16,20},{20,16},{24,28},{28,24},{1,5},{5... | collective-permute-start | bytes 983048 | tf_op jit(solution)/shard_map/ppermute | solution.py:725
  162.0 11.9 %collective-permute-start.17 = (bf16[8,160,128]{2,1,0:T(8,128)(2,1)S(1)}, bf16[8,160,128]{2,1,0:T(8,128)(2,1)S(1)}, u32[]{:S(2)}, u32[]{:S(2)}) collective-permute-start(bf16[8,160,128]{2,1,0:T(8,128)(2,1)S(1)} %get-tuple-element.255), channel_id=1, source_target_pairs={{0,2},{1,3},{2,0},{3,1},{4,6},{5,7},{6,4},{7,5},{8,10},{9,11},{10,... | collective-permute-start | bytes 983048 | tf_op jit(solution)/shard_map/ppermute | solution.py:725
  163.9 9.9 %copy-start.18 = (f32[80,300]{1,0:T(8,128)S(1)}, f32[80,300]{1,0:T(8,128)}, u32[]{:S(2)}) copy-start(f32[80,300]{1,0:T(8,128)} %get-tuple-element.185) | copy-start | bytes 288004
  174.9 1.5 collective-permute-start.24
  175.1 6.7 %collective-permute-start.23 = (bf16[4,160,128]{2,1,0:T(8,128)(2,1)S(1)}, bf16[4,160,128]{2,1,0:T(8,128)(2,1)S(1)}, u32[]{:S(2)}, u32[]{:S(2)}) collective-permute-start(bf16[4,160,128]{2,1,0:T(8,128)(2,1)S(1)} %get-tuple-element.252), channel_id=1, source_target_pairs={{0,2},{1,3},{2,0},{3,1},{4,6},{5,7},{6,4},{7,5},{8,10},{9,11},{10,... | collective-permute-start | bytes 491528 | tf_op jit(solution)/shard_map/ppermute | solution.py:725
  175.2 6.6 %collective-permute-start.22 = (bf16[4,160,128]{2,1,0:T(8,128)(2,1)S(1)}, bf16[4,160,128]{2,1,0:T(8,128)(2,1)S(1)}, u32[]{:S(2)}, u32[]{:S(2)}) collective-permute-start(bf16[4,160,128]{2,1,0:T(8,128)(2,1)S(1)} %get-tuple-element.253), channel_id=1, source_target_pairs={{0,4},{4,0},{8,12},{12,8},{16,20},{20,16},{24,28},{28,24},{1,5},{5... | collective-permute-start | bytes 491528 | tf_op jit(solution)/shard_map/ppermute | solution.py:725
  182.0 6.6 %copy-start.10 = (bf16[1024,300]{1,0:T(8,128)(2,1)S(1)}, bf16[1024,300]{1,0:T(8,128)(2,1)}, u32[]{:S(2)}) copy-start(bf16[1024,300]{1,0:T(8,128)(2,1)} %get-tuple-element.189) | copy-start | bytes 1843204
  182.7 13.5 %collective-permute-start.28 = (bf16[1,320,128]{2,1,0:T(8,128)(2,1)}, bf16[1,320,128]{2,1,0:T(8,128)(2,1)}, u32[]{:S(2)}, u32[]{:S(2)}) collective-permute-start(bf16[1,320,128]{2,1,0:T(8,128)(2,1)} %get-tuple-element.279), channel_id=1, source_target_pairs={{0,24},{4,28},{8,16},{12,20},{16,8},{20,12},{24,0},{28,4},{1,25},{... | collective-permute-start | bytes 245768 | tf_op jit(solution)/shard_map/ppermute | solution.py:725
  186.3 5.9 %copy-start.1 = (f32[1024,300]{1,0:T(8,128)S(1)}, f32[1024,300]{1,0:T(8,128)}, u32[]{:S(2)}) copy-start(f32[1024,300]{1,0:T(8,128)} %get-tuple-element.190) | copy-start | bytes 3686404
  189.7 12.0 %collective-permute-start.25 = (f32[80,600]{1,0:T(8,128)}, f32[80,600]{1,0:T(8,128)}, u32[]{:S(2)}, u32[]{:S(2)}) collective-permute-start(f32[80,600]{1,0:T(8,128)} %add.170), channel_id=1, source_target_pairs={{0,2},{1,3},{2,0},{3,1},{4,6},{5,7},{6,4},{7,5},{8,10},{9,11},{10,... | collective-permute-start | bytes 576008 | tf_op jit(solution)/shard_map/ppermute | solution.py:725
  191.4 6.0 %collective-permute-start.26 = (bf16[1,320,128]{2,1,0:T(8,128)(2,1)}, bf16[1,320,128]{2,1,0:T(8,128)(2,1)}, u32[]{:S(2)}, u32[]{:S(2)}) collective-permute-start(bf16[1,320,128]{2,1,0:T(8,128)(2,1)} %get-tuple-element.278), channel_id=1, source_target_pairs={{0,8},{4,12},{8,0},{12,4},{16,24},{20,28},{24,16},{28,20},{1,9},{5... | collective-permute-start | bytes 245768 | tf_op jit(solution)/shard_map/ppermute | solution.py:725
  191.4 6.0 %collective-permute-start.27 = (bf16[1,320,128]{2,1,0:T(8,128)(2,1)S(1)}, bf16[1,320,128]{2,1,0:T(8,128)(2,1)}, u32[]{:S(2)}, u32[]{:S(2)}) collective-permute-start(bf16[1,320,128]{2,1,0:T(8,128)(2,1)S(1)} %get-tuple-element.280), channel_id=1, source_target_pairs={{0,16},{4,20},{8,24},{12,28},{16,0},{20,4},{24,8},{28,12},{1,17},{... | collective-permute-start | bytes 245768 | tf_op jit(solution)/shard_map/ppermute | solution.py:725
  (8 other events, 18.8 us)

commit v2 on v1

--- a/solution.py
+++ b/solution.py
@@ -552,7 +552,10 @@
         self.pending[:] = [x for x in self.pending if x[0] not in names]
 
 
-def call(body, inputs, outputs, scratch, micros, leaf_rows=TILE, lazy=(), joins=(), own=(), in_smem=(), name=None, loose=(), early=None):
+LATER = ("gyl", "ge", "hb", "dpre", "act", "dbr")
+
+
+def call(body, inputs, outputs, scratch, micros, leaf_rows=TILE, lazy=(), joins=(), own=(), in_smem=(), name=None, loose=(), early=None, soon=None):
     joins = dict(joins)
     tiles = leaf_rows // TILE
     raw = {k for k, _ in joins.values()} | ({"halo_l", "halo_r"} if joins else set())
@@ -634,10 +637,15 @@
                     return every() + behind()
 
                 r.coming[k] = {"tile": wait_for, "rest": behind, "every": every, "all": whole}
-        for t in [tiles] + list(range(tiles)):
-            for i, k in enumerate(buffers):
-                if k in lazy_out or not isinstance(r.coming.get(k), dict):
-                    continue
+        order = [
+            (t, i, k)
+            for later in (False, True)
+            for t in [tiles] + list(range(tiles))
+            for i, k in enumerate(buffers)
+            if (k in LATER and k != soon) == later
+        ]
+        for t, i, k in order:
+            if k not in lazy_out and isinstance(r.coming.get(k), dict):
                 inner, total = held[k], buffers[k][0][0]
                 low, high = t * TILE, min((t + 1) * TILE, leaf_rows)
                 if t == tiles:
@@ -848,9 +856,6 @@
         return [gather_step(h, o[n], sizes) for h, o in zip(held, orders, strict=True)]
 
     rows = [to_rows(x, block_rows) if in_rows else x for x in weights_low]
-    rows, leaves, edge_feats, leaf_cot, edge_cot, graph_ids, leaf_mask = lax.optimization_barrier(
-        (rows, leaves, edge_feats, leaf_cot, edge_cot, graph_ids, leaf_mask)
-    )
     held = gather_begin(rows)
     raw = dict(leaves=leaves[0], edges=edge_feats[0], lcot=leaf_cot[0], ecot=edge_cot[0])
     marks = jnp.pad((graph_ids + 1).astype(BF), ((0, 15), (0, 0)))
@@ -1014,6 +1019,7 @@
             joins=joins,
             own=("gxl", "gel") if out_rows == own_rows else (),
             name=name,
+            soon="ge",
         )
 
     def begin(made):
@@ -1064,6 +1070,7 @@
         leaf_rows,
         lazy=lazy,
         name="first_ffn",
+        soon="gyl",
     )
     held_two, (dn,) = tie(held_two, mid.dn)
     if n_steps > 2:

time: 208 us -> 205 us (0.986)
    optimization_barrier x4 -> x0, local copies, waits for them, and re-layouts: 4.68 us -> none  [local(): lax.optimization_barrier((rows, leaves, edge_feats, leaf_cot, edge_cot, g...]
    unnamed x66 -> x75, local copies, waits for them, and re-layouts: 12 us -> 15.8 us
  transfers between devices with their start and end apart: 29 -> 29, of which waited for: 8 -> 7; matrix products, arithmetic and copies ran while one was open for 16% -> 15% of each run, Pallas kernels for 23% -> 23%
where the time goes in v2:
time: 205 us; the launch traced here: 202 us
  Pallas kernels  96.6 us (47%)
  starting transfers between devices  35.5 us (17%)
  waiting for transfers between devices  28.2 us (14%)
  local copies, waits for them, and re-layouts  21.9 us (11%)
  other arithmetic  17.8 us (9%)
    pallas_call x5, Pallas kernels, call(): pl.pallas_call(kernel, out_shape=[jax.ShapeDtypeStruct(s, d) for s, d in...  96.6 us
    ppermute x27, starting transfers between devices, exchange(): lax.ppermute(x, axis, [(i, i ^ value << shift) for i in range(sizes[axis])])  30.2 us
    ppermute x27, waiting for transfers between devices, exchange(): lax.ppermute(x, axis, [(i, i ^ value << shift) for i in range(sizes[axis])])  28.2 us
    unnamed x75, local copies, waits for them, and re-layouts  15.8 us
  transfers between devices with their start and end apart: 29, of which 7 were waited for; matrix products, arithmetic and copies ran while one was open for 15% of the time, Pallas kernels for 23%

profile of v2, /device:TPU:0, one launch (start us, length us, event | category | flops | bytes accessed | tf_op | source)
XLA Modules:
  0.0 201.9 jit_solution(1479347372716855948)
XLA Ops:
  0.7 1.1 convert_element_type.232
  1.8 0.8 slice_reduce_fusion
  3.4 5.1 %collective-permute-start.2 = (bf16[1,640,128]{2,1,0:T(8,128)(2,1)S(1)}, bf16[1,640,128]{2,1,0:T(8,128)(2,1)S(1)}, u32[]{:S(2)}, u32[]{:S(2)}) collective-permute-start(bf16[1,640,128]{2,1,0:T(8,128)(2,1)S(1)} %bitcast.87), channel_id=1, source_target_pairs={{0,24},{4,28},{8,16},{12,20},{16,8},{20,12},{24,0},{28,4},{1,25},{... | collective-permute-start | bytes 491528 | tf_op jit(solution)/shard_map/ppermute | solution.py:733
  10.3 1.2 copy.101
  11.5 1.5 copy.99
  13.0 0.7 fusion.8
  14.4 1.6 fusion.6
  17.3 1.3 collective-permute-start.10
  18.5 3.9 %collective-permute-start.9 = (bf16[528,300]{1,0:T(8,128)(2,1)}, bf16[528,300]{1,0:T(8,128)(2,1)}, u32[]{:S(2)}, u32[]{:S(2)}) collective-permute-start(bf16[528,300]{1,0:T(8,128)(2,1)} %get-tuple-element.277), channel_id=1, source_target_pairs={{0,1},{1,2},{2,3},{4,5},{5,6},{6,7},{8,9},{9,10},{10,11},{12,13},{... | collective-permute-start | bytes 950408 | tf_op jit(solution)/shard_map/ppermute | solution.py:811
  22.6 0.7 copy.112.refs_15_.refs_23_
  23.8 1.1 pad_maximum_fusion
  25.0 1.7 collective-permute-start.3
  26.7 1.5 collective-permute-start.6
  29.6 5.5 %collective-permute-done.3 = bf16[4,320,128]{2,1,0:T(8,128)(2,1)S(1)} collective-permute-done((bf16[4,320,128]{2,1,0:T(8,128)(2,1)S(1)}, bf16[4,320,128]{2,1,0:T(8,128)(2,1)S(1)}, u32[]{:S(2)}, u32[]{:S(2)}) %collective-permute-start.3) | collective-permute-done | bytes 327712 | tf_op jit(solution)/shard_map/ppermute | solution.py:733
  36.5 1.0 collective-permute-start.7
  38.5 13.9 %collective-permute-done.7 = bf16[8,320,128]{2,1,0:T(8,128)(2,1)S(1)} collective-permute-done((bf16[8,320,128]{2,1,0:T(8,128)(2,1)S(1)}, bf16[8,320,128]{2,1,0:T(8,128)(2,1)S(1)}, u32[]{:S(2)}, u32[]{:S(2)}) %collective-permute-start.7) | collective-permute-done | bytes 655392 | tf_op jit(solution)/shard_map/ppermute | solution.py:733
  53.2 0.7 copy.113.refs_16_.refs_7_.refs_24_
  54.9 0.9 broadcast_add_fusion.refs_11_.refs_4_.refs_19_
  55.8 1.8 collective-permute-done.5.refs_2_
  57.6 51.2 %front.1 = (f32[80,300]{1,0:T(8,128)}, f32[80,300]{1,0:T(8,128)}, bf16[1280,300]{1,0:T(8,128)(2,1)}, bf16[1280,300]{1,0:T(8,128)(2,1)}, bf16[1024,300]{1,0:T(8,1...) custom-call(s32[2,32]{1,0:T(2,128)} %pad_add_fusion.1.refs_0_.refs_2, ...), custom_call_target="tpu_custom_call" | custom-call | flops 60000002048 | bytes 60000000 | tf_op jit(solution)/shard_map/front/pallas_call | solution.py:685
  109.0 9.0 %last_inputs.1 = (f32[80,300]{1,0:T(8,128)}, bf16[1280,300]{1,0:T(8,128)(2,1)}, bf16[1280,300]{1,0:T(8,128)(2,1)}) custom-call(bf16[300,300]{1,0:T(8,128)(2,1)} %get-tuple-element.106.refs_0_, bf16[300,684]{1,0:T(8,128)(2,1)} %get-tuple-element.107.refs_1_, bf16[300,300]{1,0:T(8,128)(2,1)} %get-tuple-element.108.refs_2_, ...), custom_call_target="tpu_custom_call" | custom-call | flops 8999999488 | bytes 9000000 | tf_op jit(solution)/shard_map/last_inputs/pallas_call | solution.py:685
  118.2 0.8 collective-permute-start.13
  119.0 2.0 collective-permute-start.12
  121.0 12.2 %first_ffn.1 = (bf16[1360,300]{1,0:T(8,128)(2,1)}, f32[4,8,300]{2,1,0:T(8,128)}, bf16[1360,384]{1,0:T(8,128)(2,1)}, bf16[1360,1200]{1,0:T(8,128)(2,1)}) custom-call(bf16[1200,300]{1,0:T(8,128)(2,1)} %get-tuple-element.105.refs_0_, bf16[1280,300]{1,0:T(8,128)(2,1)} %get-tuple-element.117.refs_1_, bf16[1360,384]{1,0:T(8,128)(2,1)} %get-tuple-element.118.refs_2_, ...), custom_call_target="tpu_custom_call" | custom-call | flops 12999999488 | bytes 13000000 | tf_op jit(solution)/shard_map/first_ffn/pallas_call | solution.py:685
  133.5 1.3 collective-permute-start.14
  134.8 14.5 %first.1 = (bf16[1280,684]{1,0:T(8,128)(2,1)}, bf16[80,300]{1,0:T(8,128)(2,1)}, bf16[80,684]{1,0:T(8,128)(2,1)}, bf16[32,160,128]{2,1,0:T(8,128)(2,1)}, bf16[32,160,128]{2,1,0:T(8,128)(2,1)}) custom-call(bf16[300,300]{1,0:T(8,128)(2,1)} %get-tuple-element.103.refs_0_, bf16[300,684]{1,0:T(8,128)(2,1)} %get-tuple-element.104.refs_1_, ...), custom_call_target="tpu_custom_call" | custom-call | flops 17999998976 | bytes 18000000 | tf_op jit(solution)/shard_map/first/pallas_call | solution.py:685
  150.0 1.5 add_convert_fusion.9
  151.6 1.7 collective-permute-done.16
  154.0 3.6 %collective-permute-start.21 = (bf16[1,320,128]{2,1,0:T(8,128)(2,1)}, bf16[1,320,128]{2,1,0:T(8,128)(2,1)}, u32[]{:S(2)}, u32[]{:S(2)}) collective-permute-start(bf16[1,320,128]{2,1,0:T(8,128)(2,1)} %get-tuple-element.265), channel_id=1, source_target_pairs={{0,24},{4,28},{8,16},{12,20},{16,8},{20,12},{24,0},{28,4},{1,25},{... | collective-permute-start | bytes 245768 | tf_op jit(solution)/shard_map/ppermute | solution.py:733
  157.6 0.8 collective-permute-start.19
  158.5 0.8 collective-permute-start.18
  159.4 2.0 collective-permute-start.17
  161.3 9.8 %first_inputs.1 = (f32[80,300]{1,0:T(8,128)}, f32[1024,300]{1,0:T(8,128)}, f32[1024,300]{1,0:T(8,128)}) custom-call(bf16[300,300]{1,0:T(8,128)(2,1)} %get-tuple-element.154.refs_0_, bf16[300,684]{1,0:T(8,128)(2,1)} %get-tuple-element.104.refs_1_, bf16[300,300]{1,0:T(8,128)(2,1)} %get-tuple-element.155.refs_2_, bf16[300,300]{1,0:T(8,128)(2,1)} %get-tuple-element.156.refs_3_, ...), custom_call_target="tpu_custom_call" | custom-call | flops 8999999488 | bytes 9000000 | tf_op jit(solution)/shard_map/first_inputs/pallas_call | solution.py:685
  171.1 1.0 maximum_select_fusion
  172.5 1.3 collective-permute-start.22
  174.5 4.5 %collective-permute-done.23 = bf16[4,160,128]{2,1,0:T(8,128)(2,1)S(1)} collective-permute-done((bf16[4,160,128]{2,1,0:T(8,128)(2,1)S(1)}, bf16[4,160,128]{2,1,0:T(8,128)(2,1)S(1)}, u32[]{:S(2)}, u32[]{:S(2)}) %collective-permute-start.23) | collective-permute-done | bytes 163872 | tf_op jit(solution)/shard_map/ppermute | solution.py:733
  180.0 3.6 %collective-permute-start.28 = (bf16[1,320,128]{2,1,0:T(8,128)(2,1)}, bf16[1,320,128]{2,1,0:T(8,128)(2,1)}, u32[]{:S(2)}, u32[]{:S(2)}) collective-permute-start(bf16[1,320,128]{2,1,0:T(8,128)(2,1)} %get-tuple-element.263), channel_id=1, source_target_pairs={{0,24},{4,28},{8,16},{12,20},{16,8},{20,12},{24,0},{28,4},{1,25},{... | collective-permute-start | bytes 245768 | tf_op jit(solution)/shard_map/ppermute | solution.py:733
  183.6 2.3 %copy.117 = bf16[1,1024,300]{1,2,0:T(8,128)(2,1)} copy(bf16[1,1024,300]{2,1,0:T(8,128)(2,1)} %bitcast.86) | data formatting | bytes 1228800
  185.9 1.1 copy.118
  187.0 1.7 collective-permute-start.25
  188.7 0.8 collective-permute-start.27
  189.5 2.0 %copy.119 = f32[1,1024,300]{1,0,2:T(1,128)} copy(f32[1,1024,300]{2,1,0:T(8,128)S(1)} %bitcast.73) | data formatting | bytes 2457600
  191.5 2.0 %copy.120 = f32[1,1024,300]{1,0,2:T(1,128)} copy(f32[1,1024,300]{2,1,0:T(8,128)S(1)} %bitcast.72) | data formatting | bytes 2457600
  193.5 1.0 convert_add_fusion
  194.7 1.1 convert_add_fusion.1
  196.6 2.4 %fusion.25 = (bf16[2,36600]{1,0:T(2,128)(2,1)}, f32[2,36600]{1,0:T(2,128)}, f32[2,36600]{1,0:T(2,128)}, f32[2,36600]{1,0:T(2,128)}, f32[2,36600]{1,0:T(2,128)}) fusion(f32[2,36600]{1,0:T(2,128)S(1)} %copy-done.9, f32[2,36600]{1,0:T(2,128)S(1)} %copy-done.16, f32[2,36600]{1,0:T(2,128)S(1)} %copy-done.17, f32[1,36600]{1,0:T(1,128)S(1)} %stack_reshape.7, ...), kind=kLoop, calls=%fused_computation.125 | loop fusion | flops 1244400 | bytes 2488800 | tf_op jit(solution)/shard_map/convert_element_type | solution.py:1149
  199.0 1.1 add.171
  200.7 0.7 slice_bitcast_fusion
  (152 shorter events, 16.2 us)
Async XLA Ops:
  0.6 8.5 %copy-start.24 = (s32[1,1024]{1,0:T(1,128)S(1)}, s32[1,1024]{1,0:T(1,128)}, u32[]{:S(2)}) copy-start(s32[1,1024]{1,0:T(1,128)} %param.24) | copy-start | bytes 12292
  0.7 8.5 %copy-start.23 = (s32[1,1024]{1,0:T(1,128)S(1)}, s32[1,1024]{1,0:T(1,128)}, u32[]{:S(2)}) copy-start(s32[1,1024]{1,0:T(1,128)} %param.22) | copy-start | bytes 12292
  0.7 8.5 %copy-start.11 = (bf16[1,1024,300]{1,2,0:T(8,128)(2,1)S(1)}, bf16[1,1024,300]{1,2,0:T(8,128)(2,1)}, u32[]{:S(2)}) copy-start(bf16[1,1024,300]{1,2,0:T(8,128)(2,1)} %param.17) | copy-start | bytes 1843204
  2.8 6.8 %copy-start.12 = (bf16[1,1024,300]{1,2,0:T(8,128)(2,1)S(1)}, bf16[1,1024,300]{1,2,0:T(8,128)(2,1)}, u32[]{:S(2)}) copy-start(bf16[1,1024,300]{1,2,0:T(8,128)(2,1)} %param.18) | copy-start | bytes 1843204
  3.4 20.4 %collective-permute-start.2 = (bf16[1,640,128]{2,1,0:T(8,128)(2,1)S(1)}, bf16[1,640,128]{2,1,0:T(8,128)(2,1)S(1)}, u32[]{:S(2)}, u32[]{:S(2)}) collective-permute-start(bf16[1,640,128]{2,1,0:T(8,128)(2,1)S(1)} %bitcast.87), channel_id=1, source_target_pairs={{0,24},{4,28},{8,16},{12,20},{16,8},{20,12},{24,0},{28,4},{1,25},{... | collective-permute-start | bytes 491528 | tf_op jit(solution)/shard_map/ppermute | solution.py:733
  8.5 15.3 %collective-permute-start.1 = (bf16[1,640,128]{2,1,0:T(8,128)(2,1)S(1)}, bf16[1,640,128]{2,1,0:T(8,128)(2,1)}, u32[]{:S(2)}, u32[]{:S(2)}) collective-permute-start(bf16[1,640,128]{2,1,0:T(8,128)(2,1)S(1)} %bitcast.88), channel_id=1, source_target_pairs={{0,16},{4,20},{8,24},{12,28},{16,0},{20,4},{24,8},{28,12},{1,17},{... | collective-permute-start | bytes 491528 | tf_op jit(solution)/shard_map/ppermute | solution.py:733
  8.5 15.3 %collective-permute-start = (bf16[1,640,128]{2,1,0:T(8,128)(2,1)S(1)}, bf16[1,640,128]{2,1,0:T(8,128)(2,1)}, u32[]{:S(2)}, u32[]{:S(2)}) collective-permute-start(bf16[1,640,128]{2,1,0:T(8,128)(2,1)S(1)} %bitcast.89), channel_id=1, source_target_pairs={{0,8},{4,12},{8,0},{12,4},{16,24},{20,28},{24,16},{28,20},{1,9},{5... | collective-permute-start | bytes 491528 | tf_op jit(solution)/shard_map/ppermute | solution.py:733
  10.3 3.4 %copy-start.7 = (bf16[1,1024,300]{2,1,0:T(8,128)(2,1)}, bf16[1,1024,300]{2,1,0:T(8,128)(2,1)S(1)}, u32[]{:S(2)}) copy-start(bf16[1,1024,300]{2,1,0:T(8,128)(2,1)S(1)} %copy.100) | copy-start | bytes 1843204
  11.5 5.2 %copy-start.25 = (pred[300]{0:T(512)(128)(4,1)S(1)}, pred[300]{0:T(512)(128)(4,1)}, u32[]{:S(2)}) copy-start(pred[300]{0:T(512)(128)(4,1)} %constant.19.clone.1) | copy-start | bytes 904
  11.5 11.0 %copy-start.26 = (s32[32]{0:T(128)S(1)}, s32[32]{0:T(128)}, u32[]{:S(2)}) copy-start(s32[32]{0:T(128)} %param.25) | copy-start | bytes 388
  11.5 11.0 %copy-start.27 = (s32[1,80]{1,0:T(1,128)S(1)}, s32[1,80]{1,0:T(1,128)}, u32[]{:S(2)}) copy-start(s32[1,80]{1,0:T(1,128)} %param.23) | copy-start | bytes 964
  13.0 11.9 %copy-start.8 = (bf16[1,1024,300]{2,1,0:T(8,128)(2,1)}, bf16[1,1024,300]{2,1,0:T(8,128)(2,1)S(1)}, u32[]{:S(2)}) copy-start(bf16[1,1024,300]{2,1,0:T(8,128)(2,1)S(1)} %copy.99) | copy-start | bytes 1843204
  17.3 11.0 %collective-permute-start.10 = (bf16[528,300]{1,0:T(8,128)(2,1)S(1)}, bf16[528,300]{1,0:T(8,128)(2,1)}, u32[]{:S(2)}, u32[]{:S(2)}) collective-permute-start(bf16[528,300]{1,0:T(8,128)(2,1)S(1)} %get-tuple-element.276), channel_id=1, source_target_pairs={{1,0},{2,1},{3,2},{5,4},{6,5},{7,6},{9,8},{10,9},{11,10},{13,12},{... | collective-permute-start | bytes 950408 | tf_op jit(solution)/shard_map/ppermute | solution.py:812
  18.5 10.4 %collective-permute-start.9 = (bf16[528,300]{1,0:T(8,128)(2,1)}, bf16[528,300]{1,0:T(8,128)(2,1)}, u32[]{:S(2)}, u32[]{:S(2)}) collective-permute-start(bf16[528,300]{1,0:T(8,128)(2,1)} %get-tuple-element.277), channel_id=1, source_target_pairs={{0,1},{1,2},{2,3},{4,5},{5,6},{6,7},{8,9},{9,10},{10,11},{12,13},{... | collective-permute-start | bytes 950408 | tf_op jit(solution)/shard_map/ppermute | solution.py:811
  25.0 10.2 %collective-permute-start.3 = (bf16[4,320,128]{2,1,0:T(8,128)(2,1)S(1)}, bf16[4,320,128]{2,1,0:T(8,128)(2,1)S(1)}, u32[]{:S(2)}, u32[]{:S(2)}) collective-permute-start(bf16[4,320,128]{2,1,0:T(8,128)(2,1)S(1)} %get-tuple-element.97), channel_id=1, source_target_pairs={{0,4},{4,0},{8,12},{12,8},{16,20},{20,16},{24,28},{28,24},{1,5},{5... | collective-permute-start | bytes 983048 | tf_op jit(solution)/shard_map/ppermute | solution.py:733
  26.7 9.7 %collective-permute-start.6 = (bf16[4,320,128]{2,1,0:T(8,128)(2,1)S(1)}, bf16[4,320,128]{2,1,0:T(8,128)(2,1)S(1)}, u32[]{:S(2)}, u32[]{:S(2)}) collective-permute-start(bf16[4,320,128]{2,1,0:T(8,128)(2,1)S(1)} %get-tuple-element.98), channel_id=1, source_target_pairs={{0,2},{1,3},{2,0},{3,1},{4,6},{5,7},{6,4},{7,5},{8,10},{9,11},{10,... | collective-permute-start | bytes 983048 | tf_op jit(solution)/shard_map/ppermute | solution.py:733
  35.2 17.4 %collective-permute-start.4 = (bf16[8,320,128]{2,1,0:T(8,128)(2,1)S(1)}, bf16[8,320,128]{2,1,0:T(8,128)(2,1)S(1)}, u32[]{:S(2)}, u32[]{:S(2)}) collective-permute-start(bf16[8,320,128]{2,1,0:T(8,128)(2,1)S(1)} %pad_maximum_fusion.1), channel_id=1, source_target_pairs={{0,2},{1,3},{2,0},{3,1},{4,6},{5,7},{6,4},{7,5},{8,10},{9,11},{10,... | collective-permute-start | bytes 1966088 | tf_op jit(solution)/shard_map/ppermute | solution.py:733
  36.5 15.9 %collective-permute-start.7 = (bf16[8,320,128]{2,1,0:T(8,128)(2,1)S(1)}, bf16[8,320,128]{2,1,0:T(8,128)(2,1)S(1)}, u32[]{:S(2)}, u32[]{:S(2)}) collective-permute-start(bf16[8,320,128]{2,1,0:T(8,128)(2,1)S(1)} %pad_maximum_fusion.2), channel_id=1, source_target_pairs={{0,4},{4,0},{8,12},{12,8},{16,20},{20,16},{24,28},{28,24},{1,5},{5... | collective-permute-start | bytes 1966088 | tf_op jit(solution)/shard_map/ppermute | solution.py:733
  38.0 16.2 %copy-start.22 = (s32[1,1280]{1,0:T(1,128)}, s32[1,1280]{1,0:T(1,128)S(1)}, u32[]{:S(2)}) copy-start(s32[1,1280]{1,0:T(1,128)S(1)} %get-tuple-element.289.refs_12_.refs_5_.refs_20_) | copy-start | bytes 15364
  52.5 3.3 %collective-permute-start.8 = (bf16[16,320,128]{2,1,0:T(8,128)(2,1)S(1)}, bf16[16,320,128]{2,1,0:T(8,128)(2,1)}, u32[]{:S(2)}, u32[]{:S(2)}) collective-permute-start(bf16[16,320,128]{2,1,0:T(8,128)(2,1)S(1)} %constant_dynamic-update-slice_fusion.9.refs_3_), channel_id=1, source_target_pairs={{0,1},{1,0},{2,3},{3,2},{4,5},{5,4},{6,7},{7,6},{8,9},{9,8},{10,11... | collective-permute-start | bytes 3932168 | tf_op jit(solution)/shard_map/ppermute | solution.py:733
  52.7 4.9 %copy-start.21 = (bf16[16,320,128]{2,1,0:T(8,128)(2,1)}, bf16[16,320,128]{2,1,0:T(8,128)(2,1)S(1)}, u32[]{:S(2)}) copy-start(bf16[16,320,128]{2,1,0:T(8,128)(2,1)S(1)} %constant_dynamic-update-slice_fusion.6.refs_1_) | copy-start | bytes 3932164
  52.7 4.9 %collective-permute-start.5 = (bf16[16,320,128]{2,1,0:T(8,128)(2,1)S(1)}, bf16[16,320,128]{2,1,0:T(8,128)(2,1)}, u32[]{:S(2)}, u32[]{:S(2)}) collective-permute-start(bf16[16,320,128]{2,1,0:T(8,128)(2,1)S(1)} %constant_dynamic-update-slice_fusion.6.refs_1_), channel_id=1, source_target_pairs={{0,1},{1,0},{2,3},{3,2},{4,5},{5,4},{6,7},{7,6},{8,9},{9,8},{10,11... | collective-permute-start | bytes 3932168 | tf_op jit(solution)/shard_map/ppermute | solution.py:733
  108.8 9.2 %collective-permute-start.11 = (bf16[32,160,128]{2,1,0:T(8,128)(2,1)}, bf16[32,160,128]{2,1,0:T(8,128)(2,1)S(1)}, u32[]{:S(2)}, u32[]{:S(2)}) collective-permute-start(bf16[32,160,128]{2,1,0:T(8,128)(2,1)} %get-tuple-element.123), channel_id=1, source_target_pairs={{0,1},{1,0},{2,3},{3,2},{4,5},{5,4},{6,7},{7,6},{8,9},{9,8},{10,11... | collective-permute-start | bytes 3932168 | tf_op jit(solution)/shard_map/ppermute | solution.py:733
  109.0 9.0 %copy-start.3 = (bf16[32,160,128]{2,1,0:T(8,128)(2,1)S(1)}, bf16[32,160,128]{2,1,0:T(8,128)(2,1)}, u32[]{:S(2)}) copy-start(bf16[32,160,128]{2,1,0:T(8,128)(2,1)} %get-tuple-element.127) | copy-start | bytes 3932164
  118.0 15.3 %copy-start.4 = (bf16[32,160,128]{2,1,0:T(8,128)(2,1)}, bf16[32,160,128]{2,1,0:T(8,128)(2,1)S(1)}, u32[]{:S(2)}) copy-start(bf16[32,160,128]{2,1,0:T(8,128)(2,1)S(1)} %collective-permute-done.11) | copy-start | bytes 3932164
  118.2 15.0 %collective-permute-start.13 = (bf16[8,160,128]{2,1,0:T(8,128)(2,1)S(1)}, bf16[8,160,128]{2,1,0:T(8,128)(2,1)S(1)}, u32[]{:S(2)}, u32[]{:S(2)}) collective-permute-start(bf16[8,160,128]{2,1,0:T(8,128)(2,1)S(1)} %get-tuple-element.244), channel_id=1, source_target_pairs={{0,4},{4,0},{8,12},{12,8},{16,20},{20,16},{24,28},{28,24},{1,5},{5... | collective-permute-start | bytes 983048 | tf_op jit(solution)/shard_map/ppermute | solution.py:733
  119.0 14.2 %collective-permute-start.12 = (bf16[8,160,128]{2,1,0:T(8,128)(2,1)S(1)}, bf16[8,160,128]{2,1,0:T(8,128)(2,1)S(1)}, u32[]{:S(2)}, u32[]{:S(2)}) collective-permute-start(bf16[8,160,128]{2,1,0:T(8,128)(2,1)S(1)} %get-tuple-element.245), channel_id=1, source_target_pairs={{0,2},{1,3},{2,0},{3,1},{4,6},{5,7},{6,4},{7,5},{8,10},{9,11},{10,... | collective-permute-start | bytes 983048 | tf_op jit(solution)/shard_map/ppermute | solution.py:733
  133.2 16.1 %copy-start.14 = (bf16[8,160,128]{2,1,0:T(8,128)(2,1)}, bf16[8,160,128]{2,1,0:T(8,128)(2,1)S(1)}, u32[]{:S(2)}) copy-start(bf16[8,160,128]{2,1,0:T(8,128)(2,1)S(1)} %collective-permute-done.13) | copy-start | bytes 983044
  133.2 16.1 %copy-start.15 = (bf16[8,160,128]{2,1,0:T(8,128)(2,1)}, bf16[8,160,128]{2,1,0:T(8,128)(2,1)S(1)}, u32[]{:S(2)}) copy-start(bf16[8,160,128]{2,1,0:T(8,128)(2,1)S(1)} %collective-permute-done.12) | copy-start | bytes 983044
  133.4 15.9 %collective-permute-start.15 = (bf16[4,160,128]{2,1,0:T(8,128)(2,1)S(1)}, bf16[4,160,128]{2,1,0:T(8,128)(2,1)S(1)}, u32[]{:S(2)}, u32[]{:S(2)}) collective-permute-start(bf16[4,160,128]{2,1,0:T(8,128)(2,1)S(1)} %get-tuple-element.242), channel_id=1, source_target_pairs={{0,2},{1,3},{2,0},{3,1},{4,6},{5,7},{6,4},{7,5},{8,10},{9,11},{10,... | collective-permute-start | bytes 491528 | tf_op jit(solution)/shard_map/ppermute | solution.py:733
  133.5 15.8 %collective-permute-start.14 = (bf16[4,160,128]{2,1,0:T(8,128)(2,1)S(1)}, bf16[4,160,128]{2,1,0:T(8,128)(2,1)S(1)}, u32[]{:S(2)}, u32[]{:S(2)}) collective-permute-start(bf16[4,160,128]{2,1,0:T(8,128)(2,1)S(1)} %get-tuple-element.243), channel_id=1, source_target_pairs={{0,4},{4,0},{8,12},{12,8},{16,20},{20,16},{24,28},{28,24},{1,5},{5... | collective-permute-start | bytes 491528 | tf_op jit(solution)/shard_map/ppermute | solution.py:733
  150.0 8.3 %copy-start.2 = (bf16[32,160,128]{2,1,0:T(8,128)(2,1)S(1)}, bf16[32,160,128]{2,1,0:T(8,128)(2,1)}, u32[]{:S(2)}) copy-start(bf16[32,160,128]{2,1,0:T(8,128)(2,1)} %get-tuple-element.144) | copy-start | bytes 3932164
  150.0 3.2 %collective-permute-start.16 = (bf16[32,160,128]{2,1,0:T(8,128)(2,1)}, bf16[32,160,128]{2,1,0:T(8,128)(2,1)S(1)}, u32[]{:S(2)}, u32[]{:S(2)}) collective-permute-start(bf16[32,160,128]{2,1,0:T(8,128)(2,1)} %get-tuple-element.150), channel_id=1, source_target_pairs={{0,1},{1,0},{2,3},{3,2},{4,5},{5,4},{6,7},{7,6},{8,9},{9,8},{10,11... | collective-permute-start | bytes 3932168 | tf_op jit(solution)/shard_map/ppermute | solution.py:733
  154.0 17.1 %collective-permute-start.21 = (bf16[1,320,128]{2,1,0:T(8,128)(2,1)}, bf16[1,320,128]{2,1,0:T(8,128)(2,1)}, u32[]{:S(2)}, u32[]{:S(2)}) collective-permute-start(bf16[1,320,128]{2,1,0:T(8,128)(2,1)} %get-tuple-element.265), channel_id=1, source_target_pairs={{0,24},{4,28},{8,16},{12,20},{16,8},{20,12},{24,0},{28,4},{1,25},{... | collective-permute-start | bytes 245768 | tf_op jit(solution)/shard_map/ppermute | solution.py:733
  157.6 13.5 %collective-permute-start.20 = (bf16[1,320,128]{2,1,0:T(8,128)(2,1)}, bf16[1,320,128]{2,1,0:T(8,128)(2,1)}, u32[]{:S(2)}, u32[]{:S(2)}) collective-permute-start(bf16[1,320,128]{2,1,0:T(8,128)(2,1)} %get-tuple-element.266), channel_id=1, source_target_pairs={{0,16},{4,20},{8,24},{12,28},{16,0},{20,4},{24,8},{28,12},{1,17},{... | collective-permute-start | bytes 245768 | tf_op jit(solution)/shard_map/ppermute | solution.py:733
  157.6 13.5 %collective-permute-start.19 = (bf16[1,320,128]{2,1,0:T(8,128)(2,1)}, bf16[1,320,128]{2,1,0:T(8,128)(2,1)}, u32[]{:S(2)}, u32[]{:S(2)}) collective-permute-start(bf16[1,320,128]{2,1,0:T(8,128)(2,1)} %get-tuple-element.267), channel_id=1, source_target_pairs={{0,8},{4,12},{8,0},{12,4},{16,24},{20,28},{24,16},{28,20},{1,9},{5... | collective-permute-start | bytes 245768 | tf_op jit(solution)/shard_map/ppermute | solution.py:733
  158.5 12.6 %collective-permute-start.18 = (bf16[8,160,128]{2,1,0:T(8,128)(2,1)S(1)}, bf16[8,160,128]{2,1,0:T(8,128)(2,1)S(1)}, u32[]{:S(2)}, u32[]{:S(2)}) collective-permute-start(bf16[8,160,128]{2,1,0:T(8,128)(2,1)S(1)} %get-tuple-element.238), channel_id=1, source_target_pairs={{0,4},{4,0},{8,12},{12,8},{16,20},{20,16},{24,28},{28,24},{1,5},{5... | collective-permute-start | bytes 983048 | tf_op jit(solution)/shard_map/ppermute | solution.py:733
  159.4 11.8 %collective-permute-start.17 = (bf16[8,160,128]{2,1,0:T(8,128)(2,1)S(1)}, bf16[8,160,128]{2,1,0:T(8,128)(2,1)S(1)}, u32[]{:S(2)}, u32[]{:S(2)}) collective-permute-start(bf16[8,160,128]{2,1,0:T(8,128)(2,1)S(1)} %get-tuple-element.239), channel_id=1, source_target_pairs={{0,2},{1,3},{2,0},{3,1},{4,6},{5,7},{6,4},{7,5},{8,10},{9,11},{10,... | collective-permute-start | bytes 983048 | tf_op jit(solution)/shard_map/ppermute | solution.py:733
  161.3 9.8 %copy-start.19 = (f32[80,300]{1,0:T(8,128)S(1)}, f32[80,300]{1,0:T(8,128)}, u32[]{:S(2)}) copy-start(f32[80,300]{1,0:T(8,128)} %get-tuple-element.169) | copy-start | bytes 288004
  172.2 1.6 collective-permute-start.24
  172.4 6.7 %collective-permute-start.23 = (bf16[4,160,128]{2,1,0:T(8,128)(2,1)S(1)}, bf16[4,160,128]{2,1,0:T(8,128)(2,1)S(1)}, u32[]{:S(2)}, u32[]{:S(2)}) collective-permute-start(bf16[4,160,128]{2,1,0:T(8,128)(2,1)S(1)} %get-tuple-element.236), channel_id=1, source_target_pairs={{0,2},{1,3},{2,0},{3,1},{4,6},{5,7},{6,4},{7,5},{8,10},{9,11},{10,... | collective-permute-start | bytes 491528 | tf_op jit(solution)/shard_map/ppermute | solution.py:733
  172.5 6.6 %collective-permute-start.22 = (bf16[4,160,128]{2,1,0:T(8,128)(2,1)S(1)}, bf16[4,160,128]{2,1,0:T(8,128)(2,1)S(1)}, u32[]{:S(2)}, u32[]{:S(2)}) collective-permute-start(bf16[4,160,128]{2,1,0:T(8,128)(2,1)S(1)} %get-tuple-element.237), channel_id=1, source_target_pairs={{0,4},{4,0},{8,12},{12,8},{16,20},{20,16},{24,28},{28,24},{1,5},{5... | collective-permute-start | bytes 491528 | tf_op jit(solution)/shard_map/ppermute | solution.py:733
  179.3 6.6 %copy-start.10 = (bf16[1024,300]{1,0:T(8,128)(2,1)S(1)}, bf16[1024,300]{1,0:T(8,128)(2,1)}, u32[]{:S(2)}) copy-start(bf16[1024,300]{1,0:T(8,128)(2,1)} %get-tuple-element.173) | copy-start | bytes 1843204
  180.0 13.5 %collective-permute-start.28 = (bf16[1,320,128]{2,1,0:T(8,128)(2,1)}, bf16[1,320,128]{2,1,0:T(8,128)(2,1)}, u32[]{:S(2)}, u32[]{:S(2)}) collective-permute-start(bf16[1,320,128]{2,1,0:T(8,128)(2,1)} %get-tuple-element.263), channel_id=1, source_target_pairs={{0,24},{4,28},{8,16},{12,20},{16,8},{20,12},{24,0},{28,4},{1,25},{... | collective-permute-start | bytes 245768 | tf_op jit(solution)/shard_map/ppermute | solution.py:733
  183.6 5.9 %copy-start.1 = (f32[1024,300]{1,0:T(8,128)S(1)}, f32[1024,300]{1,0:T(8,128)}, u32[]{:S(2)}) copy-start(f32[1024,300]{1,0:T(8,128)} %get-tuple-element.174) | copy-start | bytes 3686404
  187.0 12.0 %collective-permute-start.25 = (f32[80,600]{1,0:T(8,128)}, f32[80,600]{1,0:T(8,128)}, u32[]{:S(2)}, u32[]{:S(2)}) collective-permute-start(f32[80,600]{1,0:T(8,128)} %add.170), channel_id=1, source_target_pairs={{0,2},{1,3},{2,0},{3,1},{4,6},{5,7},{6,4},{7,5},{8,10},{9,11},{10,... | collective-permute-start | bytes 576008 | tf_op jit(solution)/shard_map/ppermute | solution.py:733
  188.7 6.0 %collective-permute-start.26 = (bf16[1,320,128]{2,1,0:T(8,128)(2,1)}, bf16[1,320,128]{2,1,0:T(8,128)(2,1)}, u32[]{:S(2)}, u32[]{:S(2)}) collective-permute-start(bf16[1,320,128]{2,1,0:T(8,128)(2,1)} %get-tuple-element.262), channel_id=1, source_target_pairs={{0,8},{4,12},{8,0},{12,4},{16,24},{20,28},{24,16},{28,20},{1,9},{5... | collective-permute-start | bytes 245768 | tf_op jit(solution)/shard_map/ppermute | solution.py:733
  188.7 6.0 %collective-permute-start.27 = (bf16[1,320,128]{2,1,0:T(8,128)(2,1)S(1)}, bf16[1,320,128]{2,1,0:T(8,128)(2,1)}, u32[]{:S(2)}, u32[]{:S(2)}) collective-permute-start(bf16[1,320,128]{2,1,0:T(8,128)(2,1)S(1)} %get-tuple-element.264), channel_id=1, source_target_pairs={{0,16},{4,20},{8,24},{12,28},{16,0},{20,4},{24,8},{28,12},{1,17},{... | collective-permute-start | bytes 245768 | tf_op jit(solution)/shard_map/ppermute | solution.py:733
  (9 other events, 17.9 us)

commit v3 on v2

--- a/solution.py
+++ b/solution.py
@@ -640,7 +640,7 @@
         order = [
             (t, i, k)
             for later in (False, True)
-            for t in [tiles] + list(range(tiles))
+            for t in ([tiles, *range(tiles)] if "dz" in inputs else range(tiles + 1))
             for i, k in enumerate(buffers)
             if (k in LATER and k != soon) == later
         ]

time: 205 us -> 205 us (level)
  transfers between devices with their start and end apart: 29 -> 29, of which waited for: 7 -> 7; matrix products, arithmetic and copies ran while one was open for 15% -> 15% of each run, Pallas kernels for 23% -> 22%
where the time goes in v3:
time: 205 us; the launch traced here: 202 us
  Pallas kernels  96.5 us (47%)
  starting transfers between devices  35.5 us (17%)
  waiting for transfers between devices  28.2 us (14%)
  local copies, waits for them, and re-layouts  21.9 us (11%)
  other arithmetic  17.8 us (9%)
    pallas_call x5, Pallas kernels, call(): pl.pallas_call(kernel, out_shape=[jax.ShapeDtypeStruct(s, d) for s, d in...  96.5 us
    ppermute x27, starting transfers between devices, exchange(): lax.ppermute(x, axis, [(i, i ^ value << shift) for i in range(sizes[axis])])  30.2 us
    ppermute x27, waiting for transfers between devices, exchange(): lax.ppermute(x, axis, [(i, i ^ value << shift) for i in range(sizes[axis])])  28.2 us
    unnamed x75, local copies, waits for them, and re-layouts  15.8 us
  transfers between devices with their start and end apart: 29, of which 7 were waited for; matrix products, arithmetic and copies ran while one was open for 15% of the time, Pallas kernels for 22%

profile of v3, /device:TPU:0, one launch (start us, length us, event | category | flops | bytes accessed | tf_op | source)
XLA Modules:
  0.0 201.8 jit_solution(13386771252108635422)
XLA Ops:
  0.7 1.1 convert_element_type.232
  1.8 0.8 slice_reduce_fusion
  3.4 5.1 %collective-permute-start.2 = (bf16[1,640,128]{2,1,0:T(8,128)(2,1)S(1)}, bf16[1,640,128]{2,1,0:T(8,128)(2,1)S(1)}, u32[]{:S(2)}, u32[]{:S(2)}) collective-permute-start(bf16[1,640,128]{2,1,0:T(8,128)(2,1)S(1)} %bitcast.87), channel_id=1, source_target_pairs={{0,24},{4,28},{8,16},{12,20},{16,8},{20,12},{24,0},{28,4},{1,25},{... | collective-permute-start | bytes 491528 | tf_op jit(solution)/shard_map/ppermute | solution.py:733
  10.3 1.2 copy.101
  11.5 1.5 copy.99
  13.0 0.7 fusion.8
  14.4 1.6 fusion.6
  17.3 1.3 collective-permute-start.10
  18.5 3.9 %collective-permute-start.9 = (bf16[528,300]{1,0:T(8,128)(2,1)}, bf16[528,300]{1,0:T(8,128)(2,1)}, u32[]{:S(2)}, u32[]{:S(2)}) collective-permute-start(bf16[528,300]{1,0:T(8,128)(2,1)} %get-tuple-element.277), channel_id=1, source_target_pairs={{0,1},{1,2},{2,3},{4,5},{5,6},{6,7},{8,9},{9,10},{10,11},{12,13},{... | collective-permute-start | bytes 950408 | tf_op jit(solution)/shard_map/ppermute | solution.py:811
  22.6 0.7 copy.112.refs_15_.refs_23_
  23.8 1.1 pad_maximum_fusion
  25.0 1.7 collective-permute-start.3
  26.7 1.5 collective-permute-start.6
  29.6 5.5 %collective-permute-done.3 = bf16[4,320,128]{2,1,0:T(8,128)(2,1)S(1)} collective-permute-done((bf16[4,320,128]{2,1,0:T(8,128)(2,1)S(1)}, bf16[4,320,128]{2,1,0:T(8,128)(2,1)S(1)}, u32[]{:S(2)}, u32[]{:S(2)}) %collective-permute-start.3) | collective-permute-done | bytes 327712 | tf_op jit(solution)/shard_map/ppermute | solution.py:733
  36.5 1.0 collective-permute-start.7
  38.5 13.9 %collective-permute-done.7 = bf16[8,320,128]{2,1,0:T(8,128)(2,1)S(1)} collective-permute-done((bf16[8,320,128]{2,1,0:T(8,128)(2,1)S(1)}, bf16[8,320,128]{2,1,0:T(8,128)(2,1)S(1)}, u32[]{:S(2)}, u32[]{:S(2)}) %collective-permute-start.7) | collective-permute-done | bytes 655392 | tf_op jit(solution)/shard_map/ppermute | solution.py:733
  53.2 0.7 copy.113.refs_16_.refs_7_.refs_24_
  54.9 0.9 broadcast_add_fusion.refs_11_.refs_4_.refs_19_
  55.8 1.8 collective-permute-done.5.refs_2_
  57.6 51.2 %front.1 = (f32[80,300]{1,0:T(8,128)}, f32[80,300]{1,0:T(8,128)}, bf16[1280,300]{1,0:T(8,128)(2,1)}, bf16[1280,300]{1,0:T(8,128)(2,1)}, bf16[1024,300]{1,0:T(8,1...) custom-call(s32[2,32]{1,0:T(2,128)} %pad_add_fusion.1.refs_0_.refs_2, ...), custom_call_target="tpu_custom_call" | custom-call | flops 60000002048 | bytes 60000000 | tf_op jit(solution)/shard_map/front/pallas_call | solution.py:685
  109.0 9.0 %last_inputs.1 = (f32[80,300]{1,0:T(8,128)}, bf16[1280,300]{1,0:T(8,128)(2,1)}, bf16[1280,300]{1,0:T(8,128)(2,1)}) custom-call(bf16[300,300]{1,0:T(8,128)(2,1)} %get-tuple-element.106.refs_0_, bf16[300,684]{1,0:T(8,128)(2,1)} %get-tuple-element.107.refs_1_, bf16[300,300]{1,0:T(8,128)(2,1)} %get-tuple-element.108.refs_2_, ...), custom_call_target="tpu_custom_call" | custom-call | flops 8999999488 | bytes 9000000 | tf_op jit(solution)/shard_map/last_inputs/pallas_call | solution.py:685
  118.2 0.8 collective-permute-start.13
  119.0 2.0 collective-permute-start.12
  121.0 12.1 %first_ffn.1 = (bf16[1360,300]{1,0:T(8,128)(2,1)}, f32[4,8,300]{2,1,0:T(8,128)}, bf16[1360,384]{1,0:T(8,128)(2,1)}, bf16[1360,1200]{1,0:T(8,128)(2,1)}) custom-call(bf16[1200,300]{1,0:T(8,128)(2,1)} %get-tuple-element.105.refs_0_, bf16[1280,300]{1,0:T(8,128)(2,1)} %get-tuple-element.117.refs_1_, bf16[1360,384]{1,0:T(8,128)(2,1)} %get-tuple-element.118.refs_2_, ...), custom_call_target="tpu_custom_call" | custom-call | flops 12999999488 | bytes 13000000 | tf_op jit(solution)/shard_map/first_ffn/pallas_call | solution.py:685
  133.4 1.3 collective-permute-start.14
  134.7 14.5 %first.1 = (bf16[1280,684]{1,0:T(8,128)(2,1)}, bf16[80,300]{1,0:T(8,128)(2,1)}, bf16[80,684]{1,0:T(8,128)(2,1)}, bf16[32,160,128]{2,1,0:T(8,128)(2,1)}, bf16[32,160,128]{2,1,0:T(8,128)(2,1)}) custom-call(bf16[300,300]{1,0:T(8,128)(2,1)} %get-tuple-element.103.refs_0_, bf16[300,684]{1,0:T(8,128)(2,1)} %get-tuple-element.104.refs_1_, ...), custom_call_target="tpu_custom_call" | custom-call | flops 17999998976 | bytes 18000000 | tf_op jit(solution)/shard_map/first/pallas_call | solution.py:685
  149.9 1.5 add_convert_fusion.9
  151.5 1.7 collective-permute-done.16
  153.9 3.6 %collective-permute-start.21 = (bf16[1,320,128]{2,1,0:T(8,128)(2,1)}, bf16[1,320,128]{2,1,0:T(8,128)(2,1)}, u32[]{:S(2)}, u32[]{:S(2)}) collective-permute-start(bf16[1,320,128]{2,1,0:T(8,128)(2,1)} %get-tuple-element.265), channel_id=1, source_target_pairs={{0,24},{4,28},{8,16},{12,20},{16,8},{20,12},{24,0},{28,4},{1,25},{... | collective-permute-start | bytes 245768 | tf_op jit(solution)/shard_map/ppermute | solution.py:733
  157.5 0.8 collective-permute-start.19
  158.4 0.8 collective-permute-start.18
  159.3 1.9 collective-permute-start.17
  161.2 9.8 %first_inputs.1 = (f32[80,300]{1,0:T(8,128)}, f32[1024,300]{1,0:T(8,128)}, f32[1024,300]{1,0:T(8,128)}) custom-call(bf16[300,300]{1,0:T(8,128)(2,1)} %get-tuple-element.154.refs_0_, bf16[300,684]{1,0:T(8,128)(2,1)} %get-tuple-element.104.refs_1_, bf16[300,300]{1,0:T(8,128)(2,1)} %get-tuple-element.155.refs_2_, bf16[300,300]{1,0:T(8,128)(2,1)} %get-tuple-element.156.refs_3_, ...), custom_call_target="tpu_custom_call" | custom-call | flops 8999999488 | bytes 9000000 | tf_op jit(solution)/shard_map/first_inputs/pallas_call | solution.py:685
  171.0 1.0 maximum_select_fusion
  172.4 1.3 collective-permute-start.22
  174.4 4.6 %collective-permute-done.23 = bf16[4,160,128]{2,1,0:T(8,128)(2,1)S(1)} collective-permute-done((bf16[4,160,128]{2,1,0:T(8,128)(2,1)S(1)}, bf16[4,160,128]{2,1,0:T(8,128)(2,1)S(1)}, u32[]{:S(2)}, u32[]{:S(2)}) %collective-permute-start.23) | collective-permute-done | bytes 163872 | tf_op jit(solution)/shard_map/ppermute | solution.py:733
  179.9 3.6 %collective-permute-start.28 = (bf16[1,320,128]{2,1,0:T(8,128)(2,1)}, bf16[1,320,128]{2,1,0:T(8,128)(2,1)}, u32[]{:S(2)}, u32[]{:S(2)}) collective-permute-start(bf16[1,320,128]{2,1,0:T(8,128)(2,1)} %get-tuple-element.263), channel_id=1, source_target_pairs={{0,24},{4,28},{8,16},{12,20},{16,8},{20,12},{24,0},{28,4},{1,25},{... | collective-permute-start | bytes 245768 | tf_op jit(solution)/shard_map/ppermute | solution.py:733
  183.5 2.3 %copy.117 = bf16[1,1024,300]{1,2,0:T(8,128)(2,1)} copy(bf16[1,1024,300]{2,1,0:T(8,128)(2,1)} %bitcast.86) | data formatting | bytes 1228800
  185.8 1.1 copy.118
  186.9 1.7 collective-permute-start.25
  188.6 0.8 collective-permute-start.27
  189.4 2.0 %copy.119 = f32[1,1024,300]{1,0,2:T(1,128)} copy(f32[1,1024,300]{2,1,0:T(8,128)S(1)} %bitcast.73) | data formatting | bytes 2457600
  191.4 2.0 %copy.120 = f32[1,1024,300]{1,0,2:T(1,128)} copy(f32[1,1024,300]{2,1,0:T(8,128)S(1)} %bitcast.72) | data formatting | bytes 2457600
  193.4 1.0 convert_add_fusion
  194.6 1.1 convert_add_fusion.1
  196.5 2.4 %fusion.25 = (bf16[2,36600]{1,0:T(2,128)(2,1)}, f32[2,36600]{1,0:T(2,128)}, f32[2,36600]{1,0:T(2,128)}, f32[2,36600]{1,0:T(2,128)}, f32[2,36600]{1,0:T(2,128)}) fusion(f32[2,36600]{1,0:T(2,128)S(1)} %copy-done.9, f32[2,36600]{1,0:T(2,128)S(1)} %copy-done.16, f32[2,36600]{1,0:T(2,128)S(1)} %copy-done.17, f32[1,36600]{1,0:T(1,128)S(1)} %stack_reshape.7, ...), kind=kLoop, calls=%fused_computation.125 | loop fusion | flops 1244400 | bytes 2488800 | tf_op jit(solution)/shard_map/convert_element_type | solution.py:1149
  198.9 1.1 add.171
  200.6 0.7 slice_bitcast_fusion
  (152 shorter events, 16.3 us)
Async XLA Ops:
  0.6 8.5 %copy-start.24 = (s32[1,1024]{1,0:T(1,128)S(1)}, s32[1,1024]{1,0:T(1,128)}, u32[]{:S(2)}) copy-start(s32[1,1024]{1,0:T(1,128)} %param.24) | copy-start | bytes 12292
  0.7 8.5 %copy-start.23 = (s32[1,1024]{1,0:T(1,128)S(1)}, s32[1,1024]{1,0:T(1,128)}, u32[]{:S(2)}) copy-start(s32[1,1024]{1,0:T(1,128)} %param.22) | copy-start | bytes 12292
  0.7 8.5 %copy-start.11 = (bf16[1,1024,300]{1,2,0:T(8,128)(2,1)S(1)}, bf16[1,1024,300]{1,2,0:T(8,128)(2,1)}, u32[]{:S(2)}) copy-start(bf16[1,1024,300]{1,2,0:T(8,128)(2,1)} %param.17) | copy-start | bytes 1843204
  2.8 6.8 %copy-start.12 = (bf16[1,1024,300]{1,2,0:T(8,128)(2,1)S(1)}, bf16[1,1024,300]{1,2,0:T(8,128)(2,1)}, u32[]{:S(2)}) copy-start(bf16[1,1024,300]{1,2,0:T(8,128)(2,1)} %param.18) | copy-start | bytes 1843204
  3.4 20.4 %collective-permute-start.2 = (bf16[1,640,128]{2,1,0:T(8,128)(2,1)S(1)}, bf16[1,640,128]{2,1,0:T(8,128)(2,1)S(1)}, u32[]{:S(2)}, u32[]{:S(2)}) collective-permute-start(bf16[1,640,128]{2,1,0:T(8,128)(2,1)S(1)} %bitcast.87), channel_id=1, source_target_pairs={{0,24},{4,28},{8,16},{12,20},{16,8},{20,12},{24,0},{28,4},{1,25},{... | collective-permute-start | bytes 491528 | tf_op jit(solution)/shard_map/ppermute | solution.py:733
  8.5 15.3 %collective-permute-start.1 = (bf16[1,640,128]{2,1,0:T(8,128)(2,1)S(1)}, bf16[1,640,128]{2,1,0:T(8,128)(2,1)}, u32[]{:S(2)}, u32[]{:S(2)}) collective-permute-start(bf16[1,640,128]{2,1,0:T(8,128)(2,1)S(1)} %bitcast.88), channel_id=1, source_target_pairs={{0,16},{4,20},{8,24},{12,28},{16,0},{20,4},{24,8},{28,12},{1,17},{... | collective-permute-start | bytes 491528 | tf_op jit(solution)/shard_map/ppermute | solution.py:733
  8.5 15.3 %collective-permute-start = (bf16[1,640,128]{2,1,0:T(8,128)(2,1)S(1)}, bf16[1,640,128]{2,1,0:T(8,128)(2,1)}, u32[]{:S(2)}, u32[]{:S(2)}) collective-permute-start(bf16[1,640,128]{2,1,0:T(8,128)(2,1)S(1)} %bitcast.89), channel_id=1, source_target_pairs={{0,8},{4,12},{8,0},{12,4},{16,24},{20,28},{24,16},{28,20},{1,9},{5... | collective-permute-start | bytes 491528 | tf_op jit(solution)/shard_map/ppermute | solution.py:733
  10.3 3.4 %copy-start.7 = (bf16[1,1024,300]{2,1,0:T(8,128)(2,1)}, bf16[1,1024,300]{2,1,0:T(8,128)(2,1)S(1)}, u32[]{:S(2)}) copy-start(bf16[1,1024,300]{2,1,0:T(8,128)(2,1)S(1)} %copy.100) | copy-start | bytes 1843204
  11.5 5.2 %copy-start.25 = (pred[300]{0:T(512)(128)(4,1)S(1)}, pred[300]{0:T(512)(128)(4,1)}, u32[]{:S(2)}) copy-start(pred[300]{0:T(512)(128)(4,1)} %constant.19.clone.1) | copy-start | bytes 904
  11.5 11.0 %copy-start.26 = (s32[32]{0:T(128)S(1)}, s32[32]{0:T(128)}, u32[]{:S(2)}) copy-start(s32[32]{0:T(128)} %param.25) | copy-start | bytes 388
  11.5 11.0 %copy-start.27 = (s32[1,80]{1,0:T(1,128)S(1)}, s32[1,80]{1,0:T(1,128)}, u32[]{:S(2)}) copy-start(s32[1,80]{1,0:T(1,128)} %param.23) | copy-start | bytes 964
  13.0 11.9 %copy-start.8 = (bf16[1,1024,300]{2,1,0:T(8,128)(2,1)}, bf16[1,1024,300]{2,1,0:T(8,128)(2,1)S(1)}, u32[]{:S(2)}) copy-start(bf16[1,1024,300]{2,1,0:T(8,128)(2,1)S(1)} %copy.99) | copy-start | bytes 1843204
  17.3 11.0 %collective-permute-start.10 = (bf16[528,300]{1,0:T(8,128)(2,1)S(1)}, bf16[528,300]{1,0:T(8,128)(2,1)}, u32[]{:S(2)}, u32[]{:S(2)}) collective-permute-start(bf16[528,300]{1,0:T(8,128)(2,1)S(1)} %get-tuple-element.276), channel_id=1, source_target_pairs={{1,0},{2,1},{3,2},{5,4},{6,5},{7,6},{9,8},{10,9},{11,10},{13,12},{... | collective-permute-start | bytes 950408 | tf_op jit(solution)/shard_map/ppermute | solution.py:812
  18.5 10.4 %collective-permute-start.9 = (bf16[528,300]{1,0:T(8,128)(2,1)}, bf16[528,300]{1,0:T(8,128)(2,1)}, u32[]{:S(2)}, u32[]{:S(2)}) collective-permute-start(bf16[528,300]{1,0:T(8,128)(2,1)} %get-tuple-element.277), channel_id=1, source_target_pairs={{0,1},{1,2},{2,3},{4,5},{5,6},{6,7},{8,9},{9,10},{10,11},{12,13},{... | collective-permute-start | bytes 950408 | tf_op jit(solution)/shard_map/ppermute | solution.py:811
  25.0 10.2 %collective-permute-start.3 = (bf16[4,320,128]{2,1,0:T(8,128)(2,1)S(1)}, bf16[4,320,128]{2,1,0:T(8,128)(2,1)S(1)}, u32[]{:S(2)}, u32[]{:S(2)}) collective-permute-start(bf16[4,320,128]{2,1,0:T(8,128)(2,1)S(1)} %get-tuple-element.97), channel_id=1, source_target_pairs={{0,4},{4,0},{8,12},{12,8},{16,20},{20,16},{24,28},{28,24},{1,5},{5... | collective-permute-start | bytes 983048 | tf_op jit(solution)/shard_map/ppermute | solution.py:733
  26.7 9.7 %collective-permute-start.6 = (bf16[4,320,128]{2,1,0:T(8,128)(2,1)S(1)}, bf16[4,320,128]{2,1,0:T(8,128)(2,1)S(1)}, u32[]{:S(2)}, u32[]{:S(2)}) collective-permute-start(bf16[4,320,128]{2,1,0:T(8,128)(2,1)S(1)} %get-tuple-element.98), channel_id=1, source_target_pairs={{0,2},{1,3},{2,0},{3,1},{4,6},{5,7},{6,4},{7,5},{8,10},{9,11},{10,... | collective-permute-start | bytes 983048 | tf_op jit(solution)/shard_map/ppermute | solution.py:733
  35.2 17.4 %collective-permute-start.4 = (bf16[8,320,128]{2,1,0:T(8,128)(2,1)S(1)}, bf16[8,320,128]{2,1,0:T(8,128)(2,1)S(1)}, u32[]{:S(2)}, u32[]{:S(2)}) collective-permute-start(bf16[8,320,128]{2,1,0:T(8,128)(2,1)S(1)} %pad_maximum_fusion.1), channel_id=1, source_target_pairs={{0,2},{1,3},{2,0},{3,1},{4,6},{5,7},{6,4},{7,5},{8,10},{9,11},{10,... | collective-permute-start | bytes 1966088 | tf_op jit(solution)/shard_map/ppermute | solution.py:733
  36.5 15.9 %collective-permute-start.7 = (bf16[8,320,128]{2,1,0:T(8,128)(2,1)S(1)}, bf16[8,320,128]{2,1,0:T(8,128)(2,1)S(1)}, u32[]{:S(2)}, u32[]{:S(2)}) collective-permute-start(bf16[8,320,128]{2,1,0:T(8,128)(2,1)S(1)} %pad_maximum_fusion.2), channel_id=1, source_target_pairs={{0,4},{4,0},{8,12},{12,8},{16,20},{20,16},{24,28},{28,24},{1,5},{5... | collective-permute-start | bytes 1966088 | tf_op jit(solution)/shard_map/ppermute | solution.py:733
  38.0 16.2 %copy-start.22 = (s32[1,1280]{1,0:T(1,128)}, s32[1,1280]{1,0:T(1,128)S(1)}, u32[]{:S(2)}) copy-start(s32[1,1280]{1,0:T(1,128)S(1)} %get-tuple-element.289.refs_12_.refs_5_.refs_20_) | copy-start | bytes 15364
  52.5 3.3 %collective-permute-start.8 = (bf16[16,320,128]{2,1,0:T(8,128)(2,1)S(1)}, bf16[16,320,128]{2,1,0:T(8,128)(2,1)}, u32[]{:S(2)}, u32[]{:S(2)}) collective-permute-start(bf16[16,320,128]{2,1,0:T(8,128)(2,1)S(1)} %constant_dynamic-update-slice_fusion.9.refs_3_), channel_id=1, source_target_pairs={{0,1},{1,0},{2,3},{3,2},{4,5},{5,4},{6,7},{7,6},{8,9},{9,8},{10,11... | collective-permute-start | bytes 3932168 | tf_op jit(solution)/shard_map/ppermute | solution.py:733
  52.7 4.9 %copy-start.21 = (bf16[16,320,128]{2,1,0:T(8,128)(2,1)}, bf16[16,320,128]{2,1,0:T(8,128)(2,1)S(1)}, u32[]{:S(2)}) copy-start(bf16[16,320,128]{2,1,0:T(8,128)(2,1)S(1)} %constant_dynamic-update-slice_fusion.6.refs_1_) | copy-start | bytes 3932164
  52.7 4.9 %collective-permute-start.5 = (bf16[16,320,128]{2,1,0:T(8,128)(2,1)S(1)}, bf16[16,320,128]{2,1,0:T(8,128)(2,1)}, u32[]{:S(2)}, u32[]{:S(2)}) collective-permute-start(bf16[16,320,128]{2,1,0:T(8,128)(2,1)S(1)} %constant_dynamic-update-slice_fusion.6.refs_1_), channel_id=1, source_target_pairs={{0,1},{1,0},{2,3},{3,2},{4,5},{5,4},{6,7},{7,6},{8,9},{9,8},{10,11... | collective-permute-start | bytes 3932168 | tf_op jit(solution)/shard_map/ppermute | solution.py:733
  108.8 9.2 %collective-permute-start.11 = (bf16[32,160,128]{2,1,0:T(8,128)(2,1)}, bf16[32,160,128]{2,1,0:T(8,128)(2,1)S(1)}, u32[]{:S(2)}, u32[]{:S(2)}) collective-permute-start(bf16[32,160,128]{2,1,0:T(8,128)(2,1)} %get-tuple-element.123), channel_id=1, source_target_pairs={{0,1},{1,0},{2,3},{3,2},{4,5},{5,4},{6,7},{7,6},{8,9},{9,8},{10,11... | collective-permute-start | bytes 3932168 | tf_op jit(solution)/shard_map/ppermute | solution.py:733
  109.0 9.0 %copy-start.3 = (bf16[32,160,128]{2,1,0:T(8,128)(2,1)S(1)}, bf16[32,160,128]{2,1,0:T(8,128)(2,1)}, u32[]{:S(2)}) copy-start(bf16[32,160,128]{2,1,0:T(8,128)(2,1)} %get-tuple-element.127) | copy-start | bytes 3932164
  118.0 15.2 %copy-start.4 = (bf16[32,160,128]{2,1,0:T(8,128)(2,1)}, bf16[32,160,128]{2,1,0:T(8,128)(2,1)S(1)}, u32[]{:S(2)}) copy-start(bf16[32,160,128]{2,1,0:T(8,128)(2,1)S(1)} %collective-permute-done.11) | copy-start | bytes 3932164
  118.2 14.9 %collective-permute-start.13 = (bf16[8,160,128]{2,1,0:T(8,128)(2,1)S(1)}, bf16[8,160,128]{2,1,0:T(8,128)(2,1)S(1)}, u32[]{:S(2)}, u32[]{:S(2)}) collective-permute-start(bf16[8,160,128]{2,1,0:T(8,128)(2,1)S(1)} %get-tuple-element.244), channel_id=1, source_target_pairs={{0,4},{4,0},{8,12},{12,8},{16,20},{20,16},{24,28},{28,24},{1,5},{5... | collective-permute-start | bytes 983048 | tf_op jit(solution)/shard_map/ppermute | solution.py:733
  119.0 14.1 %collective-permute-start.12 = (bf16[8,160,128]{2,1,0:T(8,128)(2,1)S(1)}, bf16[8,160,128]{2,1,0:T(8,128)(2,1)S(1)}, u32[]{:S(2)}, u32[]{:S(2)}) collective-permute-start(bf16[8,160,128]{2,1,0:T(8,128)(2,1)S(1)} %get-tuple-element.245), channel_id=1, source_target_pairs={{0,2},{1,3},{2,0},{3,1},{4,6},{5,7},{6,4},{7,5},{8,10},{9,11},{10,... | collective-permute-start | bytes 983048 | tf_op jit(solution)/shard_map/ppermute | solution.py:733
  133.1 16.1 %copy-start.14 = (bf16[8,160,128]{2,1,0:T(8,128)(2,1)}, bf16[8,160,128]{2,1,0:T(8,128)(2,1)S(1)}, u32[]{:S(2)}) copy-start(bf16[8,160,128]{2,1,0:T(8,128)(2,1)S(1)} %collective-permute-done.13) | copy-start | bytes 983044
  133.1 16.1 %copy-start.15 = (bf16[8,160,128]{2,1,0:T(8,128)(2,1)}, bf16[8,160,128]{2,1,0:T(8,128)(2,1)S(1)}, u32[]{:S(2)}) copy-start(bf16[8,160,128]{2,1,0:T(8,128)(2,1)S(1)} %collective-permute-done.12) | copy-start | bytes 983044
  133.3 15.9 %collective-permute-start.15 = (bf16[4,160,128]{2,1,0:T(8,128)(2,1)S(1)}, bf16[4,160,128]{2,1,0:T(8,128)(2,1)S(1)}, u32[]{:S(2)}, u32[]{:S(2)}) collective-permute-start(bf16[4,160,128]{2,1,0:T(8,128)(2,1)S(1)} %get-tuple-element.242), channel_id=1, source_target_pairs={{0,2},{1,3},{2,0},{3,1},{4,6},{5,7},{6,4},{7,5},{8,10},{9,11},{10,... | collective-permute-start | bytes 491528 | tf_op jit(solution)/shard_map/ppermute | solution.py:733
  133.4 15.8 %collective-permute-start.14 = (bf16[4,160,128]{2,1,0:T(8,128)(2,1)S(1)}, bf16[4,160,128]{2,1,0:T(8,128)(2,1)S(1)}, u32[]{:S(2)}, u32[]{:S(2)}) collective-permute-start(bf16[4,160,128]{2,1,0:T(8,128)(2,1)S(1)} %get-tuple-element.243), channel_id=1, source_target_pairs={{0,4},{4,0},{8,12},{12,8},{16,20},{20,16},{24,28},{28,24},{1,5},{5... | collective-permute-start | bytes 491528 | tf_op jit(solution)/shard_map/ppermute | solution.py:733
  149.9 8.3 %copy-start.2 = (bf16[32,160,128]{2,1,0:T(8,128)(2,1)S(1)}, bf16[32,160,128]{2,1,0:T(8,128)(2,1)}, u32[]{:S(2)}) copy-start(bf16[32,160,128]{2,1,0:T(8,128)(2,1)} %get-tuple-element.144) | copy-start | bytes 3932164
  149.9 3.2 %collective-permute-start.16 = (bf16[32,160,128]{2,1,0:T(8,128)(2,1)}, bf16[32,160,128]{2,1,0:T(8,128)(2,1)S(1)}, u32[]{:S(2)}, u32[]{:S(2)}) collective-permute-start(bf16[32,160,128]{2,1,0:T(8,128)(2,1)} %get-tuple-element.150), channel_id=1, source_target_pairs={{0,1},{1,0},{2,3},{3,2},{4,5},{5,4},{6,7},{7,6},{8,9},{9,8},{10,11... | collective-permute-start | bytes 3932168 | tf_op jit(solution)/shard_map/ppermute | solution.py:733
  153.9 17.1 %collective-permute-start.21 = (bf16[1,320,128]{2,1,0:T(8,128)(2,1)}, bf16[1,320,128]{2,1,0:T(8,128)(2,1)}, u32[]{:S(2)}, u32[]{:S(2)}) collective-permute-start(bf16[1,320,128]{2,1,0:T(8,128)(2,1)} %get-tuple-element.265), channel_id=1, source_target_pairs={{0,24},{4,28},{8,16},{12,20},{16,8},{20,12},{24,0},{28,4},{1,25},{... | collective-permute-start | bytes 245768 | tf_op jit(solution)/shard_map/ppermute | solution.py:733
  157.5 13.5 %collective-permute-start.20 = (bf16[1,320,128]{2,1,0:T(8,128)(2,1)}, bf16[1,320,128]{2,1,0:T(8,128)(2,1)}, u32[]{:S(2)}, u32[]{:S(2)}) collective-permute-start(bf16[1,320,128]{2,1,0:T(8,128)(2,1)} %get-tuple-element.266), channel_id=1, source_target_pairs={{0,16},{4,20},{8,24},{12,28},{16,0},{20,4},{24,8},{28,12},{1,17},{... | collective-permute-start | bytes 245768 | tf_op jit(solution)/shard_map/ppermute | solution.py:733
  157.5 13.5 %collective-permute-start.19 = (bf16[1,320,128]{2,1,0:T(8,128)(2,1)}, bf16[1,320,128]{2,1,0:T(8,128)(2,1)}, u32[]{:S(2)}, u32[]{:S(2)}) collective-permute-start(bf16[1,320,128]{2,1,0:T(8,128)(2,1)} %get-tuple-element.267), channel_id=1, source_target_pairs={{0,8},{4,12},{8,0},{12,4},{16,24},{20,28},{24,16},{28,20},{1,9},{5... | collective-permute-start | bytes 245768 | tf_op jit(solution)/shard_map/ppermute | solution.py:733
  158.4 12.6 %collective-permute-start.18 = (bf16[8,160,128]{2,1,0:T(8,128)(2,1)S(1)}, bf16[8,160,128]{2,1,0:T(8,128)(2,1)S(1)}, u32[]{:S(2)}, u32[]{:S(2)}) collective-permute-start(bf16[8,160,128]{2,1,0:T(8,128)(2,1)S(1)} %get-tuple-element.238), channel_id=1, source_target_pairs={{0,4},{4,0},{8,12},{12,8},{16,20},{20,16},{24,28},{28,24},{1,5},{5... | collective-permute-start | bytes 983048 | tf_op jit(solution)/shard_map/ppermute | solution.py:733
  159.3 11.8 %collective-permute-start.17 = (bf16[8,160,128]{2,1,0:T(8,128)(2,1)S(1)}, bf16[8,160,128]{2,1,0:T(8,128)(2,1)S(1)}, u32[]{:S(2)}, u32[]{:S(2)}) collective-permute-start(bf16[8,160,128]{2,1,0:T(8,128)(2,1)S(1)} %get-tuple-element.239), channel_id=1, source_target_pairs={{0,2},{1,3},{2,0},{3,1},{4,6},{5,7},{6,4},{7,5},{8,10},{9,11},{10,... | collective-permute-start | bytes 983048 | tf_op jit(solution)/shard_map/ppermute | solution.py:733
  161.2 9.8 %copy-start.19 = (f32[80,300]{1,0:T(8,128)S(1)}, f32[80,300]{1,0:T(8,128)}, u32[]{:S(2)}) copy-start(f32[80,300]{1,0:T(8,128)} %get-tuple-element.169) | copy-start | bytes 288004
  172.1 1.6 collective-permute-start.24
  172.3 6.7 %collective-permute-start.23 = (bf16[4,160,128]{2,1,0:T(8,128)(2,1)S(1)}, bf16[4,160,128]{2,1,0:T(8,128)(2,1)S(1)}, u32[]{:S(2)}, u32[]{:S(2)}) collective-permute-start(bf16[4,160,128]{2,1,0:T(8,128)(2,1)S(1)} %get-tuple-element.236), channel_id=1, source_target_pairs={{0,2},{1,3},{2,0},{3,1},{4,6},{5,7},{6,4},{7,5},{8,10},{9,11},{10,... | collective-permute-start | bytes 491528 | tf_op jit(solution)/shard_map/ppermute | solution.py:733
  172.4 6.6 %collective-permute-start.22 = (bf16[4,160,128]{2,1,0:T(8,128)(2,1)S(1)}, bf16[4,160,128]{2,1,0:T(8,128)(2,1)S(1)}, u32[]{:S(2)}, u32[]{:S(2)}) collective-permute-start(bf16[4,160,128]{2,1,0:T(8,128)(2,1)S(1)} %get-tuple-element.237), channel_id=1, source_target_pairs={{0,4},{4,0},{8,12},{12,8},{16,20},{20,16},{24,28},{28,24},{1,5},{5... | collective-permute-start | bytes 491528 | tf_op jit(solution)/shard_map/ppermute | solution.py:733
  179.2 6.6 %copy-start.10 = (bf16[1024,300]{1,0:T(8,128)(2,1)S(1)}, bf16[1024,300]{1,0:T(8,128)(2,1)}, u32[]{:S(2)}) copy-start(bf16[1024,300]{1,0:T(8,128)(2,1)} %get-tuple-element.173) | copy-start | bytes 1843204
  179.9 13.5 %collective-permute-start.28 = (bf16[1,320,128]{2,1,0:T(8,128)(2,1)}, bf16[1,320,128]{2,1,0:T(8,128)(2,1)}, u32[]{:S(2)}, u32[]{:S(2)}) collective-permute-start(bf16[1,320,128]{2,1,0:T(8,128)(2,1)} %get-tuple-element.263), channel_id=1, source_target_pairs={{0,24},{4,28},{8,16},{12,20},{16,8},{20,12},{24,0},{28,4},{1,25},{... | collective-permute-start | bytes 245768 | tf_op jit(solution)/shard_map/ppermute | solution.py:733
  183.5 5.9 %copy-start.1 = (f32[1024,300]{1,0:T(8,128)S(1)}, f32[1024,300]{1,0:T(8,128)}, u32[]{:S(2)}) copy-start(f32[1024,300]{1,0:T(8,128)} %get-tuple-element.174) | copy-start | bytes 3686404
  186.9 12.0 %collective-permute-start.25 = (f32[80,600]{1,0:T(8,128)}, f32[80,600]{1,0:T(8,128)}, u32[]{:S(2)}, u32[]{:S(2)}) collective-permute-start(f32[80,600]{1,0:T(8,128)} %add.170), channel_id=1, source_target_pairs={{0,2},{1,3},{2,0},{3,1},{4,6},{5,7},{6,4},{7,5},{8,10},{9,11},{10,... | collective-permute-start | bytes 576008 | tf_op jit(solution)/shard_map/ppermute | solution.py:733
  188.6 6.0 %collective-permute-start.26 = (bf16[1,320,128]{2,1,0:T(8,128)(2,1)}, bf16[1,320,128]{2,1,0:T(8,128)(2,1)}, u32[]{:S(2)}, u32[]{:S(2)}) collective-permute-start(bf16[1,320,128]{2,1,0:T(8,128)(2,1)} %get-tuple-element.262), channel_id=1, source_target_pairs={{0,8},{4,12},{8,0},{12,4},{16,24},{20,28},{24,16},{28,20},{1,9},{5... | collective-permute-start | bytes 245768 | tf_op jit(solution)/shard_map/ppermute | solution.py:733
  188.6 6.0 %collective-permute-start.27 = (bf16[1,320,128]{2,1,0:T(8,128)(2,1)S(1)}, bf16[1,320,128]{2,1,0:T(8,128)(2,1)}, u32[]{:S(2)}, u32[]{:S(2)}) collective-permute-start(bf16[1,320,128]{2,1,0:T(8,128)(2,1)S(1)} %get-tuple-element.264), channel_id=1, source_target_pairs={{0,16},{4,20},{8,24},{12,28},{16,0},{20,4},{24,8},{28,12},{1,17},{... | collective-permute-start | bytes 245768 | tf_op jit(solution)/shard_map/ppermute | solution.py:733
  (9 other events, 17.9 us)
